TPU v7x, 32 devices: a whole 2x2x4 slice. The times are simulated.
32 devices in a mesh: ex: 8 (over z, core), pb: 4 (over y, x).
Axes of the slice: x: 2, y: 2, z: 4, core: 2. Of those that a mesh axis runs over, the one named last changes fastest.
Arguments:
- train_sketch: bfloat16 [6144, 8192], P(('ex', 'pb')), may hold values from -6 to 6
- query_sketch: bfloat16 [768, 8192], P('pb'), may hold values from -0.0625 to 0.0625
- residual: float32 [6144], P(('ex', 'pb')), may hold values from 0.05 to 1
- example_source: int32 [6144], P(('ex', 'pb')), may hold values from 0 to 8191, as said below
- source_place: int32 [8192], replicated, may hold values from 0 to 8191, as said below
Outputs:
- source_scores: float32 [8192, 768], P(('ex', 'pb'))
Inputs may be any that keep to these rules, and one draw needn't show every extreme that they name: source_place names each row 0 to 8191 once. `example_source`: of the 192 examples of one device, at most 48 have sources whose table row lies with any one owner (row // 1024); one owner receives exactly 48 from every device. Of them, at most 12 have table rows in any one share of that owner (row % 1024 // (1024 / 4)); in every draw some share of one owner receives exactly 12 from every device.
All inputs are finite; a program needn't handle non-finite values.
Results may differ from a plain program's by a relative error of at most 0.0029.
Values may be sent and summed in bfloat16 or wider, within the bound.
No kernel may reach another device: no remote copies, remote signals or barrier semaphores. Data moves between devices by JAX's collectives and lax.ppermute only.
A program may use at most 64 MiB of HBM per device.

v0:
```python
import jax
import jax.numpy as jnp
from jax import lax
from jax.sharding import PartitionSpec as P

SRC_DEV = 1024


def passed_along(value, axis, steps):
    count = lax.axis_size(axis)
    pairs = [(source, (source + steps) % count) for source in range(count)]
    return lax.ppermute(value, axis, pairs)


def on_device(train_sketch, query_sketch, residual, example_source, source_place):
    rows_here = train_sketch.shape[0]
    block_width = query_sketch.shape[0]
    cycle_size = lax.axis_size("pb")
    cycle_index = lax.axis_index("pb")
    queries_all = block_width * cycle_size

    def block_scores(held):
        return jnp.einsum("rk,qk->rq", train_sketch, held, preferred_element_type=jnp.float32)

    initial = jnp.zeros((rows_here, queries_all), jnp.float32)
    initial = lax.dynamic_update_slice_in_dim(
        initial, block_scores(query_sketch), cycle_index * block_width, 1
    )

    def advance(turn_no, state_pair):
        held, table = state_pair
        held = passed_along(held, "pb", 1)
        anchor = (cycle_index - turn_no) % cycle_size
        table = lax.dynamic_update_slice_in_dim(table, block_scores(held), anchor * block_width, 1)
        return (held, table)

    scores = lax.fori_loop(1, cycle_size, advance, (query_sketch, initial))[1]
    weighted = (scores * residual[:, None]).astype(jnp.bfloat16)
    placed = jnp.take(source_place, example_source)
    owner_count = lax.axis_size("ex")
    capacity = max(2, 2 * rows_here // owner_count)
    owner_id = placed // SRC_DEV
    slot_id = placed % SRC_DEV
    onehot_own = (owner_id[:, None] == jnp.arange(owner_count, dtype=jnp.int32)[None, :]).astype(
        jnp.int32
    )
    earlier = jnp.cumsum(onehot_own, axis=0) - onehot_own
    rank_in = jnp.sum(earlier * onehot_own, axis=1)
    target = owner_id * capacity + rank_in
    buffer_rows = (
        jnp.zeros((owner_count * capacity, queries_all), jnp.bfloat16).at[target].set(weighted)
    )
    buffer_slots = jnp.full((owner_count * capacity,), -1, jnp.int32).at[target].set(slot_id)
    got_rows, got_slots = (
        lax.all_to_all(buffer_rows, "ex", split_axis=0, concat_axis=0, tiled=True),
        lax.all_to_all(buffer_slots, "ex", split_axis=0, concat_axis=0, tiled=True),
    )
    onehot = (jnp.arange(SRC_DEV, dtype=jnp.int32)[:, None] == got_slots[None, :]).astype(
        jnp.bfloat16
    )
    partial_table = jnp.dot(onehot, got_rows, preferred_element_type=jnp.float32)
    return lax.psum_scatter(partial_table, "pb", scatter_dimension=0, tiled=True)


def solution(mesh):
    return jax.shard_map(
        on_device,
        mesh=mesh,
        in_specs=(P(("ex", "pb"), None), P("pb", None), P(("ex", "pb")), P(("ex", "pb")), P()),
        out_specs=P(("ex", "pb"), None),
        check_vma=False,
    )
```

profile of v0, /device:TPU:0, one launch (start us, length us, event | category | flops | bytes accessed | tf_op | source)
XLA Modules:
  0.0 334.1 jit_solution(14805417852768348237)
XLA Ops:
  6.5 0.0 copy-start
  6.5 0.0 copy-start.1
  6.5 3.9 %copy.19 = bf16[192,8192]{1,0:T(8,128)(2,1)} copy(bf16[192,8192]{1,0:T(8,128)(2,1)} %param.8) | data formatting | bytes 6291456
  10.4 0.0 copy-done.1
  10.4 0.0 copy-done
  10.4 1.4 gather_fusion
  11.9 0.6 reduce-window.6
  12.5 0.2 slice_reduce_fusion
  12.8 0.1 add_bitcast_fusion
  12.9 1.2 scatter_custom_fusion
  14.1 0.7 all_to_all.14
  14.8 6.3 %all-to-all-start = ((s32[8,48,1]{1,2,0:T(1,128)}), s32[8,48,1]{1,2,0:T(1,128)S(1)}, u32[]{:S(2)}, u32[]{:S(2)}) async-start(s32[8,48,1]{1,2,0:T(1,128)} %bitcast.3), calls=%async_computation | async-start | bytes 8192 | tf_op jit(solution)/shard_map/all_to_all | solution.py:56
  21.1 3.8 %fusion.10 = f32[192,192]{1,0:T(8,128)S(1)} fusion(bf16[192,8192]{1,0:T(8,128)(2,1)} %param.7, bf16[192,8192]{1,0:T(8,128)(2,1)} %copy.19), kind=kOutput, calls=%fused_computation.32 | convolution fusion | flops 603979776 | bytes 6438912 | tf_op jit(solution)/shard_map/rk,qk->rq/dot_general | solution.py:23
  24.9 0.9 broadcast_in_dim.28
  25.8 1.7 dynamic_update_slice.13
  27.5 0.0 copy-start.2
  27.5 231.5 %while.17 = (s32[]{:T(128)}, bf16[192,8192]{1,0:T(8,128)(2,1)}, f32[192,768]{1,0:T(8,128)}, bf16[192,8192]{1,0:T(8,128)(2,1)}, s32[]{:T(128)}, /*index=5*/s32[]{...) while((s32[]{:T(128)}, bf16[192,8192]{1,0:T(8,128)(2,1)}, f32[192,768]{1,0:T(8,128)}, ...), condition=%wide.region_5.6_spmd, body=%wide.region_4.5_spmd.sunk | while | flops 603979776 | bytes 25608504 | solution.py:37
  27.5 1.7 collective-permute-start
  29.2 69.9 %collective-permute-done = bf16[192,8192]{1,0:T(8,128)(2,1)S(1)} collective-permute-done((bf16[192,8192]{1,0:T(8,128)(2,1)}, bf16[192,8192]{1,0:T(8,128)(2,1)S(1)}, u32[]{:S(2)}, u32[]{:S(2)}) %collective-permute-start) | collective-permute-done | bytes 3145760 | tf_op jit(solution)/shard_map/while/body/eval_jaxpr/ppermute | solution.py:12
  99.2 2.9 fusion.21
  102.1 1.8 dynamic_update_slice.15
  103.8 1.7 copy.16
  105.5 0.8 collective-permute-start
  106.3 70.1 %collective-permute-done = bf16[192,8192]{1,0:T(8,128)(2,1)S(1)} collective-permute-done((bf16[192,8192]{1,0:T(8,128)(2,1)}, bf16[192,8192]{1,0:T(8,128)(2,1)S(1)}, u32[]{:S(2)}, u32[]{:S(2)}) %collective-permute-start) | collective-permute-done | bytes 3145760 | tf_op jit(solution)/shard_map/while/body/eval_jaxpr/ppermute | solution.py:12
  176.3 2.9 fusion.21
  179.2 1.7 dynamic_update_slice.15
  180.9 1.7 copy.16
  182.6 0.0 collective-permute-start
  182.6 69.9 %collective-permute-done = bf16[192,8192]{1,0:T(8,128)(2,1)S(1)} collective-permute-done((bf16[192,8192]{1,0:T(8,128)(2,1)}, bf16[192,8192]{1,0:T(8,128)(2,1)S(1)}, u32[]{:S(2)}, u32[]{:S(2)}) %collective-permute-start) | collective-permute-done | bytes 3145760 | tf_op jit(solution)/shard_map/while/body/eval_jaxpr/ppermute | solution.py:12
  252.5 2.9 fusion.21
  255.4 2.0 dynamic_update_slice.15
  257.4 1.7 copy.16
  259.1 0.0 copy-done.2
  259.1 2.8 scatter_custom_fusion.1
  261.9 0.0 all-to-all-done
  261.9 3.9 %all-to-all-start.1 = ((bf16[8,48,768]{2,1,0:T(8,128)(2,1)}), bf16[8,48,768]{2,1,0:T(8,128)(2,1)S(1)}, u32[]{:S(2)}, u32[]{:S(2)}) async-start(bf16[8,48,768]{2,1,0:T(8,128)(2,1)} %bitcast.4), calls=%async_computation.1 | async-start | bytes 1179648 | tf_op jit(solution)/shard_map/all_to_all | solution.py:55
  265.8 0.0 reduce-scatter.2.cloned.1.call-start
  265.8 0.5 broadcast.76
  266.3 0.7 reduce.5
  267.0 0.1 eq.52
  267.1 15.5 %all-to-all-done.1 = bf16[8,48,768]{2,1,0:T(8,128)(2,1)S(1)} async-done(((bf16[8,48,768]{2,1,0:T(8,128)(2,1)}), bf16[8,48,768]{2,1,0:T(8,128)(2,1)S(1)}, u32[]{:S(2)}, u32[]{:S(2)}) %all-to-all-start.1) | async-done | bytes 589856 | tf_op jit(solution)/shard_map/all_to_all | solution.py:55
  282.5 2.6 fusion
  285.2 0.0 reduce-scatter.2.cloned.1.call-update
  285.2 42.1 %reduce-scatter.2.cloned.1.call-done = f32[256,768]{1,0:T(8,128)} async-done(((f32[1024,768]{1,0:T(8,128)}), f32[256,768]{1,0:T(8,128)}) %reduce-scatter.2.cloned.1.call-update) | async-done | bytes 786448 | tf_op jit(solution)/shard_map/reduce_scatter | solution.py:62
  (9 shorter events, 0.1 us)
Async XLA Ops:
  6.5 3.9 %copy-start = (s32[8192]{0:T(1024)S(1)}, s32[8192]{0:T(1024)}, u32[]{:S(2)}) copy-start(s32[8192]{0:T(1024)} %param.11) | copy-start | bytes 98308
  6.5 3.9 %copy-start.1 = (s32[192]{0:T(256)S(1)}, s32[192]{0:T(256)}, u32[]{:S(2)}) copy-start(s32[192]{0:T(256)} %param.10) | copy-start | bytes 2308
  14.8 247.1 %all-to-all-start = ((s32[8,48,1]{1,2,0:T(1,128)}), s32[8,48,1]{1,2,0:T(1,128)S(1)}, u32[]{:S(2)}, u32[]{:S(2)}) async-start(s32[8,48,1]{1,2,0:T(1,128)} %bitcast.3), calls=%async_computation | async-start | bytes 8192 | tf_op jit(solution)/shard_map/all_to_all | solution.py:56
  27.5 231.5 %copy-start.2 = (f32[192]{0:T(256)S(1)}, f32[192]{0:T(256)}, u32[]{:S(2)}) copy-start(f32[192]{0:T(256)} %param.9) | copy-start | bytes 2308
  27.5 71.6 %collective-permute-start = (bf16[192,8192]{1,0:T(8,128)(2,1)}, bf16[192,8192]{1,0:T(8,128)(2,1)S(1)}, u32[]{:S(2)}, u32[]{:S(2)}) collective-permute-start(bf16[192,8192]{1,0:T(8,128)(2,1)} %get-tuple-element.194), channel_id=1, source_target_pairs={{0,1},{1,2},{2,3},{3,0},{4,5},{5,6},{6,7},{7,4},{8,9},{9,10},{10,1... | collective-permute-start | bytes 9437192 | tf_op jit(solution)/shard_map/while/body/eval_jaxpr/ppermute | solution.py:12
  105.5 70.8 %collective-permute-start = (bf16[192,8192]{1,0:T(8,128)(2,1)}, bf16[192,8192]{1,0:T(8,128)(2,1)S(1)}, u32[]{:S(2)}, u32[]{:S(2)}) collective-permute-start(bf16[192,8192]{1,0:T(8,128)(2,1)} %get-tuple-element.194), channel_id=1, source_target_pairs={{0,1},{1,2},{2,3},{3,0},{4,5},{5,6},{6,7},{7,4},{8,9},{9,10},{10,1... | collective-permute-start | bytes 9437192 | tf_op jit(solution)/shard_map/while/body/eval_jaxpr/ppermute | solution.py:12
  182.6 69.9 %collective-permute-start = (bf16[192,8192]{1,0:T(8,128)(2,1)}, bf16[192,8192]{1,0:T(8,128)(2,1)S(1)}, u32[]{:S(2)}, u32[]{:S(2)}) collective-permute-start(bf16[192,8192]{1,0:T(8,128)(2,1)} %get-tuple-element.194), channel_id=1, source_target_pairs={{0,1},{1,2},{2,3},{3,0},{4,5},{5,6},{6,7},{7,4},{8,9},{9,10},{10,1... | collective-permute-start | bytes 9437192 | tf_op jit(solution)/shard_map/while/body/eval_jaxpr/ppermute | solution.py:12
  261.9 20.7 %all-to-all-start.1 = ((bf16[8,48,768]{2,1,0:T(8,128)(2,1)}), bf16[8,48,768]{2,1,0:T(8,128)(2,1)S(1)}, u32[]{:S(2)}, u32[]{:S(2)}) async-start(bf16[8,48,768]{2,1,0:T(8,128)(2,1)} %bitcast.4), calls=%async_computation.1 | async-start | bytes 1179648 | tf_op jit(solution)/shard_map/all_to_all | solution.py:55
  265.8 61.5 %reduce-scatter.2.cloned.1.call-start = ((), (), s32[]{:S(2)}) async-start(), calls=%async_computation.3 | async-start | bytes 3932160 | tf_op jit(solution)/shard_map/reduce_scatter | solution.py:62
Sparse Core Ops, SparseCore 0:
  285.3 41.9 reduce-scatter.1
where the time goes:
time: 335 us; the launch traced here: 334 us
  waiting for transfers between devices  267 us (80%)
  local copies, waits for them, and re-layouts  21 us (6%)
  matrix products  15.1 us (5%)
  between operations  13.5 us (4%)
  starting transfers between devices  12.8 us (4%)
  other arithmetic  4.24 us (1%)
    ppermute x3, waiting for transfers between devices, passed_along(): return lax.ppermute(value, axis, pairs)  210 us
    reduce_scatter x1, waiting for transfers between devices, on_device(): lax.psum_scatter(partial_table, 'pb', scatter_dimension=0, tiled=True)  42.1 us
    all_to_all x1, waiting for transfers between devices, on_device(): lax.all_to_all(buffer_rows, 'ex', split_axis=0, concat_axis=0, tiled=True)  15.5 us
    dot_general x4, matrix products, block_scores(): jnp.einsum('rk,qk->rq', train_sketch, held, preferred_element_type=jnp.fl...  12.5 us
  transfers between devices with their start and end apart: 6, of which 5 were waited for; matrix products, arithmetic and copies ran while one was open for 9% of the time, Pallas kernels for 0%

commit v1 on v0

v1 whole, which is shorter than its diff:
```python
import functools
import math

import jax
import jax.numpy as jnp
from jax import lax
from jax.experimental import pallas as pl
from jax.experimental.pallas import tpu as pltpu
from jax.sharding import PartitionSpec as P

BOTH = ("ex", "pb")
NT = (((1,), (1,)), ((), ()))


def moved(value, axis, target):
    count = lax.axis_size(axis)
    return lax.ppermute(value, axis, [(i, target(i)) for i in range(count)])


def partial_kernel(count, own_ref, other_ref, *refs):
    pieces, (own_out, other_out) = refs[:count], refs[count:]
    queries = jnp.concatenate([piece[...] for piece in pieces], axis=0)

    @pl.when(pl.program_id(0) == 0)
    def _():
        own_out[...] = jnp.zeros_like(own_out)
        other_out[...] = jnp.zeros_like(other_out)

    other_out[...] += lax.dot_general(other_ref[...], queries, NT, preferred_element_type=jnp.float32)
    own_out[...] += lax.dot_general(own_ref[...], queries, NT, preferred_element_type=jnp.float32)


def partials(own, other, pieces):
    rows, depth = own.shape
    width = sum(piece.shape[0] for piece in pieces)
    step = math.gcd(depth, 1024)
    chunk = lambda height: pl.BlockSpec((height, step), lambda k: (0, k))
    whole = pl.BlockSpec((rows, width), lambda k: (0, 0))
    return pl.pallas_call(
        functools.partial(partial_kernel, len(pieces)),
        grid=(depth // step,),
        in_specs=[chunk(rows), chunk(rows)] + [chunk(piece.shape[0]) for piece in pieces],
        out_specs=[whole, whole],
        out_shape=[jax.ShapeDtypeStruct((rows, width), jnp.float32)] * 2,
        compiler_params=pltpu.CompilerParams(vmem_limit_bytes=40 << 20),
        cost_estimate=pl.CostEstimate(
            flops=4 * rows * width * depth, bytes_accessed=2 * depth * (2 * rows + width), transcendentals=0
        ),
    )(own, other, *pieces)


def one_hot(hits):
    return jnp.where(hits, 1.0, 0.0).astype(jnp.bfloat16)


def pick(select, values):
    return jnp.dot(select, values, preferred_element_type=jnp.float32)


def packed_kernel(full, own_a, got_a, own_b, got_b, residual_ref, column_ref, target_ref, out_ref):
    scale = residual_ref[...]
    weighted = jnp.concatenate(
        [
            ((own_a[...] + got_a[...]) * scale).astype(jnp.bfloat16),
            ((own_b[...] + got_b[...]) * scale).astype(jnp.bfloat16),
        ],
        axis=1,
    )
    rows, width = weighted.shape
    order = one_hot(lax.broadcasted_iota(jnp.int32, (width, width), 1) == column_ref[...])
    ordered = pick(weighted, order).astype(jnp.bfloat16)
    height = out_ref.shape[0]
    at = 0
    for index in range(full // 8):
        row = lax.broadcasted_iota(jnp.int32, (height, rows), 0)
        select = one_hot(row == target_ref[index : index + 1, :])
        out_ref[:, at : at + width] = pick(select, ordered).astype(jnp.bfloat16)
        at += width
    if out_ref.shape[1] > at:
        half = width // 2
        index = full // 8
        row = lax.broadcasted_iota(jnp.int32, (height, rows), 0)
        left = one_hot(row == target_ref[index : index + 1, :])
        right = one_hot(row == target_ref[index + 1 : index + 2, :])
        both = pick(left, ordered[:, :half]) + pick(right, ordered[:, half:])
        out_ref[:, at:] = both.astype(jnp.bfloat16)


def table_kernel(full, got_ref, slot_ref, out_ref):
    height, width = out_ref.shape
    received = got_ref.shape[0]
    row = lax.broadcasted_iota(jnp.int32, (height, received), 0)
    total = None
    at = 0
    for index in range(full // 8):
        part = pick(one_hot(row == slot_ref[index : index + 1, :]), got_ref[:, at : at + width])
        total = part if total is None else total + part
        at += width
    if got_ref.shape[1] > at:
        half = width // 2
        index = full // 8
        for side in range(2):
            part = pick(one_hot(row == slot_ref[index + side : index + side + 1, :]), got_ref[:, at:])
            span = slice(side * half, (side + 1) * half)
            out_ref[:, span] = part if total is None else total[:, span] + part
    else:
        out_ref[...] = total


def on_device(train, query, residual, example_source, source_place):
    rows, depth = train.shape
    block = query.shape[0]
    ex, pb = lax.axis_size("ex"), lax.axis_size("pb")
    me_ex, me_pb = lax.axis_index("ex"), lax.axis_index("pb")
    devices = ex * pb
    side = math.isqrt(pb)
    assert side * side == pb and ex % 4 == 0
    table_rows = source_place.shape[0] // devices
    core, layer = me_ex % 2, (me_ex // 2) % 2
    deep = depth // 2
    half = block // 2
    lent = half * 2 // 3 // 8 * 8

    along_x = lambda d: lambda i: i // side * side + (i + d) % side
    along_y = lambda d: lambda i: (i + d * side) % pb
    on_core = lambda i: i ^ 1
    on_z = lambda i: i ^ 2
    steps = range(1, side)

    first = layer * half
    second = half - first
    cut = lambda start, count: lax.dynamic_slice(query, (start, core * deep), (count, deep))
    front, back = cut(first, half), cut(second, half)
    x_one = [moved(front, "pb", along_x(d)) for d in steps]
    y_one = [moved(back, "pb", along_y(d)) for d in steps]
    x_rest = [moved(back[lent:], "pb", along_x(d)) for d in steps]
    y_rest = [moved(front[lent:], "pb", along_y(d)) for d in steps]
    other = moved(lax.dynamic_slice(train, (0, (1 - core) * deep), (rows, deep)), "ex", on_core)
    own = lax.dynamic_slice(train, (0, core * deep), (rows, deep))

    placed = jnp.take(source_place, example_source)
    placed_all = lax.all_gather(placed, BOTH, tiled=True).reshape(devices, rows)
    capacity = max(1, -(-2 * rows // devices))
    full, rest = capacity // 8 * 8, capacity % 8
    if rest > 4:
        full, rest = full + 8, 0
    goal = placed // table_rows
    before = jnp.arange(rows)[None, :] < jnp.arange(rows)[:, None]
    rank = jnp.sum((goal[:, None] == goal[None, :]) & before, axis=1).astype(jnp.int32)
    groups = [jnp.where(rank // 8 == index, goal * 8 + rank % 8, -1) for index in range(full // 8)]
    if rest:
        late = rank >= full
        groups += [jnp.where(late, goal * 8 + g * 4 + rank - full, -1) for g in range(2)]
    target = jnp.stack(groups)

    mine = placed_all // table_rows == me_ex * pb + me_pb
    rank_all = jnp.cumsum(mine.astype(jnp.int32), axis=1) - 1
    slot_all = placed_all % table_rows

    def slots(rank_wanted):
        hit = mine[:, None, :] & (rank_all[:, None, :] == rank_wanted[None, :, None])
        found = jnp.sum(jnp.where(hit, slot_all[:, None, :] + 1, 0), axis=2) - 1
        return found.reshape(devices * 8)

    eight = jnp.arange(8, dtype=jnp.int32)
    slot_groups = [slots(eight + 8 * index) for index in range(full // 8)]
    if rest:
        slot_groups += [slots(jnp.where(eight // 4 == g, full + eight % 4, rows)) for g in range(2)]
    slot = jnp.stack(slot_groups)

    early = [front, back] + x_one + y_one
    early_own, early_other = partials(own, other, early)
    early_got = moved(early_other, "ex", on_core)

    x_lent = moved(jnp.concatenate([v[:lent] for v in x_one], axis=0), "ex", on_z)
    y_lent = moved(jnp.concatenate([v[:lent] for v in y_one], axis=0), "ex", on_z)
    y_all = y_one[0] if side == 2 else jnp.concatenate(y_one, axis=0)
    x_all = x_one[0] if side == 2 else jnp.concatenate(x_one, axis=0)
    x_two = [moved(y_all, "pb", along_x(d)) for d in steps]
    y_two = [moved(x_all, "pb", along_y(d)) for d in steps]
    late_pieces = x_two + y_two + [x_lent, y_lent] + x_rest + y_rest
    late_own, late_other = partials(own, other, late_pieces)
    late_got = moved(late_other, "ex", on_core)

    my_x, my_y = me_pb % side, me_pb // side
    at = lambda dx, dy: ((my_y - dy) % side * side + (my_x - dx) % side) * block
    span = lambda start, count: start + jnp.arange(count, dtype=jnp.int32)
    columns = [span(at(0, 0) + first, half), span(at(0, 0) + second, half)]
    columns += [span(at(d, 0) + first, half) for d in steps]
    columns += [span(at(0, d) + second, half) for d in steps]
    for d in steps:
        columns += [span(at(d, up) + second, half) for up in steps]
    for up in steps:
        columns += [span(at(d, up) + first, half) for d in steps]
    columns += [span(at(d, 0) + second, lent) for d in steps]
    columns += [span(at(0, d) + first, lent) for d in steps]
    columns += [span(at(d, 0) + second + lent, half - lent) for d in steps]
    columns += [span(at(0, d) + first + lent, half - lent) for d in steps]
    column = jnp.concatenate(columns)[:, None]

    width = block * pb
    payload = full // 8 * width + (width // 2 if rest else 0)
    packed = pl.pallas_call(
        functools.partial(packed_kernel, full),
        out_shape=jax.ShapeDtypeStruct((devices * 8, payload), jnp.bfloat16),
        compiler_params=pltpu.CompilerParams(vmem_limit_bytes=48 << 20),
    )(early_own, early_got, late_own, late_got, residual[:, None], column, target)
    got = lax.all_to_all(packed.reshape(devices, 8, payload), BOTH, split_axis=0, concat_axis=0)
    return pl.pallas_call(
        functools.partial(table_kernel, full),
        out_shape=jax.ShapeDtypeStruct((table_rows, width), jnp.float32),
        compiler_params=pltpu.CompilerParams(vmem_limit_bytes=48 << 20),
    )(got.reshape(devices * 8, payload), slot)


def solution(mesh):
    return jax.shard_map(
        on_device,
        mesh=mesh,
        in_specs=(P(BOTH, None), P("pb", None), P(BOTH), P(BOTH), P()),
        out_specs=P(BOTH, None),
        check_vma=False,
    )
```

time: 335 us -> 131 us (0.39)
  waiting for transfers between devices: 267 us -> 26.2 us
  blocking collectives: 0 us -> 53.3 us
  matrix products: 15.1 us -> 0 us
  between operations: 13.5 us -> 0.2 us
  Pallas kernels: 0 us -> 12.7 us
  local copies, waits for them, and re-layouts: 21 us -> 16.7 us
    ppermute x3 -> x11, waiting for transfers between devices: 210 us -> 10.7 us  [moved(): return lax.ppermute(value, axis, [(i, target(i)) for i in range(count)])]
    unnamed x0 -> x1, blocking collectives: none -> 53.3 us
    reduce_scatter x1 -> x0, waiting for transfers between devices: 42.1 us -> none  [on_device(): lax.psum_scatter(partial_table, 'pb', scatter_dimension=0, tiled=True)]
    dot_general x5 -> x0, matrix products: 15.1 us -> none  [the longest x4 12.5 us: block_scores(): jnp.einsum('rk,qk->rq', train_sketch, held, preferred_element_type=jnp.fl...]
    pallas_call x0 -> x4, Pallas kernels: none -> 12.7 us  [the longest x2 9.57 us: partials(): pl.pallas_call(functools.partial(partial_kernel, len(pieces)), grid=(dept...]
    ppermute x3 -> x11, starting transfers between devices: 2.49 us -> 11.4 us  [moved(): return lax.ppermute(value, axis, [(i, target(i)) for i in range(count)])]
    all_to_all x2 -> x1, starting transfers between devices: 10.2 us -> 2.61 us  [on_device(): lax.all_to_all(packed.reshape(devices, 8, payload), BOTH, split_axis=0, c...]
    dynamic_update_slice x4 -> x0, local copies, waits for them, and re-layouts: 7.18 us -> none  [the longest x3 5.44 us: advance(): lax.dynamic_update_slice_in_dim(table, block_scores(held), anchor * block...]
  transfers between devices with their start and end apart: 6 -> 12, of which waited for: 5 -> 4; matrix products, arithmetic and copies ran while one was open for 9% -> 15% of each run, Pallas kernels for 0% -> 7%
where the time goes in v1:
time: 131 us; the launch traced here: 130 us
  blocking collectives  53.3 us (41%)
  waiting for transfers between devices  26.2 us (20%)
  local copies, waits for them, and re-layouts  16.7 us (13%)
  starting transfers between devices  14 us (11%)
  Pallas kernels  12.7 us (10%)
  other arithmetic  6.96 us (5%)
    unnamed x1, blocking collectives  53.3 us
    all_to_all x1, waiting for transfers between devices, on_device(): lax.all_to_all(packed.reshape(devices, 8, payload), BOTH, split_axis=0, c...  15.5 us
    ppermute x11, starting transfers between devices, moved(): return lax.ppermute(value, axis, [(i, target(i)) for i in range(count)])  11.4 us
    ppermute x11, waiting for transfers between devices, moved(): return lax.ppermute(value, axis, [(i, target(i)) for i in range(count)])  10.7 us
    pallas_call x2, Pallas kernels, partials(): pl.pallas_call(functools.partial(partial_kernel, len(pieces)), grid=(dept...  9.57 us
    slice x2, local copies, waits for them, and re-layouts, on_device(): v[:lent]  3.76 us
    dynamic_slice x1, local copies, waits for them, and re-layouts, on_device(): lax.dynamic_slice(train, (0, (1 - core) * deep), (rows, deep))  3.41 us
    add x5, other arithmetic, on_device(): span = lambda start, count: start + jnp.arange(count, dtype=jnp.int32)  2.85 us
  transfers between devices with their start and end apart: 12, of which 4 were waited for; matrix products, arithmetic and copies ran while one was open for 15% of the time, Pallas kernels for 7%

profile of v1, /device:TPU:0, one launch (start us, length us, event | category | flops | bytes accessed | tf_op | source)
XLA Modules:
  0.0 130.1 jit_solution(10022839202160771599)
XLA Ops:
  0.0 3.4 %constant_dynamic-slice_fusion = (bf16[192,4096]{1,0:T(8,128)(2,1)}, bf16[192,4096]{1,0:T(8,128)(2,1)S(1)}) fusion(bf16[192,8192]{1,0:T(8,128)(2,1)} %param.5, s32[]{:T(128)S(6)} %select_n.224, s32[]{:T(128)S(6)} %select_n.223), kind=kLoop, calls=%fused_computation.65 | loop fusion | bytes 6291464 | tf_op jit(solution)/shard_map/dynamic_slice | solution.py:138
  3.4 0.5 collective-permute-start
  3.9 2.7 %fusion.10 = (bf16[96,4096]{1,0:T(8,128)(2,1)}, bf16[96,4096]{1,0:T(8,128)(2,1)}) fusion(bf16[192,8192]{1,0:T(8,128)(2,1)} %param.6, s32[]{:T(128)S(6)} %select_n.228, s32[]{:T(128)S(6)} %select_n.223, s32[]{:T(128)S(6)} %select_n.227), kind=kLoop, calls=%fused_computation.69 | loop fusion | bytes 3145740 | tf_op jit(solution)/shard_map/dynamic_slice | solution.py:132
  6.5 2.5 %collective-permute-start.1 = (bf16[96,4096]{1,0:T(8,128)(2,1)}, bf16[96,4096]{1,0:T(8,128)(2,1)}, u32[]{:S(2)}, u32[]{:S(2)}) collective-permute-start(bf16[96,4096]{1,0:T(8,128)(2,1)} %get-tuple-element.19.refs_0_), channel_id=1, source_target_pairs={{0,1},{1,0},{2,3},{3,2},{4,5},{5,4},{6,7},{7,6},{8,9},{9,8},{10,11... | collective-permute-start | bytes 2359304 | tf_op jit(solution)/shard_map/ppermute | solution.py:17
  9.0 1.5 %collective-permute-start.2 = (bf16[96,4096]{1,0:T(8,128)(2,1)}, bf16[96,4096]{1,0:T(8,128)(2,1)}, u32[]{:S(2)}, u32[]{:S(2)}) collective-permute-start(bf16[96,4096]{1,0:T(8,128)(2,1)} %get-tuple-element.18.refs_1_), channel_id=1, source_target_pairs={{0,2},{1,3},{2,0},{3,1},{4,6},{5,7},{6,4},{7,5},{8,10},{9,11},{10,... | collective-permute-start | bytes 2359304 | tf_op jit(solution)/shard_map/ppermute | solution.py:17
  10.6 1.9 %fusion.9 = (bf16[32,4096]{1,0:T(8,128)(2,1)}, bf16[32,4096]{1,0:T(8,128)(2,1)}) fusion(bf16[192,8192]{1,0:T(8,128)(2,1)} %param.6, s32[]{:T(128)S(6)} %add.383, s32[]{:T(128)S(6)} %select_n.223, s32[]{:T(128)S(6)} %add.382), kind=kLoop, calls=%fused_computation.68 | loop fusion | bytes 1048588 | tf_op jit(solution)/shard_map/slice | solution.py:137
  12.4 0.5 collective-permute-start.8
  13.0 1.4 %gather_fusion = s32[192]{0:T(256)S(1)} fusion(s32[8192]{0:T(1024)S(1)} %copy-done, s32[1024]{0:T(1024)S(1)} %pad_clamp_fusion), kind=kCustom, calls=%fused_computation | custom fusion | bytes 2304 | tf_op jit(solution)/shard_map/jit(_take)/gather | solution.py:141
  14.4 0.1 fusion.8
  14.6 53.3 %all-reduce.1 = s32[6144]{0:T(1024)S(1)} all-reduce(s32[6144]{0:T(1024)S(1)} %get-tuple-element.22), channel_id=1, replica_groups=mesh['ex'=8,'pb'=4] {'ex','pb'}, use_global_device_ids=true, to_apply=%add.1 | all-reduce | flops 6144 | bytes 49152
  67.8 0.1 reshape.231
  67.9 0.6 copy-done.4
  68.5 0.6 reduce-window.6
  69.1 0.6 iota_add_fusion.8
  69.7 0.6 iota_add_fusion.6
  70.3 0.2 slice_reduce_fusion
  70.4 0.6 iota_add_fusion.2
  71.0 0.0 collective-permute-done.2.refs_3_
  71.0 2.3 %collective-permute-start.4 = (bf16[96,4096]{1,0:T(8,128)(2,1)}, bf16[96,4096]{1,0:T(8,128)(2,1)}, u32[]{:S(2)}, u32[]{:S(2)}) collective-permute-start(bf16[96,4096]{1,0:T(8,128)(2,1)} %collective-permute-done.2.refs_3_), channel_id=1, source_target_pairs={{0,1},{1,0},{2,3},{3,2},{4,5},{5,4},{6,7},{7,6},{8,9},{9,8},{10,11... | collective-permute-start | bytes 2359304 | tf_op jit(solution)/shard_map/ppermute | solution.py:17
  73.3 0.5 collective-permute-start.5
  73.8 0.5 iota_add_fusion.4
  74.3 0.2 convert_reduce_fusion
  74.5 1.9 %slice.30 = bf16[64,4096]{1,0:T(8,128)(2,1)} slice(bf16[96,4096]{1,0:T(8,128)(2,1)} %collective-permute-done.1.refs_2_), slice={[0:64], [0:4096]} | slice | bytes 1048576 | tf_op jit(solution)/shard_map/slice | solution.py:175
  76.4 0.4 collective-permute-start.6
  76.8 1.9 %slice.31 = bf16[64,4096]{1,0:T(8,128)(2,1)} slice(bf16[96,4096]{1,0:T(8,128)(2,1)} %collective-permute-done.2.refs_3_), slice={[0:64], [0:4096]} | slice | bytes 1048576 | tf_op jit(solution)/shard_map/slice | solution.py:176
  78.7 1.6 %collective-permute-start.7 = (bf16[64,4096]{1,0:T(8,128)(2,1)}, bf16[64,4096]{1,0:T(8,128)(2,1)}, u32[]{:S(2)}, u32[]{:S(2)}) collective-permute-start(bf16[64,4096]{1,0:T(8,128)(2,1)} %slice.31), channel_id=1, source_target_pairs={{0,8},{4,12},{8,0},{12,4},{16,24},{20,28},{24,16},{28,20},{1,9},{5... | collective-permute-start | bytes 1572872 | tf_op jit(solution)/shard_map/ppermute | solution.py:17
  80.3 0.6 compare_select_fusion.3
  80.9 1.6 %collective-permute-start.9 = (bf16[32,4096]{1,0:T(8,128)(2,1)}, bf16[32,4096]{1,0:T(8,128)(2,1)}, u32[]{:S(2)}, u32[]{:S(2)}) collective-permute-start(bf16[32,4096]{1,0:T(8,128)(2,1)} %get-tuple-element.16), channel_id=1, source_target_pairs={{0,2},{1,3},{2,0},{3,1},{4,6},{5,7},{6,4},{7,5},{8,10},{9,11},{10,... | collective-permute-start | bytes 786440 | tf_op jit(solution)/shard_map/ppermute | solution.py:17
  82.5 0.6 iota_add_fusion
  83.0 0.8 copy.10.residual_ref
  83.8 0.8 concatenate.3
  84.6 0.9 broadcast_in_dim.66.column_ref
  85.6 0.7 pad_add_fusion.target_ref
  86.3 4.8 %shard_map.55 = (f32[192,384]{1,0:T(8,128)S(1)}, f32[192,384]{1,0:T(8,128)S(1)}) custom-call(bf16[192,4096]{1,0:T(8,128)(2,1)S(1)} %get-tuple-element.21.own_ref, bf16[192,4096]{1,0:T(8,128)(2,1)S(1)} %collective-permute-done.other_ref, bf16[96,4096]{1,0:T(8,128)(2,1)} %get-tuple-element.19.refs_0_, bf16[96,4096]{1,0:T(8,128)(2,1)} %get-tuple-element.18.refs_1_, ...), custom_call_target="tpu_custom_call" | custom-call | flops 1207959552 | bytes 6291456 | tf_op jit(solution)/shard_map/pallas_call | solution.py:39
  91.1 5.3 %collective-permute-done.9.refs_5_ = bf16[32,4096]{1,0:T(8,128)(2,1)} collective-permute-done((bf16[32,4096]{1,0:T(8,128)(2,1)}, bf16[32,4096]{1,0:T(8,128)(2,1)}, u32[]{:S(2)}, u32[]{:S(2)}) %collective-permute-start.9) | collective-permute-done | bytes 262176 | tf_op jit(solution)/shard_map/ppermute | solution.py:17
  96.4 4.0 %collective-permute-done.7.refs_3_ = bf16[64,4096]{1,0:T(8,128)(2,1)} collective-permute-done((bf16[64,4096]{1,0:T(8,128)(2,1)}, bf16[64,4096]{1,0:T(8,128)(2,1)}, u32[]{:S(2)}, u32[]{:S(2)}) %collective-permute-start.7) | collective-permute-done | bytes 524320 | tf_op jit(solution)/shard_map/ppermute | solution.py:17
  100.4 4.7 %shard_map.56 = (f32[192,384]{1,0:T(8,128)S(1)}, f32[192,384]{1,0:T(8,128)S(1)}) custom-call(bf16[192,4096]{1,0:T(8,128)(2,1)S(1)} %get-tuple-element.21.own_ref, bf16[192,4096]{1,0:T(8,128)(2,1)S(1)} %collective-permute-done.other_ref, bf16[96,4096]{1,0:T(8,128)(2,1)} %collective-permute-done.4.refs_0_, bf16[96,4096]{1,0:T(8,128)(2,1)} %collective-permute-done.5.refs_1_, ...), custom_call_target="tpu_custom_call" | custom-call | flops 1207959552 | bytes 6291456 | tf_op jit(solution)/shard_map/pallas_call | solution.py:39
  105.2 0.1 collective-permute-start.10
  105.3 0.1 copy_bitcast_fusion
  105.4 1.5 %collective-permute-done.10.got_b = f32[192,384]{1,0:T(8,128)S(1)} collective-permute-done((f32[192,384]{1,0:T(8,128)S(1)}, f32[192,384]{1,0:T(8,128)S(1)}, u32[]{:S(2)}, u32[]{:S(2)}) %collective-permute-start.10) | collective-permute-done | bytes 294944 | tf_op jit(solution)/shard_map/ppermute | solution.py:17
  106.8 1.8 %shard_map.57 = bf16[256,1152]{1,0:T(8,128)(2,1)} custom-call(f32[192,384]{1,0:T(8,128)S(1)} %get-tuple-element.9.own_a, f32[192,384]{1,0:T(8,128)S(1)} %collective-permute-done.3.got_a, f32[192,384]{1,0:T(8,128)S(1)} %get-tuple-element.11.own_b, f32[192,384]{1,0:T(8,128)S(1)} %collective-permute-done.10.got_b, f32[192,1]{1,0:T(8,128)S(1)} %copy.10.residual_ref, ...), custom_call_target="tpu_custom_call" | custom-call | tf_op jit(solution)/shard_map/pallas_call | solution.py:203
  108.6 2.6 %all-to-all-start = ((bf16[32,8,1152]{2,1,0:T(8,128)(2,1)}), bf16[32,8,1152]{2,1,0:T(8,128)(2,1)S(1)}, u32[]{:S(2)}, u32[]{:S(2)}) async-start(bf16[32,8,1152]{2,1,0:T(8,128)(2,1)} %bitcast.4), calls=%async_computation | async-start | bytes 1179648 | tf_op jit(solution)/shard_map/all_to_all | solution.py:208
  111.3 1.7 %select_reduce_fusion.2 = (s32[32,8]{1,0:T(8,128)S(1)}, s32[32,8]{1,0:T(8,128)S(1)}, s32[32,8]{1,0:T(8,128)S(1)}) fusion(s32[32,192]{1,0:T(8,128)S(1)} %get-tuple-element.39, s32[32,192]{1,0:T(8,128)S(1)} %get-tuple-element.40, pred[32,192]{1,0:T(8,128)(4,1)S(1)} %fusion.2, s32[8]{0:T(128)S(1)} %get-tuple-element.28, s32[8]{0:T(128)S(1)} %get-tuple-element.27), kind=kLoop, calls=%fused_computation.3 | loop fusion | flops 589056 | bytes 58432 | tf_op jit(solution)/shard_map/reduce_sum | solution.py:162
  113.0 0.1 sub.93
  113.1 0.1 sub.91
  113.2 0.1 sub.88
  113.3 15.5 %all-to-all-done = bf16[32,8,1152]{2,1,0:T(8,128)(2,1)S(1)} async-done(((bf16[32,8,1152]{2,1,0:T(8,128)(2,1)}), bf16[32,8,1152]{2,1,0:T(8,128)(2,1)S(1)}, u32[]{:S(2)}, u32[]{:S(2)}) %all-to-all-start) | async-done | bytes 589856 | tf_op jit(solution)/shard_map/all_to_all | solution.py:208
  128.8 1.3 shard_map.58
  (37 shorter events, 0.2 us)
Async XLA Ops:
  0.0 13.0 %copy-start = (s32[8192]{0:T(1024)S(1)}, s32[8192]{0:T(1024)}, u32[]{:S(2)}) copy-start(s32[8192]{0:T(1024)} %param.9) | copy-start | bytes 98308
  3.4 9.5 %copy-start.7 = (s32[192]{0:T(256)S(1)}, s32[192]{0:T(256)}, u32[]{:S(2)}) copy-start(s32[192]{0:T(256)} %param.8) | copy-start | bytes 2308
  3.4 77.5 %collective-permute-start = (bf16[192,4096]{1,0:T(8,128)(2,1)}, bf16[192,4096]{1,0:T(8,128)(2,1)S(1)}, u32[]{:S(2)}, u32[]{:S(2)}) collective-permute-start(bf16[192,4096]{1,0:T(8,128)(2,1)} %get-tuple-element.20), channel_id=1, source_target_pairs={{0,4},{4,0},{8,12},{12,8},{16,20},{20,16},{24,28},{28,24},{1,5},{5... | collective-permute-start | bytes 4718600 | tf_op jit(solution)/shard_map/ppermute | solution.py:17
  6.5 66.8 %collective-permute-start.1 = (bf16[96,4096]{1,0:T(8,128)(2,1)}, bf16[96,4096]{1,0:T(8,128)(2,1)}, u32[]{:S(2)}, u32[]{:S(2)}) collective-permute-start(bf16[96,4096]{1,0:T(8,128)(2,1)} %get-tuple-element.19.refs_0_), channel_id=1, source_target_pairs={{0,1},{1,0},{2,3},{3,2},{4,5},{5,4},{6,7},{7,6},{8,9},{9,8},{10,11... | collective-permute-start | bytes 2359304 | tf_op jit(solution)/shard_map/ppermute | solution.py:17
  9.0 62.0 %collective-permute-start.2 = (bf16[96,4096]{1,0:T(8,128)(2,1)}, bf16[96,4096]{1,0:T(8,128)(2,1)}, u32[]{:S(2)}, u32[]{:S(2)}) collective-permute-start(bf16[96,4096]{1,0:T(8,128)(2,1)} %get-tuple-element.18.refs_1_), channel_id=1, source_target_pairs={{0,2},{1,3},{2,0},{3,1},{4,6},{5,7},{6,4},{7,5},{8,10},{9,11},{10,... | collective-permute-start | bytes 2359304 | tf_op jit(solution)/shard_map/ppermute | solution.py:17
  12.4 66.3 %collective-permute-start.8 = (bf16[32,4096]{1,0:T(8,128)(2,1)}, bf16[32,4096]{1,0:T(8,128)(2,1)S(1)}, u32[]{:S(2)}, u32[]{:S(2)}) collective-permute-start(bf16[32,4096]{1,0:T(8,128)(2,1)} %get-tuple-element.17), channel_id=1, source_target_pairs={{0,1},{1,0},{2,3},{3,2},{4,5},{5,4},{6,7},{7,6},{8,9},{9,8},{10,11... | collective-permute-start | bytes 786440 | tf_op jit(solution)/shard_map/ppermute | solution.py:17
  67.9 0.6 copy-start.4
  69.1 13.9 %copy-start.2 = (s32[32,2,128]{2,0,1:T(8,128)}, s32[32,2,128]{2,0,1:T(8,128)S(1)}, u32[]{:S(2)}) copy-start(s32[32,2,128]{2,0,1:T(8,128)S(1)} %reduce-window.6) | copy-start | bytes 98308
  71.0 29.4 %collective-permute-start.4 = (bf16[96,4096]{1,0:T(8,128)(2,1)}, bf16[96,4096]{1,0:T(8,128)(2,1)}, u32[]{:S(2)}, u32[]{:S(2)}) collective-permute-start(bf16[96,4096]{1,0:T(8,128)(2,1)} %collective-permute-done.2.refs_3_), channel_id=1, source_target_pairs={{0,1},{1,0},{2,3},{3,2},{4,5},{5,4},{6,7},{7,6},{8,9},{9,8},{10,11... | collective-permute-start | bytes 2359304 | tf_op jit(solution)/shard_map/ppermute | solution.py:17
  73.3 27.1 %collective-permute-start.5 = (bf16[96,4096]{1,0:T(8,128)(2,1)}, bf16[96,4096]{1,0:T(8,128)(2,1)}, u32[]{:S(2)}, u32[]{:S(2)}) collective-permute-start(bf16[96,4096]{1,0:T(8,128)(2,1)} %collective-permute-done.1.refs_2_), channel_id=1, source_target_pairs={{0,2},{1,3},{2,0},{3,1},{4,6},{5,7},{6,4},{7,5},{8,10},{9,11},{10,... | collective-permute-start | bytes 2359304 | tf_op jit(solution)/shard_map/ppermute | solution.py:17
  76.4 20.0 %collective-permute-start.6 = (bf16[64,4096]{1,0:T(8,128)(2,1)}, bf16[64,4096]{1,0:T(8,128)(2,1)}, u32[]{:S(2)}, u32[]{:S(2)}) collective-permute-start(bf16[64,4096]{1,0:T(8,128)(2,1)} %slice.30), channel_id=1, source_target_pairs={{0,8},{4,12},{8,0},{12,4},{16,24},{20,28},{24,16},{28,20},{1,9},{5... | collective-permute-start | bytes 1572872 | tf_op jit(solution)/shard_map/ppermute | solution.py:17
  78.7 21.7 %collective-permute-start.7 = (bf16[64,4096]{1,0:T(8,128)(2,1)}, bf16[64,4096]{1,0:T(8,128)(2,1)}, u32[]{:S(2)}, u32[]{:S(2)}) collective-permute-start(bf16[64,4096]{1,0:T(8,128)(2,1)} %slice.31), channel_id=1, source_target_pairs={{0,8},{4,12},{8,0},{12,4},{16,24},{20,28},{24,16},{28,20},{1,9},{5... | collective-permute-start | bytes 1572872 | tf_op jit(solution)/shard_map/ppermute | solution.py:17
  80.9 15.5 %collective-permute-start.9 = (bf16[32,4096]{1,0:T(8,128)(2,1)}, bf16[32,4096]{1,0:T(8,128)(2,1)}, u32[]{:S(2)}, u32[]{:S(2)}) collective-permute-start(bf16[32,4096]{1,0:T(8,128)(2,1)} %get-tuple-element.16), channel_id=1, source_target_pairs={{0,2},{1,3},{2,0},{3,1},{4,6},{5,7},{6,4},{7,5},{8,10},{9,11},{10,... | collective-permute-start | bytes 786440 | tf_op jit(solution)/shard_map/ppermute | solution.py:17
  85.6 5.5 %copy-start.6 = (s32[32,3]{0,1:T(4,128)}, s32[32,3]{0,1:T(4,128)S(1)}, u32[]{:S(2)}) copy-start(s32[32,3]{0,1:T(4,128)S(1)} %reduce-window.9) | copy-start | bytes 1156
  96.4 8.9 %copy-start.3 = (s32[32,2,128]{2,0,1:T(8,128)S(1)}, s32[32,2,128]{2,0,1:T(8,128)}, u32[]{:S(2)}) copy-start(s32[32,2,128]{2,0,1:T(8,128)} %copy-done.2) | copy-start | bytes 98308
  96.4 8.9 %slice-start = ((s32[32,3]{0,1:T(4,128)}), s32[32,2]{0,1:T(2,128)S(1)}, s32[]{:S(2)}) async-start(s32[32,3]{0,1:T(4,128)} %copy-done.6), calls=%async_computation.1 | async-start | bytes 2048 | tf_op jit(solution)/shard_map/slice.1
  96.4 10.4 %copy-start.1 = (s32[768,1]{1,0:T(8,128)S(1)}, s32[768,1]{1,0:T(8,128)}, u32[]{:S(2)}) copy-start(s32[768,1]{1,0:T(8,128)} %broadcast_in_dim.66.column_ref) | copy-start | bytes 9220
  96.4 9.0 %collective-permute-start.3 = (f32[192,384]{1,0:T(8,128)S(1)}, f32[192,384]{1,0:T(8,128)S(1)}, u32[]{:S(2)}, u32[]{:S(2)}) collective-permute-start(f32[192,384]{1,0:T(8,128)S(1)} %get-tuple-element.10), channel_id=1, source_target_pairs={{0,4},{4,0},{8,12},{12,8},{16,20},{20,16},{24,28},{28,24},{1,5},{5... | collective-permute-start | bytes 884744 | tf_op jit(solution)/shard_map/ppermute | solution.py:17
  105.2 6.1 %copy-start.5 = (s32[32,192]{1,0:T(8,128)S(1)}, s32[32,192]{1,0:T(8,128)}, u32[]{:S(2)}) copy-start(s32[32,192]{1,0:T(8,128)} %copy-done.4) | copy-start | bytes 73732
  105.2 1.6 %collective-permute-start.10 = (f32[192,384]{1,0:T(8,128)S(1)}, f32[192,384]{1,0:T(8,128)S(1)}, u32[]{:S(2)}, u32[]{:S(2)}) collective-permute-start(f32[192,384]{1,0:T(8,128)S(1)} %get-tuple-element.12), channel_id=1, source_target_pairs={{0,4},{4,0},{8,12},{12,8},{16,20},{20,16},{24,28},{28,24},{1,5},{5... | collective-permute-start | bytes 884744 | tf_op jit(solution)/shard_map/ppermute | solution.py:17
  108.6 20.1 %all-to-all-start = ((bf16[32,8,1152]{2,1,0:T(8,128)(2,1)}), bf16[32,8,1152]{2,1,0:T(8,128)(2,1)S(1)}, u32[]{:S(2)}, u32[]{:S(2)}) async-start(bf16[32,8,1152]{2,1,0:T(8,128)(2,1)} %bitcast.4), calls=%async_computation | async-start | bytes 1179648 | tf_op jit(solution)/shard_map/all_to_all | solution.py:208

commit v2 on v1

--- a/solution.py
+++ b/solution.py
@@ -139,7 +139,6 @@
     own = lax.dynamic_slice(train, (0, core * deep), (rows, deep))
 
     placed = jnp.take(source_place, example_source)
-    placed_all = lax.all_gather(placed, BOTH, tiled=True).reshape(devices, rows)
     capacity = max(1, -(-2 * rows // devices))
     full, rest = capacity // 8 * 8, capacity % 8
     if rest > 4:
@@ -153,20 +152,20 @@
         groups += [jnp.where(late, goal * 8 + g * 4 + rank - full, -1) for g in range(2)]
     target = jnp.stack(groups)
 
-    mine = placed_all // table_rows == me_ex * pb + me_pb
-    rank_all = jnp.cumsum(mine.astype(jnp.int32), axis=1) - 1
-    slot_all = placed_all % table_rows
-
-    def slots(rank_wanted):
-        hit = mine[:, None, :] & (rank_all[:, None, :] == rank_wanted[None, :, None])
-        found = jnp.sum(jnp.where(hit, slot_all[:, None, :] + 1, 0), axis=2) - 1
-        return found.reshape(devices * 8)
-
-    eight = jnp.arange(8, dtype=jnp.int32)
-    slot_groups = [slots(eight + 8 * index) for index in range(full // 8)]
+    lanes = -(-capacity // 128) * 128
+    there = goal[None, None, :] == jnp.arange(devices, dtype=jnp.int32)[:, None, None]
+    hit = there & (rank[None, None, :] == jnp.arange(capacity, dtype=jnp.int32)[None, :, None])
+    wanted = jnp.sum(jnp.where(hit, (placed % table_rows + 1)[None, None, :], 0), axis=2) - 1
+    wanted = jnp.pad(wanted, ((0, 0), (0, lanes - capacity)), constant_values=-1)
+    slot_all = lax.all_to_all(wanted.reshape(devices, 1, lanes), BOTH, split_axis=0, concat_axis=0)
+    slot_all = jnp.pad(slot_all[:, 0, :capacity], ((0, 0), (0, 8)), constant_values=-1)
+
+    slot_groups = [slot_all[:, 8 * index : 8 * index + 8] for index in range(full // 8)]
     if rest:
-        slot_groups += [slots(jnp.where(eight // 4 == g, full + eight % 4, rows)) for g in range(2)]
-    slot = jnp.stack(slot_groups)
+        tail = jnp.where(jnp.arange(4) < rest, slot_all[:, full : full + 4], -1)
+        none = jnp.full_like(tail, -1)
+        slot_groups += [jnp.concatenate(pair, axis=1) for pair in ((tail, none), (none, tail))]
+    slot = jnp.stack(slot_groups).reshape(len(slot_groups), devices * 8)
 
     early = [front, back] + x_one + y_one
     early_own, early_other = partials(own, other, early)

time: 131 us -> 101 us (0.77)
  blocking collectives: 53.3 us -> 0 us
  waiting for transfers between devices: 26.2 us -> 46.3 us
  starting transfers between devices: 14 us -> 21.5 us
  other arithmetic: 6.96 us -> 0.65 us
  Pallas kernels: 12.7 us -> 14.8 us
    unnamed x1 -> x0, blocking collectives: 53.3 us -> none
    ppermute x11, waiting for transfers between devices: 10.7 us -> 29.2 us  [moved(): return lax.ppermute(value, axis, [(i, target(i)) for i in range(count)])]
    all_to_all x0 -> x1, starting transfers between devices: none -> 4.89 us  [on_device(): lax.all_to_all(wanted.reshape(devices, 1, lanes), BOTH, split_axis=0, con...]
    all_to_all x1, starting transfers between devices: 2.61 us -> 5.68 us  [on_device(): lax.all_to_all(packed.reshape(devices, 8, payload), BOTH, split_axis=0, c...]
    add x5, other arithmetic: 2.85 us -> 0.02 us  [on_device(): span = lambda start, count: start + jnp.arange(count, dtype=jnp.int32)]
    unnamed x17 -> x14, local copies, waits for them, and re-layouts: 0.61 us -> 2.4 us
    all_to_all x1, waiting for transfers between devices: 15.5 us -> 17.1 us  [on_device(): lax.all_to_all(packed.reshape(devices, 8, payload), BOTH, split_axis=0, c...]
    reduce_sum x1, other arithmetic: 1.71 us -> 0.28 us  [on_device(): jnp.sum(jnp.where(hit, (placed % table_rows + 1)[None, None, :], 0), axis=2)]
  transfers between devices with their start and end apart: 12 -> 13, of which waited for: 4 -> 5; matrix products, arithmetic and copies ran while one was open for 15% -> 12% of each run, Pallas kernels for 7% -> 13%
where the time goes in v2:
time: 101 us; the launch traced here: 100 us
  waiting for transfers between devices  46.3 us (46%)
  starting transfers between devices  21.5 us (21%)
  local copies, waits for them, and re-layouts  17 us (17%)
  Pallas kernels  14.8 us (15%)
    ppermute x11, waiting for transfers between devices, moved(): return lax.ppermute(value, axis, [(i, target(i)) for i in range(count)])  29.2 us
    all_to_all x1, waiting for transfers between devices, on_device(): lax.all_to_all(packed.reshape(devices, 8, payload), BOTH, split_axis=0, c...  17.1 us
    ppermute x11, starting transfers between devices, moved(): return lax.ppermute(value, axis, [(i, target(i)) for i in range(count)])  10.9 us
    pallas_call x2, Pallas kernels, partials(): pl.pallas_call(functools.partial(partial_kernel, len(pieces)), grid=(dept...  10.7 us
    all_to_all x1, starting transfers between devices, on_device(): lax.all_to_all(packed.reshape(devices, 8, payload), BOTH, split_axis=0, c...  5.68 us
    all_to_all x1, starting transfers between devices, on_device(): lax.all_to_all(wanted.reshape(devices, 1, lanes), BOTH, split_axis=0, con...  4.89 us
    slice x2, local copies, waits for them, and re-layouts, on_device(): v[:lent]  3.72 us
    dynamic_slice x1, local copies, waits for them, and re-layouts, on_device(): lax.dynamic_slice(train, (0, (1 - core) * deep), (rows, deep))  3.43 us
  transfers between devices with their start and end apart: 13, of which 5 were waited for; matrix products, arithmetic and copies ran while one was open for 12% of the time, Pallas kernels for 13%

profile of v2, /device:TPU:0, one launch (start us, length us, event | category | flops | bytes accessed | tf_op | source)
XLA Modules:
  0.0 100.4 jit_solution(13370771061938844404)
XLA Ops:
  0.0 3.4 %constant_dynamic-slice_fusion = (bf16[192,4096]{1,0:T(8,128)(2,1)}, bf16[192,4096]{1,0:T(8,128)(2,1)S(1)}) fusion(bf16[192,8192]{1,0:T(8,128)(2,1)} %param.5, s32[]{:T(128)S(6)} %select_n.167, s32[]{:T(128)S(6)} %select_n.166), kind=kLoop, calls=%fused_computation.44 | loop fusion | bytes 6291464 | tf_op jit(solution)/shard_map/dynamic_slice | solution.py:138
  3.4 0.5 collective-permute-start
  3.9 2.7 %fusion.4 = (bf16[96,4096]{1,0:T(8,128)(2,1)}, bf16[96,4096]{1,0:T(8,128)(2,1)}) fusion(bf16[192,8192]{1,0:T(8,128)(2,1)} %param.6, s32[]{:T(128)S(6)} %select_n.171, s32[]{:T(128)S(6)} %select_n.166, s32[]{:T(128)S(6)} %select_n.170), kind=kLoop, calls=%fused_computation.47 | loop fusion | bytes 3145740 | tf_op jit(solution)/shard_map/dynamic_slice | solution.py:132
  6.6 2.5 %collective-permute-start.1 = (bf16[96,4096]{1,0:T(8,128)(2,1)}, bf16[96,4096]{1,0:T(8,128)(2,1)}, u32[]{:S(2)}, u32[]{:S(2)}) collective-permute-start(bf16[96,4096]{1,0:T(8,128)(2,1)} %get-tuple-element.16.refs_0_), channel_id=1, source_target_pairs={{0,1},{1,0},{2,3},{3,2},{4,5},{5,4},{6,7},{7,6},{8,9},{9,8},{10,11... | collective-permute-start | bytes 2359304 | tf_op jit(solution)/shard_map/ppermute | solution.py:17
  9.1 1.5 %collective-permute-start.2 = (bf16[96,4096]{1,0:T(8,128)(2,1)}, bf16[96,4096]{1,0:T(8,128)(2,1)}, u32[]{:S(2)}, u32[]{:S(2)}) collective-permute-start(bf16[96,4096]{1,0:T(8,128)(2,1)} %get-tuple-element.15.refs_1_), channel_id=1, source_target_pairs={{0,2},{1,3},{2,0},{3,1},{4,6},{5,7},{6,4},{7,5},{8,10},{9,11},{10,... | collective-permute-start | bytes 2359304 | tf_op jit(solution)/shard_map/ppermute | solution.py:17
  10.6 1.9 %fusion.3 = (bf16[32,4096]{1,0:T(8,128)(2,1)}, bf16[32,4096]{1,0:T(8,128)(2,1)}) fusion(bf16[192,8192]{1,0:T(8,128)(2,1)} %param.6, s32[]{:T(128)S(6)} %add.304, s32[]{:T(128)S(6)} %select_n.166, s32[]{:T(128)S(6)} %add.303), kind=kLoop, calls=%fused_computation.46 | loop fusion | bytes 1048588 | tf_op jit(solution)/shard_map/slice | solution.py:137
  12.5 0.5 collective-permute-start.8
  13.0 1.4 %gather_fusion = s32[192]{0:T(256)S(1)} fusion(s32[8192]{0:T(1024)S(1)} %copy-done, s32[1024]{0:T(1024)S(1)} %pad_clamp_fusion), kind=kCustom, calls=%fused_computation | custom fusion | bytes 2304 | tf_op jit(solution)/shard_map/jit(_take)/gather | solution.py:141
  14.5 0.2 convert_reduce_fusion
  14.7 0.3 select_reduce_fusion
  15.0 14.0 %collective-permute-done.2.refs_3_ = bf16[96,4096]{1,0:T(8,128)(2,1)} collective-permute-done((bf16[96,4096]{1,0:T(8,128)(2,1)}, bf16[96,4096]{1,0:T(8,128)(2,1)}, u32[]{:S(2)}, u32[]{:S(2)}) %collective-permute-start.2) | collective-permute-done | bytes 786464 | tf_op jit(solution)/shard_map/ppermute | solution.py:17
  29.1 0.3 collective-permute-start.4
  29.4 0.0 collective-permute-done.1.refs_2_
  29.4 1.7 %collective-permute-start.5 = (bf16[96,4096]{1,0:T(8,128)(2,1)}, bf16[96,4096]{1,0:T(8,128)(2,1)}, u32[]{:S(2)}, u32[]{:S(2)}) collective-permute-start(bf16[96,4096]{1,0:T(8,128)(2,1)} %collective-permute-done.1.refs_2_), channel_id=1, source_target_pairs={{0,2},{1,3},{2,0},{3,1},{4,6},{5,7},{6,4},{7,5},{8,10},{9,11},{10,... | collective-permute-start | bytes 2359304 | tf_op jit(solution)/shard_map/ppermute | solution.py:17
  31.1 0.7 copy.12
  31.8 4.9 %all-to-all-start.1 = ((s32[32,1,128]{2,1,0:T(1,128)}), s32[32,1,128]{2,1,0:T(1,128)S(1)}, u32[]{:S(2)}, u32[]{:S(2)}) async-start(s32[32,1,128]{2,1,0:T(1,128)} %copy.12), calls=%async_computation.1 | async-start | bytes 32768 | tf_op jit(solution)/shard_map/all_to_all | solution.py:160
  36.8 1.9 %slice.32 = bf16[64,4096]{1,0:T(8,128)(2,1)} slice(bf16[96,4096]{1,0:T(8,128)(2,1)} %collective-permute-done.1.refs_2_), slice={[0:64], [0:4096]} | slice | bytes 1048576 | tf_op jit(solution)/shard_map/slice | solution.py:174
  38.7 1.8 %collective-permute-start.6 = (bf16[64,4096]{1,0:T(8,128)(2,1)}, bf16[64,4096]{1,0:T(8,128)(2,1)}, u32[]{:S(2)}, u32[]{:S(2)}) collective-permute-start(bf16[64,4096]{1,0:T(8,128)(2,1)} %slice.32), channel_id=1, source_target_pairs={{0,8},{4,12},{8,0},{12,4},{16,24},{20,28},{24,16},{28,20},{1,9},{5... | collective-permute-start | bytes 1572872 | tf_op jit(solution)/shard_map/ppermute | solution.py:17
  40.4 1.9 %slice.33 = bf16[64,4096]{1,0:T(8,128)(2,1)} slice(bf16[96,4096]{1,0:T(8,128)(2,1)} %collective-permute-done.2.refs_3_), slice={[0:64], [0:4096]} | slice | bytes 1048576 | tf_op jit(solution)/shard_map/slice | solution.py:175
  42.3 0.0 collective-permute-done.8.refs_4_
  42.3 0.7 copy-done.3
  43.0 0.3 collective-permute-start.7
  43.3 0.0 collective-permute-done.other_ref
  43.3 1.8 %collective-permute-start.9 = (bf16[32,4096]{1,0:T(8,128)(2,1)}, bf16[32,4096]{1,0:T(8,128)(2,1)}, u32[]{:S(2)}, u32[]{:S(2)}) collective-permute-start(bf16[32,4096]{1,0:T(8,128)(2,1)} %get-tuple-element.13), channel_id=1, source_target_pairs={{0,2},{1,3},{2,0},{3,1},{4,6},{5,7},{6,4},{7,5},{8,10},{9,11},{10,... | collective-permute-start | bytes 786440 | tf_op jit(solution)/shard_map/ppermute | solution.py:17
  45.2 5.4 %shard_map.55 = (f32[192,384]{1,0:T(8,128)S(1)}, f32[192,384]{1,0:T(8,128)}) custom-call(bf16[192,4096]{1,0:T(8,128)(2,1)S(1)} %get-tuple-element.18.own_ref, bf16[192,4096]{1,0:T(8,128)(2,1)S(1)} %collective-permute-done.other_ref, bf16[96,4096]{1,0:T(8,128)(2,1)} %get-tuple-element.16.refs_0_, bf16[96,4096]{1,0:T(8,128)(2,1)} %get-tuple-element.15.refs_1_, ...), custom_call_target="tpu_custom_call" | custom-call | flops 1207959552 | bytes 6291456 | tf_op jit(solution)/shard_map/pallas_call | solution.py:39
  50.6 3.8 %collective-permute-done.9.refs_5_ = bf16[32,4096]{1,0:T(8,128)(2,1)} collective-permute-done((bf16[32,4096]{1,0:T(8,128)(2,1)}, bf16[32,4096]{1,0:T(8,128)(2,1)}, u32[]{:S(2)}, u32[]{:S(2)}) %collective-permute-start.9) | collective-permute-done | bytes 262176 | tf_op jit(solution)/shard_map/ppermute | solution.py:17
  54.4 0.0 collective-permute-start.3
  54.4 0.0 collective-permute-done.6.refs_2_
  54.4 10.0 %collective-permute-done.7.refs_3_ = bf16[64,4096]{1,0:T(8,128)(2,1)} collective-permute-done((bf16[64,4096]{1,0:T(8,128)(2,1)}, bf16[64,4096]{1,0:T(8,128)(2,1)}, u32[]{:S(2)}, u32[]{:S(2)}) %collective-permute-start.7) | collective-permute-done | bytes 524320 | tf_op jit(solution)/shard_map/ppermute | solution.py:17
  64.4 0.0 collective-permute-done.4.refs_0_
  64.4 0.0 collective-permute-done.5.refs_1_
  64.4 5.3 %shard_map.56 = (f32[192,384]{1,0:T(8,128)S(1)}, f32[192,384]{1,0:T(8,128)}) custom-call(bf16[192,4096]{1,0:T(8,128)(2,1)S(1)} %get-tuple-element.18.own_ref, bf16[192,4096]{1,0:T(8,128)(2,1)S(1)} %collective-permute-done.other_ref, bf16[96,4096]{1,0:T(8,128)(2,1)} %collective-permute-done.4.refs_0_, bf16[96,4096]{1,0:T(8,128)(2,1)} %collective-permute-done.5.refs_1_, ...), custom_call_target="tpu_custom_call" | custom-call | flops 1207959552 | bytes 6291456 | tf_op jit(solution)/shard_map/pallas_call | solution.py:39
  69.7 0.7 copy-done.1
  70.4 0.0 collective-permute-start.10
  70.4 0.1 copy.10.residual_ref
  70.5 0.1 concatenate.10
  70.6 0.2 broadcast_in_dim.56.column_ref
  70.8 1.4 %collective-permute-done.10.got_b = f32[192,384]{1,0:T(8,128)S(1)} collective-permute-done((f32[192,384]{1,0:T(8,128)}, f32[192,384]{1,0:T(8,128)S(1)}, u32[]{:S(2)}, u32[]{:S(2)}) %collective-permute-start.10) | collective-permute-done | bytes 294944 | tf_op jit(solution)/shard_map/ppermute | solution.py:17
  72.2 1.0 copy-done.2
  73.1 2.8 %shard_map.57 = bf16[256,1152]{1,0:T(8,128)(2,1)} custom-call(f32[192,384]{1,0:T(8,128)S(1)} %get-tuple-element.9.own_a, f32[192,384]{1,0:T(8,128)} %collective-permute-done.3.got_a, f32[192,384]{1,0:T(8,128)S(1)} %copy-done.2, f32[192,384]{1,0:T(8,128)S(1)} %collective-permute-done.10.got_b, f32[192,1]{1,0:T(8,128)S(1)} %copy.10.residual_ref, ...), custom_call_target="tpu_custom_call" | custom-call | tf_op jit(solution)/shard_map/pallas_call | solution.py:202
  75.9 5.7 %all-to-all-start = ((bf16[32,8,1152]{2,1,0:T(8,128)(2,1)}), bf16[32,8,1152]{2,1,0:T(8,128)(2,1)S(1)}, u32[]{:S(2)}, u32[]{:S(2)}) async-start(bf16[32,8,1152]{2,1,0:T(8,128)(2,1)} %bitcast.4), calls=%async_computation | async-start | bytes 1179648 | tf_op jit(solution)/shard_map/all_to_all | solution.py:207
  81.6 0.1 slice_select_fusion
  81.7 0.1 fusion.5
  81.8 0.1 stack.21
  81.8 0.1 stack.20
  81.9 0.1 stack.19
  82.0 17.1 %all-to-all-done = bf16[32,8,1152]{2,1,0:T(8,128)(2,1)S(1)} async-done(((bf16[32,8,1152]{2,1,0:T(8,128)(2,1)}), bf16[32,8,1152]{2,1,0:T(8,128)(2,1)S(1)}, u32[]{:S(2)}, u32[]{:S(2)}) %all-to-all-start) | async-done | bytes 589856 | tf_op jit(solution)/shard_map/all_to_all | solution.py:207
  99.1 1.3 %shard_map.58 = f32[256,768]{1,0:T(8,128)} custom-call(bf16[256,1152]{1,0:T(8,128)(2,1)S(1)} %bitcast.11, s32[3,256]{1,0:T(4,128)S(1)} %pad_add_fusion.1.slot_ref), custom_call_target="tpu_custom_call" | custom-call | tf_op jit(solution)/shard_map/pallas_call | solution.py:208
  (29 shorter events, 0.1 us)
Async XLA Ops:
  0.0 13.0 %copy-start = (s32[8192]{0:T(1024)S(1)}, s32[8192]{0:T(1024)}, u32[]{:S(2)}) copy-start(s32[8192]{0:T(1024)} %param.9) | copy-start | bytes 98308
  3.4 9.6 %copy-start.5 = (s32[192]{0:T(256)S(1)}, s32[192]{0:T(256)}, u32[]{:S(2)}) copy-start(s32[192]{0:T(256)} %param.8) | copy-start | bytes 2308
  3.4 39.9 %collective-permute-start = (bf16[192,4096]{1,0:T(8,128)(2,1)}, bf16[192,4096]{1,0:T(8,128)(2,1)S(1)}, u32[]{:S(2)}, u32[]{:S(2)}) collective-permute-start(bf16[192,4096]{1,0:T(8,128)(2,1)} %get-tuple-element.17), channel_id=1, source_target_pairs={{0,4},{4,0},{8,12},{12,8},{16,20},{20,16},{24,28},{28,24},{1,5},{5... | collective-permute-start | bytes 4718600 | tf_op jit(solution)/shard_map/ppermute | solution.py:17
  6.6 22.8 %collective-permute-start.1 = (bf16[96,4096]{1,0:T(8,128)(2,1)}, bf16[96,4096]{1,0:T(8,128)(2,1)}, u32[]{:S(2)}, u32[]{:S(2)}) collective-permute-start(bf16[96,4096]{1,0:T(8,128)(2,1)} %get-tuple-element.16.refs_0_), channel_id=1, source_target_pairs={{0,1},{1,0},{2,3},{3,2},{4,5},{5,4},{6,7},{7,6},{8,9},{9,8},{10,11... | collective-permute-start | bytes 2359304 | tf_op jit(solution)/shard_map/ppermute | solution.py:17
  9.1 20.0 %collective-permute-start.2 = (bf16[96,4096]{1,0:T(8,128)(2,1)}, bf16[96,4096]{1,0:T(8,128)(2,1)}, u32[]{:S(2)}, u32[]{:S(2)}) collective-permute-start(bf16[96,4096]{1,0:T(8,128)(2,1)} %get-tuple-element.15.refs_1_), channel_id=1, source_target_pairs={{0,2},{1,3},{2,0},{3,1},{4,6},{5,7},{6,4},{7,5},{8,10},{9,11},{10,... | collective-permute-start | bytes 2359304 | tf_op jit(solution)/shard_map/ppermute | solution.py:17
  12.5 29.8 %collective-permute-start.8 = (bf16[32,4096]{1,0:T(8,128)(2,1)}, bf16[32,4096]{1,0:T(8,128)(2,1)S(1)}, u32[]{:S(2)}, u32[]{:S(2)}) collective-permute-start(bf16[32,4096]{1,0:T(8,128)(2,1)} %get-tuple-element.14), channel_id=1, source_target_pairs={{0,1},{1,0},{2,3},{3,2},{4,5},{5,4},{6,7},{7,6},{8,9},{9,8},{10,11... | collective-permute-start | bytes 786440 | tf_op jit(solution)/shard_map/ppermute | solution.py:17
  29.1 35.3 %collective-permute-start.4 = (bf16[96,4096]{1,0:T(8,128)(2,1)}, bf16[96,4096]{1,0:T(8,128)(2,1)}, u32[]{:S(2)}, u32[]{:S(2)}) collective-permute-start(bf16[96,4096]{1,0:T(8,128)(2,1)} %collective-permute-done.2.refs_3_), channel_id=1, source_target_pairs={{0,1},{1,0},{2,3},{3,2},{4,5},{5,4},{6,7},{7,6},{8,9},{9,8},{10,11... | collective-permute-start | bytes 2359304 | tf_op jit(solution)/shard_map/ppermute | solution.py:17
  29.4 35.0 %collective-permute-start.5 = (bf16[96,4096]{1,0:T(8,128)(2,1)}, bf16[96,4096]{1,0:T(8,128)(2,1)}, u32[]{:S(2)}, u32[]{:S(2)}) collective-permute-start(bf16[96,4096]{1,0:T(8,128)(2,1)} %collective-permute-done.1.refs_2_), channel_id=1, source_target_pairs={{0,2},{1,3},{2,0},{3,1},{4,6},{5,7},{6,4},{7,5},{8,10},{9,11},{10,... | collective-permute-start | bytes 2359304 | tf_op jit(solution)/shard_map/ppermute | solution.py:17
  31.8 44.1 %all-to-all-start.1 = ((s32[32,1,128]{2,1,0:T(1,128)}), s32[32,1,128]{2,1,0:T(1,128)S(1)}, u32[]{:S(2)}, u32[]{:S(2)}) async-start(s32[32,1,128]{2,1,0:T(1,128)} %copy.12), calls=%async_computation.1 | async-start | bytes 32768 | tf_op jit(solution)/shard_map/all_to_all | solution.py:160
  38.7 15.7 %collective-permute-start.6 = (bf16[64,4096]{1,0:T(8,128)(2,1)}, bf16[64,4096]{1,0:T(8,128)(2,1)}, u32[]{:S(2)}, u32[]{:S(2)}) collective-permute-start(bf16[64,4096]{1,0:T(8,128)(2,1)} %slice.32), channel_id=1, source_target_pairs={{0,8},{4,12},{8,0},{12,4},{16,24},{20,28},{24,16},{28,20},{1,9},{5... | collective-permute-start | bytes 1572872 | tf_op jit(solution)/shard_map/ppermute | solution.py:17
  42.3 0.7 copy-start.3
  43.0 21.3 %collective-permute-start.7 = (bf16[64,4096]{1,0:T(8,128)(2,1)}, bf16[64,4096]{1,0:T(8,128)(2,1)}, u32[]{:S(2)}, u32[]{:S(2)}) collective-permute-start(bf16[64,4096]{1,0:T(8,128)(2,1)} %slice.33), channel_id=1, source_target_pairs={{0,8},{4,12},{8,0},{12,4},{16,24},{20,28},{24,16},{28,20},{1,9},{5... | collective-permute-start | bytes 1572872 | tf_op jit(solution)/shard_map/ppermute | solution.py:17
  43.3 11.1 %collective-permute-start.9 = (bf16[32,4096]{1,0:T(8,128)(2,1)}, bf16[32,4096]{1,0:T(8,128)(2,1)}, u32[]{:S(2)}, u32[]{:S(2)}) collective-permute-start(bf16[32,4096]{1,0:T(8,128)(2,1)} %get-tuple-element.13), channel_id=1, source_target_pairs={{0,2},{1,3},{2,0},{3,1},{4,6},{5,7},{6,4},{7,5},{8,10},{9,11},{10,... | collective-permute-start | bytes 786440 | tf_op jit(solution)/shard_map/ppermute | solution.py:17
  45.2 19.2 %copy-start.4 = (bf16[32,4096]{1,0:T(8,128)(2,1)S(1)}, bf16[32,4096]{1,0:T(8,128)(2,1)}, u32[]{:S(2)}) copy-start(bf16[32,4096]{1,0:T(8,128)(2,1)} %copy-done.3) | copy-start | bytes 786436
  54.4 16.0 %copy-start.6 = (f32[192]{0:T(256)S(1)}, f32[192]{0:T(256)}, u32[]{:S(2)}) copy-start(f32[192]{0:T(256)} %param.7) | copy-start | bytes 2308
  54.4 16.4 %collective-permute-start.3 = (f32[192,384]{1,0:T(8,128)}, f32[192,384]{1,0:T(8,128)}, u32[]{:S(2)}, u32[]{:S(2)}) collective-permute-start(f32[192,384]{1,0:T(8,128)} %get-tuple-element.10), channel_id=1, source_target_pairs={{0,4},{4,0},{8,12},{12,8},{16,20},{20,16},{24,28},{28,24},{1,5},{5... | collective-permute-start | bytes 884744 | tf_op jit(solution)/shard_map/ppermute | solution.py:17
  69.7 0.7 copy-start.1
  70.4 1.8 %collective-permute-start.10 = (f32[192,384]{1,0:T(8,128)}, f32[192,384]{1,0:T(8,128)S(1)}, u32[]{:S(2)}, u32[]{:S(2)}) collective-permute-start(f32[192,384]{1,0:T(8,128)} %get-tuple-element.12), channel_id=1, source_target_pairs={{0,4},{4,0},{8,12},{12,8},{16,20},{20,16},{24,28},{28,24},{1,5},{5... | collective-permute-start | bytes 884744 | tf_op jit(solution)/shard_map/ppermute | solution.py:17
  72.2 1.0 copy-start.2
  75.9 23.2 %all-to-all-start = ((bf16[32,8,1152]{2,1,0:T(8,128)(2,1)}), bf16[32,8,1152]{2,1,0:T(8,128)(2,1)S(1)}, u32[]{:S(2)}, u32[]{:S(2)}) async-start(bf16[32,8,1152]{2,1,0:T(8,128)(2,1)} %bitcast.4), calls=%async_computation | async-start | bytes 1179648 | tf_op jit(solution)/shard_map/all_to_all | solution.py:207

commit v3 on v0

v3 whole, which is shorter than its diff:
```python
import functools

import jax
import jax.numpy as jnp
from jax import lax
from jax.experimental import pallas as pl
from jax.experimental.pallas import tpu as pltpu
from jax.sharding import PartitionSpec as P

BOTH = ("ex", "pb")
NT = (((1,), (1,)), ((), ()))
TN = (((0,), (0,)), ((), ()))
LIMIT = pltpu.CompilerParams(vmem_limit_bytes=20 << 20)
FULL = pltpu.CompilerParams(vmem_limit_bytes=60 << 20)
LIGHT = pl.CostEstimate(flops=1, bytes_accessed=1, transcendentals=0)
HBM = pl.BlockSpec(memory_space=pltpu.HBM)
VMEM = pl.BlockSpec(memory_space=pltpu.VMEM)


def moved(value, axis, target):
    count = lax.axis_size(axis)
    return lax.ppermute(value, axis, [(i, target(i)) for i in range(count)])


def one_hot(hits):
    return jnp.where(hits, 1.0, 0.0).astype(jnp.bfloat16)


def pick(select, values):
    return jnp.dot(select, values, preferred_element_type=jnp.float32)


def scores_kernel(groups, count, *refs):
    held, sides = sum(groups), len(groups)
    rows, pieces, outs = refs[:held], refs[held : held + count], refs[held + count :]
    stack = lambda arrays: arrays[0][...] if len(arrays) == 1 else jnp.concatenate([a[...] for a in arrays], axis=0)
    total = lax.dot_general(stack(rows), stack(pieces), NT, preferred_element_type=jnp.float32)
    at = 0
    for out in outs:
        out[...] = total[at : at + out.shape[0]]
        at += out.shape[0]


def scored(groups, pieces):
    width = sum(piece.shape[0] for piece in pieces)
    arrays = [rows for group in groups for rows in group]
    shapes = [jax.ShapeDtypeStruct((sum(rows.shape[0] for rows in group), width), jnp.float32) for group in groups]
    return pl.pallas_call(
        functools.partial(scores_kernel, [len(group) for group in groups], len(pieces)),
        out_shape=shapes,
        compiler_params=LIMIT,
        cost_estimate=LIGHT,
    )(*arrays, *pieces)


def relayed(body, inputs, shapes, rooms, sems, limit):
    return pl.pallas_call(
        body,
        in_specs=[HBM] * len(inputs),
        out_specs=[HBM] * len(shapes),
        out_shape=[jax.ShapeDtypeStruct(shape, inputs[0].dtype) for shape in shapes],
        scratch_shapes=[pltpu.VMEM(room, inputs[0].dtype) for room in rooms] + [pltpu.SemaphoreType.DMA((sems,))],
        compiler_params=limit,
        cost_estimate=LIGHT,
    )(*inputs)


def relay(sems, plan):
    arriving, leaving, at = [], [], 0
    for source, room, _ in plan:
        arriving.append(pltpu.make_async_copy(source, room, sems.at[at]))
        arriving[-1].start()
        at += 1
    for copy, (_, room, targets) in zip(arriving, plan):
        copy.wait()
        for target in targets:
            leaving.append(pltpu.make_async_copy(room, target, sems.at[at]))
            leaving[-1].start()
            at += 1
    for copy in leaving:
        copy.wait()


def cut_queries(query, lent):
    half, deep = query.shape[0] // 2, query.shape[1] // 2
    ends = half - lent

    def body(query_ref, front_ref, back_ref, x_ref, y_ref, held, sems):
        core, layer = lax.axis_index("ex") % 2, lax.axis_index("ex") // 2 % 2
        columns = pl.ds(pl.multiple_of(core * deep, 128), deep)
        starts = [layer * half, half - layer * half]
        rows = lambda start, count: query_ref.at[pl.ds(pl.multiple_of(start, 16), count), columns]
        plan = []
        for side, (start, head) in enumerate(zip(starts, (front_ref, back_ref))):
            plan.append((rows(start, lent), held.at[side, pl.ds(0, lent)], [head]))
        for side, start in enumerate(starts):
            targets = [x_ref.at[pl.ds(side * ends, ends)], y_ref.at[pl.ds((1 - side) * ends, ends)]]
            plan.append((rows(start + lent, ends), held.at[side, pl.ds(lent, ends)], targets))
        relay(sems, plan)

    shapes = [(lent, deep)] * 2 + [(2 * ends, deep)] * 2
    return relayed(body, [query], shapes, [(2, half, deep)], 10, FULL)


def cut_examples(train, count):
    rows, deep = train.shape[0], train.shape[1] // 2
    height = rows // count

    def body(train_ref, own_ref, *others):
        core = lax.axis_index("ex") % 2
        for side in range(2):

            @pl.when(core == side)
            def _():
                own_ref[...] = train_ref[:, side * deep : (side + 1) * deep]
                for index, other in enumerate(others):
                    span = slice(index * height, (index + 1) * height)
                    other[...] = train_ref[span, (1 - side) * deep : (2 - side) * deep]

    shapes = [jax.ShapeDtypeStruct(shape, train.dtype) for shape in [(rows, deep)] + [(height, deep)] * count]
    own, *others = pl.pallas_call(body, out_shape=shapes, compiler_params=LIMIT, cost_estimate=LIGHT)(train)
    return own, others


def stacked(*outputs):
    arrays = []
    for output in outputs:
        for array, _, _ in output:
            if not any(array is known for known in arrays):
                arrays.append(array)
    index_of = lambda array: next(index for index, known in enumerate(arrays) if known is array)
    plans = [[(index_of(array), first, count) for array, first, count in output] for output in outputs]

    def body(*refs):
        for plan, out in zip(plans, refs[len(arrays) :]):
            at = 0
            for index, first, count in plan:
                out[at : at + count] = refs[index][first : first + count]
                at += count

    deep = arrays[0].shape[1]
    shapes = [jax.ShapeDtypeStruct((sum(p[2] for p in plan), deep), arrays[0].dtype) for plan in plans]
    return pl.pallas_call(body, out_shape=shapes, compiler_params=LIMIT, cost_estimate=LIGHT)(*arrays)


class Slots:
    def __init__(self, capacity, width, ids):
        self.width = width
        self.full, rest = capacity // 8, capacity % 8
        if rest > 4:
            self.full, rest = self.full + 1, 0
        self.half = width // 2 if rest else 0
        self.groups = self.full + (1 if rest else 0)
        self.at = self.full * width
        self.ids = self.at + self.half
        self.lanes = self.ids + (2 * self.groups if ids else 0)


def ordered(slots, scores, spans):
    rows, total, at = scores.shape[0], None, 0
    for base, count in spans:
        if base is not None:
            column = lax.broadcasted_iota(jnp.int32, (count, slots.width), 0) + base
            place = lax.broadcasted_iota(jnp.int32, (count, slots.width), 1)
            part = pick(scores[:, at : at + count], one_hot(place == column))
            total = part if total is None else total + part
        at += count
    return total


def weighted(own, got, scale):
    return ((own[...] if got is None else own[...] + got[...]) * scale[...]).astype(jnp.bfloat16)


def selects(slots, table_rows, height, placed_row, placed_column):
    rows = placed_row.shape[1]
    goal = placed_row[...] // table_rows
    same = placed_column[...] // table_rows == goal
    before = lax.broadcasted_iota(jnp.int32, (rows, rows), 0) < lax.broadcasted_iota(jnp.int32, (rows, rows), 1)
    rank = jnp.sum(jnp.where(same & before, 1, 0), axis=0, keepdims=True)
    row = lax.broadcasted_iota(jnp.int32, (height, rows), 0)
    found = [one_hot(row == jnp.where(rank // 8 == index, goal * 8 + rank % 8, -1)) for index in range(slots.full)]
    if slots.half:
        late = rank - slots.full * 8
        found += [one_hot(row == jnp.where(late >= 0, goal * 8 + side * 4 + late, -1)) for side in range(2)]
    return found


def digits(slots, table_rows, placed_column):
    number = placed_column[...] % table_rows + 1
    lane = lax.broadcasted_iota(jnp.int32, (number.shape[0], 2 * slots.groups), 1)
    digit = jnp.where(lane % 2 == 0, number // 128, number % 128)
    kept = [jnp.where(lane // 2 == index, digit, 0) for index in range(slots.groups)]
    return [value.astype(jnp.float32).astype(jnp.bfloat16) for value in kept]


def put(slots, found, table, out_ref, ids=None, base_ref=None):
    table = table.astype(jnp.bfloat16)

    def write(start, values):
        values, span = values.astype(jnp.bfloat16), slice(start, start + values.shape[1])
        out_ref[:, span] = values if base_ref is None else values + base_ref[:, span]

    for index in range(slots.full):
        write(index * slots.width, pick(found[index], table))
    if slots.half:
        left, right = (pick(found[slots.full + i], table[:, i * slots.half : (i + 1) * slots.half]) for i in range(2))
        write(slots.at, left + right)
    if ids is not None:
        pairs = [(found[index], ids[min(index, slots.full)]) for index in range(len(found))]
        write(slots.ids, sum(pick(select, digit) for select, digit in pairs))


def called(body, shapes, *operands):
    return pl.pallas_call(body, out_shape=shapes, compiler_params=LIMIT, cost_estimate=LIGHT)(*operands)


def exchanged(rows, devices):
    apart = rows.reshape(devices, 8, rows.shape[1])
    return lax.all_to_all(apart, BOTH, split_axis=0, concat_axis=0).reshape(rows.shape)


def received(slots, ref, index):
    if index < slots.full:
        return ref[:, index * slots.width : (index + 1) * slots.width]
    half = ref[:, slots.at : slots.at + slots.half]
    row = lax.broadcasted_iota(jnp.int32, (half.shape[0], slots.width), 0)
    lane = lax.broadcasted_iota(jnp.int32, (half.shape[0], slots.width), 1)
    return jnp.where((row % 8 < 4) == (lane < slots.half), jnp.concatenate([half, half], axis=1), 0)


def places(pb, count, width):
    sender = lax.broadcasted_iota(jnp.int32, (count, width), 0) // 8 % pb
    return sender, lax.broadcasted_iota(jnp.int32, (count, width), 1) // (width // pb)


def first_table_kernel(slots, pb, table_rows, got_ref, out_ref, hot_ref=None):
    count, width = got_ref.shape[0], out_ref.shape[1]
    entry = lax.broadcasted_iota(jnp.int32, (count, table_rows), 1)
    total = None
    for index in range(slots.groups):
        at = slots.ids + 2 * index
        number = got_ref[:, at : at + 2].astype(jnp.float32)
        hot = one_hot(entry == (number[:, 0:1] * 128.0 + number[:, 1:2]).astype(jnp.int32) - 1)
        values = received(slots, got_ref, index)
        if hot_ref is not None:
            hot_ref[index] = hot
            sender, lane = places(pb, count, width)
            values = jnp.where(sender == lane, jnp.concatenate([values] * pb, axis=1), 0)
        part = lax.dot_general(hot, values, TN, preferred_element_type=jnp.float32)
        total = part if total is None else total + part
    out_ref[...] = total


def last_table_kernel(slots, pb, first_ref, hot_ref, got_ref, out_ref):
    count, width = got_ref.shape[0], out_ref.shape[1]
    total = first_ref[...]
    sender, lane = places(pb, count, width)
    for index in range(slots.groups):
        values = received(slots, got_ref, index)
        none = jnp.zeros((count, width - slots.width), values.dtype)
        below, above = jnp.concatenate([values, none], axis=1), jnp.concatenate([none, values], axis=1)
        values = jnp.where(lane < sender, below, jnp.where(lane > sender, above, 0))
        total += lax.dot_general(hot_ref[index], values, TN, preferred_element_type=jnp.float32)
    out_ref[...] = total


def on_device(train, query, residual, example_source, source_place):
    rows, depth = train.shape
    block = query.shape[0]
    ex, pb = lax.axis_size("ex"), lax.axis_size("pb")
    me_ex, me_pb = lax.axis_index("ex"), lax.axis_index("pb")
    devices = ex * pb
    table_rows = source_place.shape[0] // devices
    capacity = max(1, -(-2 * rows // devices))
    core, layer = me_ex % 2, (me_ex // 2) % 2
    deep = depth // 2
    on_core = lambda i: i ^ 1
    on_z = lambda i: i ^ 2
    on_x = lambda i: i ^ 1
    on_y = lambda i: i ^ 2
    scale = residual[:, None]
    whole = jax.ShapeDtypeStruct((table_rows, block * pb), jnp.float32)

    placed = jnp.take(source_place, example_source)
    places = placed[None, :], placed[:, None]
    packed_rows = lambda slots: jax.ShapeDtypeStruct((devices * 8, slots.lanes), jnp.bfloat16)

    if pb != 4 or ex % 4 != 0:
        other = moved(lax.dynamic_slice(train, (0, (1 - core) * deep), (rows, deep)), "ex", on_core)
        own = lax.dynamic_slice(train, (0, core * deep), (rows, deep))
        queries = lax.all_gather(lax.dynamic_slice(query, (0, core * deep), (block, deep)), "pb", tiled=True)
        slots = Slots(capacity, block * pb, True)
        own, other = scored([[own], [other]], [queries])

        def pack(own_ref, got_ref, scale_ref, row_ref, column_ref, out_ref):
            found = selects(slots, table_rows, devices * 8, row_ref, column_ref)
            put(slots, found, weighted(own_ref, got_ref, scale_ref), out_ref, digits(slots, table_rows, column_ref))

        got = exchanged(called(pack, packed_rows(slots), own, moved(other, "ex", on_core), scale, *places), devices)
        return called(functools.partial(first_table_kernel, slots, pb, table_rows), whole, got)

    half = block // 2
    lent = half * 2 // 3 // 16 * 16
    ends = half - lent
    front, back, x_sent, y_sent = cut_queries(query, lent)
    x_one = moved(front, "pb", on_x)
    y_one = moved(back, "pb", on_y)
    x_end = moved(x_sent, "pb", on_x)
    y_end = moved(y_sent, "pb", on_y)
    early, late = Slots(capacity, block, True), Slots(capacity, block * (pb - 1), False)

    def own_pack(scores_ref, scale_ref, row_ref, column_ref, out_ref):
        found = selects(early, table_rows, devices * 8, row_ref, column_ref)
        put(early, found, weighted(scores_ref, None, scale_ref), out_ref, digits(early, table_rows, column_ref))

    def spans(wanted):
        me, layer = lax.axis_index("pb"), lax.axis_index("ex") // 2 % 2
        x, y = me % 2, me // 2
        blocks = {"x": y * 2 + 1 - x, "y": (1 - y) * 2 + x, "xy": (1 - y) * 2 + 1 - x}
        starts = {"first": layer * half, "second": half - layer * half}
        place = lambda other: (other - jnp.where(other > me, 1, 0)) * block
        return [(place(blocks[over]) + starts[part] + start, count) for over, part, start, count in wanted]

    def near_pack(own_ref, got_ref, scale_ref, row_ref, column_ref, out_ref):
        found = selects(late, table_rows, devices * 8, row_ref, column_ref)
        put(late, found, ordered(late, weighted(own_ref, got_ref, scale_ref), spans(near)), out_ref)

    def far_pack(own_ref, got_ref, scale_ref, row_ref, column_ref, base_ref, out_ref):
        found = selects(late, table_rows, devices * 8, row_ref, column_ref)
        put(late, found, ordered(late, weighted(own_ref, got_ref, scale_ref), spans(far)), out_ref, None, base_ref)

    (scores_own,) = scored([[train]], [query])
    rows_own = called(own_pack, packed_rows(early), scores_own, scale, *places)
    train, rows_own = lax.optimization_barrier((train, rows_own))
    sent_own = exchanged(rows_own, devices)
    own, others = cut_examples(train, 4)
    others = [moved(part, "ex", on_core) for part in others]

    ahead = lent * 3 // 4 // 16 * 16
    z_sent, x_sent, y_sent = stacked([(x_one, 0, lent), (y_one, 0, lent)], [(y_one, 0, ahead)], [(x_one, 0, ahead)])
    z_lent = moved(z_sent, "ex", on_z)
    x_two = moved(x_sent, "pb", on_x)
    y_two = moved(y_sent, "pb", on_y)
    x_sent, y_sent = stacked(
        [(y_one, ahead, lent - ahead), (y_end, 0, ends)], [(x_one, ahead, lent - ahead), (x_end, 0, ends)]
    )
    x_last = moved(x_sent, "pb", on_x)
    y_last = moved(y_sent, "pb", on_y)

    near = [
        ("x", "first", 0, lent),
        ("y", "second", 0, lent),
        ("x", "first", lent, ends),
        ("x", "second", lent, ends),
        ("y", "second", lent, ends),
        ("y", "first", lent, ends),
        ("xy", "second", 0, ahead),
        ("xy", "first", 0, ahead),
    ]
    far = [
        ("xy", "second", ahead, lent - ahead),
        ("xy", "second", lent, ends),
        ("xy", "first", ahead, lent - ahead),
        ("xy", "first", lent, ends),
        ("x", "second", 0, lent),
        ("y", "first", 0, lent),
    ]
    own_a, other_a = scored([[own], others], [x_one, y_one, x_end, y_end, x_two, y_two])
    got_a = moved(other_a, "ex", on_core)
    base = called(near_pack, packed_rows(late), own_a, got_a, scale, *places)
    own, others, base, sent_own = lax.optimization_barrier((own, others, base, sent_own))
    (other_b,) = scored([others], [x_last, y_last, z_lent])
    got_b = moved(other_b, "ex", on_core)
    (own_b,) = scored([[own]], [x_last, y_last, z_lent])
    sent = exchanged(called(far_pack, packed_rows(late), own_b, got_b, scale, *places, base), devices)

    hot = jax.ShapeDtypeStruct((early.groups, devices * 8, table_rows), jnp.bfloat16)
    table, hot = called(functools.partial(first_table_kernel, early, pb, table_rows), [whole, hot], sent_own)
    return called(functools.partial(last_table_kernel, late, pb), whole, table, hot, sent)


def solution(mesh):
    return jax.shard_map(
        on_device,
        mesh=mesh,
        in_specs=(P(BOTH, None), P("pb", None), P(BOTH), P(BOTH), P()),
        out_specs=P(BOTH, None),
        check_vma=False,
    )
```

time: 335 us -> 86 us (0.26)
  waiting for transfers between devices: 267 us -> 22.7 us
  Pallas kernels: 0 us -> 23.4 us
  matrix products: 15.1 us -> 0 us
  between operations: 13.5 us -> 0.28 us
  starting transfers between devices: 12.8 us -> 23.3 us
  local copies, waits for them, and re-layouts: 21 us -> 15.5 us
  other arithmetic: 4.24 us -> 0.02 us
    ppermute x3 -> x15, waiting for transfers between devices: 210 us -> 8.92 us  [moved(): return lax.ppermute(value, axis, [(i, target(i)) for i in range(count)])]
    reduce_scatter x1 -> x0, waiting for transfers between devices: 42.1 us -> none  [on_device(): lax.psum_scatter(partial_table, 'pb', scatter_dimension=0, tiled=True)]
    pallas_call x0 -> x13, Pallas kernels: none -> 23.4 us  [the longest x4 8.22 us: scored(): pl.pallas_call(functools.partial(scores_kernel, [len(group) for group in...]
    dot_general x5 -> x0, matrix products: 15.1 us -> none  [the longest x4 12.5 us: block_scores(): jnp.einsum('rk,qk->rq', train_sketch, held, preferred_element_type=jnp.fl...]
    unnamed x7 -> x42, local copies, waits for them, and re-layouts: 3.89 us -> 13.8 us
    ppermute x3 -> x15, starting transfers between devices: 2.49 us -> 11.6 us  [moved(): return lax.ppermute(value, axis, [(i, target(i)) for i in range(count)])]
    dynamic_update_slice x4 -> x0, local copies, waits for them, and re-layouts: 7.18 us -> none  [the longest x3 5.44 us: advance(): lax.dynamic_update_slice_in_dim(table, block_scores(held), anchor * block...]
    while x3 -> x0, local copies, waits for them, and re-layouts: 5 us -> none
  transfers between devices with their start and end apart: 6 -> 17, of which waited for: 5 -> 6; matrix products, arithmetic and copies ran while one was open for 9% -> 2% of each run, Pallas kernels for 0% -> 18%
where the time goes in v3:
time: 86 us; the launch traced here: 85.2 us
  Pallas kernels  23.4 us (27%)
  starting transfers between devices  23.3 us (27%)
  waiting for transfers between devices  22.7 us (26%)
  local copies, waits for them, and re-layouts  15.5 us (18%)
    unnamed x42, local copies, waits for them, and re-layouts  13.8 us
    all_to_all x2, waiting for transfers between devices, exchanged(): lax.all_to_all(apart, BOTH, split_axis=0, concat_axis=0).reshape(rows.shape)  13.8 us
    ppermute x15, starting transfers between devices, moved(): return lax.ppermute(value, axis, [(i, target(i)) for i in range(count)])  11.6 us
    all_to_all x2, starting transfers between devices, exchanged(): lax.all_to_all(apart, BOTH, split_axis=0, concat_axis=0).reshape(rows.shape)  11.6 us
    ppermute x15, waiting for transfers between devices, moved(): return lax.ppermute(value, axis, [(i, target(i)) for i in range(count)])  8.92 us
    pallas_call x4, Pallas kernels, scored(): pl.pallas_call(functools.partial(scores_kernel, [len(group) for group in...  8.22 us
    pallas_call x5, Pallas kernels, called(): pl.pallas_call(body, out_shape=shapes, compiler_params=LIMIT, cost_estima...  7.53 us
    pallas_call x2, Pallas kernels, stacked(): pl.pallas_call(body, out_shape=shapes, compiler_params=LIMIT, cost_estima...  4.88 us
  transfers between devices with their start and end apart: 17, of which 6 were waited for; matrix products, arithmetic and copies ran while one was open for 2% of the time, Pallas kernels for 18%

profile of v3, /device:TPU:0, one launch (start us, length us, event | category | flops | bytes accessed | tf_op | source)
XLA Modules:
  0.0 85.2 jit_solution(4162667922323307652)
XLA Ops:
  0.0 2.6 %shard_map.58 = (bf16[64,4096]{1,0:T(8,128)(2,1)}, bf16[64,4096]{1,0:T(8,128)(2,1)}, bf16[64,4096]{1,0:T(8,128)(2,1)}, bf16[64,4096]{1,0:T(8,128)(2,1)}) custom-call(bf16[192,8192]{1,0:T(8,128)(2,1)} %query_ref.1), custom_call_target="tpu_custom_call" | custom-call | flops 1 | bytes 1 | tf_op jit(solution)/shard_map/pallas_call | solution.py:57
  2.6 3.0 %collective-permute-start.4 = (bf16[64,4096]{1,0:T(8,128)(2,1)}, bf16[64,4096]{1,0:T(8,128)(2,1)}, u32[]{:S(2)}, u32[]{:S(2)}) collective-permute-start(bf16[64,4096]{1,0:T(8,128)(2,1)} %get-tuple-element.38), channel_id=1, source_target_pairs={{0,1},{1,0},{2,3},{3,2},{4,5},{5,4},{6,7},{7,6},{8,9},{9,8},{10,11... | collective-permute-start | bytes 1572872 | tf_op jit(solution)/shard_map/ppermute | solution.py:22
  5.6 1.5 %collective-permute-start.5 = (bf16[64,4096]{1,0:T(8,128)(2,1)}, bf16[64,4096]{1,0:T(8,128)(2,1)}, u32[]{:S(2)}, u32[]{:S(2)}) collective-permute-start(bf16[64,4096]{1,0:T(8,128)(2,1)} %get-tuple-element.39), channel_id=1, source_target_pairs={{0,2},{1,3},{2,0},{3,1},{4,6},{5,7},{6,4},{7,5},{8,10},{9,11},{10,... | collective-permute-start | bytes 1572872 | tf_op jit(solution)/shard_map/ppermute | solution.py:22
  7.1 0.5 collective-permute-start.6
  7.8 1.4 %gather_fusion = s32[192]{0:T(256)S(1)} fusion(s32[8192]{0:T(1024)S(1)} %copy-done, s32[1024]{0:T(1024)S(1)} %pad_clamp_fusion), kind=kCustom, calls=%fused_computation | custom fusion | bytes 2304 | tf_op jit(solution)/shard_map/jit(_take)/gather | solution.py:285
  9.2 1.9 %copy-done.2 = bf16[192,8192]{1,0:T(8,128)(2,1)S(1)} copy-done((bf16[192,8192]{1,0:T(8,128)(2,1)S(1)}, bf16[192,8192]{1,0:T(8,128)(2,1)}, u32[]{:S(2)}) %copy-start.2) | copy-done | bytes 3145752
  11.1 1.0 %shard_map.55.scores_ref = f32[192,192]{1,0:T(8,128)S(1)} custom-call(bf16[192,8192]{1,0:T(8,128)(2,1)S(1)} %copy-done.2, bf16[192,8192]{1,0:T(8,128)(2,1)S(1)} %copy-done.1), custom_call_target="tpu_custom_call" | custom-call | flops 1 | bytes 1 | tf_op jit(solution)/shard_map/pallas_call | solution.py:48
  12.1 0.1 copy.7.column_ref
  12.3 0.1 copy.6.scale_ref
  12.4 0.5 copy-done.12
  12.9 0.7 shard_map.56
  13.6 0.6 copy-done.15
  14.2 0.7 copy-done.18
  14.9 1.9 %copy-done.3 = bf16[192,8192]{1,0:T(8,128)(2,1)S(1)} copy-done((bf16[192,8192]{1,0:T(8,128)(2,1)S(1)}, bf16[192,8192]{1,0:T(8,128)(2,1)}, u32[]{:S(2)}) %copy-start.3) | copy-done | bytes 3145752
  16.7 0.2 shard_map.57
  17.0 1.7 %collective-permute-done.4.refs_0_.refs_5_.refs_2_ = bf16[64,4096]{1,0:T(8,128)(2,1)} collective-permute-done((bf16[64,4096]{1,0:T(8,128)(2,1)}, bf16[64,4096]{1,0:T(8,128)(2,1)}, u32[]{:S(2)}, u32[]{:S(2)}) %collective-permute-start.4) | collective-permute-done | bytes 524320 | tf_op jit(solution)/shard_map/ppermute | solution.py:22
  18.7 2.1 %collective-permute-done.5.refs_1_.refs_6_.refs_0_ = bf16[64,4096]{1,0:T(8,128)(2,1)} collective-permute-done((bf16[64,4096]{1,0:T(8,128)(2,1)}, bf16[64,4096]{1,0:T(8,128)(2,1)}, u32[]{:S(2)}, u32[]{:S(2)}) %collective-permute-start.5) | collective-permute-done | bytes 524320 | tf_op jit(solution)/shard_map/ppermute | solution.py:22
  20.8 2.5 %shard_map.59 = (bf16[128,4096]{1,0:T(8,128)(2,1)}, bf16[48,4096]{1,0:T(8,128)(2,1)}, bf16[48,4096]{1,0:T(8,128)(2,1)}) custom-call(bf16[64,4096]{1,0:T(8,128)(2,1)} %collective-permute-done.4.refs_0_.refs_5_.refs_2_, bf16[64,4096]{1,0:T(8,128)(2,1)} %collective-permute-done.5.refs_1_.refs_6_.refs_0_), custom_call_target="tpu_custom_call" | custom-call | flops 1 | bytes 1 | tf_op jit(solution)/shard_map/pallas_call | solution.py:143
  23.3 1.6 %collective-permute-start.13 = (bf16[128,4096]{1,0:T(8,128)(2,1)}, bf16[128,4096]{1,0:T(8,128)(2,1)S(1)}, u32[]{:S(2)}, u32[]{:S(2)}) collective-permute-start(bf16[128,4096]{1,0:T(8,128)(2,1)} %get-tuple-element.53), channel_id=1, source_target_pairs={{0,8},{4,12},{8,0},{12,4},{16,24},{20,28},{24,16},{28,20},{1,9},{5... | collective-permute-start | bytes 3145736 | tf_op jit(solution)/shard_map/ppermute | solution.py:22
  24.9 0.5 collective-permute-start.3
  25.4 3.7 %collective-permute-done.6.refs_7_.refs_3_ = bf16[64,4096]{1,0:T(8,128)(2,1)} collective-permute-done((bf16[64,4096]{1,0:T(8,128)(2,1)}, bf16[64,4096]{1,0:T(8,128)(2,1)}, u32[]{:S(2)}, u32[]{:S(2)}) %collective-permute-start.6) | collective-permute-done | bytes 524320 | tf_op jit(solution)/shard_map/ppermute | solution.py:22
  29.1 1.7 %collective-permute-start.8 = (bf16[48,4096]{1,0:T(8,128)(2,1)}, bf16[48,4096]{1,0:T(8,128)(2,1)}, u32[]{:S(2)}, u32[]{:S(2)}) collective-permute-start(bf16[48,4096]{1,0:T(8,128)(2,1)} %get-tuple-element.42), channel_id=1, source_target_pairs={{0,1},{1,0},{2,3},{3,2},{4,5},{5,4},{6,7},{7,6},{8,9},{9,8},{10,11... | collective-permute-start | bytes 1179656 | tf_op jit(solution)/shard_map/ppermute | solution.py:22
  30.8 1.5 %collective-permute-start.9 = (bf16[48,4096]{1,0:T(8,128)(2,1)}, bf16[48,4096]{1,0:T(8,128)(2,1)}, u32[]{:S(2)}, u32[]{:S(2)}) collective-permute-start(bf16[48,4096]{1,0:T(8,128)(2,1)} %get-tuple-element.43), channel_id=1, source_target_pairs={{0,2},{1,3},{2,0},{3,1},{4,6},{5,7},{6,4},{7,5},{8,10},{9,11},{10,... | collective-permute-start | bytes 1179656 | tf_op jit(solution)/shard_map/ppermute | solution.py:22
  32.4 2.4 %shard_map.63 = (bf16[48,4096]{1,0:T(8,128)(2,1)}, bf16[48,4096]{1,0:T(8,128)(2,1)}) custom-call(bf16[64,4096]{1,0:T(8,128)(2,1)} %collective-permute-done.5.refs_1_.refs_6_.refs_0_, bf16[64,4096]{1,0:T(8,128)(2,1)} %collective-permute-done.7.refs_8_.refs_1_, bf16[64,4096]{1,0:T(8,128)(2,1)} %collective-permute-done.4.refs_0_.refs_5_.refs_2_, ...), custom_call_target="tpu_custom_call" | custom-call | flops 1 | bytes 1 | tf_op jit(solution)/shard_map/pallas_call | solution.py:143
  34.8 0.8 copy-done.6
  35.6 0.5 collective-permute-start.11
  36.1 0.7 copy-done.9
  36.8 0.3 collective-permute-start.12
  37.1 6.2 %all-to-all-start = ((bf16[32,8,292]{2,1,0:T(8,128)(2,1)}), bf16[32,8,292]{2,1,0:T(8,128)(2,1)}, u32[]{:S(2)}, u32[]{:S(2)}) async-start(bf16[32,8,292]{2,1,0:T(8,128)(2,1)} %bitcast.8), calls=%async_computation | async-start | bytes 393216 | tf_op jit(solution)/shard_map/all_to_all | solution.py:220
  43.3 1.0 %copy-done.7 = bf16[48,4096]{1,0:T(8,128)(2,1)S(1)} copy-done((bf16[48,4096]{1,0:T(8,128)(2,1)S(1)}, bf16[48,4096]{1,0:T(8,128)(2,1)}, u32[]{:S(2)}) %copy-start.7) | copy-done | bytes 393240
  44.3 1.0 %copy-done.10 = bf16[48,4096]{1,0:T(8,128)(2,1)S(1)} copy-done((bf16[48,4096]{1,0:T(8,128)(2,1)S(1)}, bf16[48,4096]{1,0:T(8,128)(2,1)}, u32[]{:S(2)}) %copy-start.10) | copy-done | bytes 393240
  45.3 3.5 %shard_map.60 = (f32[192,352]{1,0:T(8,128)S(1)}, f32[192,352]{1,0:T(8,128)S(1)}) custom-call(bf16[192,4096]{1,0:T(8,128)(2,1)S(1)} %get-tuple-element.50.refs_0_, bf16[48,4096]{1,0:T(8,128)(2,1)S(1)} %collective-permute-done.refs_1_.refs_0_, bf16[48,4096]{1,0:T(8,128)(2,1)S(1)} %collective-permute-done.1.refs_2_.refs_1_, bf16[48,4096]{1,0:T(8,128)(2,1)S(1)} %copy-done.7, ...), custom_call_target="tpu_custom_call" | custom-call | flops 1 | bytes 1 | tf_op jit(solution)/shard_map/pallas_call | solution.py:48
  48.9 0.3 collective-permute-start.10
  49.1 1.4 %collective-permute-done.10.got_ref = f32[192,352]{1,0:T(8,128)S(1)} collective-permute-done((f32[192,352]{1,0:T(8,128)S(1)}, f32[192,352]{1,0:T(8,128)S(1)}, u32[]{:S(2)}, u32[]{:S(2)}) %collective-permute-start.10) | collective-permute-done | bytes 270368 | tf_op jit(solution)/shard_map/ppermute | solution.py:22
  50.5 0.9 %copy-done.13 = s32[192,1]{1,0:T(8,128)S(1)} copy-done((s32[192,1]{1,0:T(8,128)S(1)}, s32[192,1]{1,0:T(8,128)}, u32[]{:S(2)}) %copy-start.13) | copy-done | bytes 792
  51.4 0.9 %copy-done.16 = f32[192,1]{1,0:T(8,128)S(1)} copy-done((f32[192,1]{1,0:T(8,128)S(1)}, f32[192,1]{1,0:T(8,128)}, u32[]{:S(2)}) %copy-start.16) | copy-done | bytes 792
  52.3 1.4 %shard_map.61.base_ref = bf16[256,864]{1,0:T(8,128)(2,1)S(1)} custom-call(f32[192,352]{1,0:T(8,128)S(1)} %get-tuple-element.44.own_ref, f32[192,352]{1,0:T(8,128)S(1)} %collective-permute-done.10.got_ref, f32[192,1]{1,0:T(8,128)S(1)} %copy-done.16, s32[1,192]{1,0:T(1,128)S(1)} %bitcast.11, s32[192,1]{1,0:T(8,128)S(1)} %copy-done.13), custom_call_target="tpu_custom_call" | custom-call | flops 1 | bytes 1 | tf_op jit(solution)/shard_map/pallas_call | solution.py:215
  53.8 0.5 all-to-all-done
  54.3 1.0 %copy-done.5 = bf16[48,4096]{1,0:T(8,128)(2,1)S(1)} copy-done((bf16[48,4096]{1,0:T(8,128)(2,1)S(1)}, bf16[48,4096]{1,0:T(8,128)(2,1)}, u32[]{:S(2)}) %copy-start.5) | copy-done | bytes 393240
  55.3 1.0 %copy-done.8 = bf16[48,4096]{1,0:T(8,128)(2,1)S(1)} copy-done((bf16[48,4096]{1,0:T(8,128)(2,1)S(1)}, bf16[48,4096]{1,0:T(8,128)(2,1)}, u32[]{:S(2)}) %copy-start.8) | copy-done | bytes 393240
  56.3 1.0 %copy-done.11 = bf16[48,4096]{1,0:T(8,128)(2,1)S(1)} copy-done((bf16[48,4096]{1,0:T(8,128)(2,1)S(1)}, bf16[48,4096]{1,0:T(8,128)(2,1)}, u32[]{:S(2)}) %copy-start.11) | copy-done | bytes 393240
  57.3 1.9 %shard_map.65 = f32[192,224]{1,0:T(8,128)S(1)} custom-call(bf16[48,4096]{1,0:T(8,128)(2,1)S(1)} %collective-permute-done.refs_1_.refs_0_, bf16[48,4096]{1,0:T(8,128)(2,1)S(1)} %copy-done.5, bf16[48,4096]{1,0:T(8,128)(2,1)S(1)} %copy-done.8, bf16[48,4096]{1,0:T(8,128)(2,1)S(1)} %copy-done.11, bf16[48,4096]{1,0:T(8,128)(2,1)} %collective-permute-done.11.refs_1_.refs_4_, ...), custom_call_target="tpu_custom_call" | custom-call | flops 1 | bytes 1 | tf_op jit(solution)/shard_map/pallas_call | solution.py:48
  59.3 1.8 %shard_map.64.own_ref = f32[192,224]{1,0:T(8,128)S(1)} custom-call(bf16[192,4096]{1,0:T(8,128)(2,1)S(1)} %get-tuple-element.50.refs_0_, bf16[48,4096]{1,0:T(8,128)(2,1)} %collective-permute-done.11.refs_1_.refs_4_, bf16[48,4096]{1,0:T(8,128)(2,1)} %collective-permute-done.12.refs_2_.refs_5_, bf16[128,4096]{1,0:T(8,128)(2,1)S(1)} %collective-permute-done.13.refs_3_.refs_6_), custom_call_target="tpu_custom_call" | custom-call | flops 1 | bytes 1 | tf_op jit(solution)/shard_map/pallas_call | solution.py:48
  61.1 2.1 %shard_map.66 = bf16[256,864]{1,0:T(8,128)(2,1)} custom-call(f32[192,224]{1,0:T(8,128)S(1)} %shard_map.64.own_ref, f32[192,224]{1,0:T(8,128)S(1)} %collective-permute-done.14.got_ref, f32[192,1]{1,0:T(8,128)S(1)} %copy-done.17, s32[1,192]{1,0:T(1,128)S(1)} %bitcast.12, s32[192,1]{1,0:T(8,128)S(1)} %copy-done.14, bf16[256,864]{1,0:T(8,128)(2,1)S(1)} %shard_map.61.base_ref), custom_call_target="tpu_custom_call" | custom-call | flops 1 | bytes 1 | tf_op jit(solution)/shard_map/pallas_call | solution.py:215
  63.2 5.4 %all-to-all-start.1 = ((bf16[32,8,864]{2,1,0:T(8,128)(2,1)}), bf16[32,8,864]{2,1,0:T(8,128)(2,1)S(1)}, u32[]{:S(2)}, u32[]{:S(2)}) async-start(bf16[32,8,864]{2,1,0:T(8,128)(2,1)} %bitcast.5), calls=%async_computation.1 | async-start | bytes 917504 | tf_op jit(solution)/shard_map/all_to_all | solution.py:220
  68.6 1.7 %shard_map.62 = (f32[256,768]{1,0:T(8,128)S(1)}, bf16[2,256,256]{2,1,0:T(8,128)(2,1)S(1)}) custom-call(bf16[256,292]{1,0:T(8,128)(2,1)} %bitcast.4.got_ref), custom_call_target="tpu_custom_call" | custom-call | flops 1 | bytes 1 | tf_op jit(solution)/shard_map/pallas_call | solution.py:215
  70.3 13.2 %all-to-all-done.1 = bf16[32,8,864]{2,1,0:T(8,128)(2,1)S(1)} async-done(((bf16[32,8,864]{2,1,0:T(8,128)(2,1)}), bf16[32,8,864]{2,1,0:T(8,128)(2,1)S(1)}, u32[]{:S(2)}, u32[]{:S(2)}) %all-to-all-start.1) | async-done | bytes 442400 | tf_op jit(solution)/shard_map/all_to_all | solution.py:220
  83.6 1.6 %shard_map.67 = f32[256,768]{1,0:T(8,128)} custom-call(f32[256,768]{1,0:T(8,128)S(1)} %get-tuple-element.48.first_ref, bf16[2,256,256]{2,1,0:T(8,128)(2,1)S(1)} %get-tuple-element.49.hot_ref, bf16[256,864]{1,0:T(8,128)(2,1)S(1)} %bitcast.7), custom_call_target="tpu_custom_call" | custom-call | flops 1 | bytes 1 | tf_op jit(solution)/shard_map/pallas_call | solution.py:215
  (47 shorter events, 0.3 us)
Async XLA Ops:
  0.0 7.8 %copy-start = (s32[8192]{0:T(1024)S(1)}, s32[8192]{0:T(1024)}, u32[]{:S(2)}) copy-start(s32[8192]{0:T(1024)} %param.9) | copy-start | bytes 98308
  0.0 9.2 %copy-start.1 = (bf16[192,8192]{1,0:T(8,128)(2,1)S(1)}, bf16[192,8192]{1,0:T(8,128)(2,1)}, u32[]{:S(2)}) copy-start(bf16[192,8192]{1,0:T(8,128)(2,1)} %query_ref.1) | copy-start | bytes 9437188
  0.0 7.7 %copy-start.19 = (s32[192]{0:T(256)S(1)}, s32[192]{0:T(256)}, u32[]{:S(2)}) copy-start(s32[192]{0:T(256)} %param.8) | copy-start | bytes 2308
  2.6 16.1 %collective-permute-start.4 = (bf16[64,4096]{1,0:T(8,128)(2,1)}, bf16[64,4096]{1,0:T(8,128)(2,1)}, u32[]{:S(2)}, u32[]{:S(2)}) collective-permute-start(bf16[64,4096]{1,0:T(8,128)(2,1)} %get-tuple-element.38), channel_id=1, source_target_pairs={{0,1},{1,0},{2,3},{3,2},{4,5},{5,4},{6,7},{7,6},{8,9},{9,8},{10,11... | collective-permute-start | bytes 1572872 | tf_op jit(solution)/shard_map/ppermute | solution.py:22
  5.6 15.2 %collective-permute-start.5 = (bf16[64,4096]{1,0:T(8,128)(2,1)}, bf16[64,4096]{1,0:T(8,128)(2,1)}, u32[]{:S(2)}, u32[]{:S(2)}) collective-permute-start(bf16[64,4096]{1,0:T(8,128)(2,1)} %get-tuple-element.39), channel_id=1, source_target_pairs={{0,2},{1,3},{2,0},{3,1},{4,6},{5,7},{6,4},{7,5},{8,10},{9,11},{10,... | collective-permute-start | bytes 1572872 | tf_op jit(solution)/shard_map/ppermute | solution.py:22
  7.1 22.0 %collective-permute-start.6 = (bf16[64,4096]{1,0:T(8,128)(2,1)}, bf16[64,4096]{1,0:T(8,128)(2,1)}, u32[]{:S(2)}, u32[]{:S(2)}) collective-permute-start(bf16[64,4096]{1,0:T(8,128)(2,1)} %get-tuple-element.40), channel_id=1, source_target_pairs={{0,1},{1,0},{2,3},{3,2},{4,5},{5,4},{6,7},{7,6},{8,9},{9,8},{10,11... | collective-permute-start | bytes 1572872 | tf_op jit(solution)/shard_map/ppermute | solution.py:22
  7.7 23.2 %collective-permute-start.7 = (bf16[64,4096]{1,0:T(8,128)(2,1)}, bf16[64,4096]{1,0:T(8,128)(2,1)}, u32[]{:S(2)}, u32[]{:S(2)}) collective-permute-start(bf16[64,4096]{1,0:T(8,128)(2,1)} %get-tuple-element.41), channel_id=1, source_target_pairs={{0,2},{1,3},{2,0},{3,1},{4,6},{5,7},{6,4},{7,5},{8,10},{9,11},{10,... | collective-permute-start | bytes 1572872 | tf_op jit(solution)/shard_map/ppermute | solution.py:22
  9.2 1.9 %copy-start.2 = (bf16[192,8192]{1,0:T(8,128)(2,1)S(1)}, bf16[192,8192]{1,0:T(8,128)(2,1)}, u32[]{:S(2)}) copy-start(bf16[192,8192]{1,0:T(8,128)(2,1)} %train_ref) | copy-start | bytes 9437188
  11.1 1.1 %copy-start.20 = (f32[192]{0:T(256)S(1)}, f32[192]{0:T(256)}, u32[]{:S(2)}) copy-start(f32[192]{0:T(256)} %param.7) | copy-start | bytes 2308
  12.2 0.6 copy-start.12
  13.5 0.6 copy-start.15
  14.2 0.7 copy-start.18
  14.9 1.9 %copy-start.3 = (bf16[192,8192]{1,0:T(8,128)(2,1)S(1)}, bf16[192,8192]{1,0:T(8,128)(2,1)}, u32[]{:S(2)}) copy-start(bf16[192,8192]{1,0:T(8,128)(2,1)} %train_ref) | copy-start | bytes 9437188
  17.0 7.9 %collective-permute-start = (bf16[48,4096]{1,0:T(8,128)(2,1)S(1)}, bf16[48,4096]{1,0:T(8,128)(2,1)S(1)}, u32[]{:S(2)}, u32[]{:S(2)}) collective-permute-start(bf16[48,4096]{1,0:T(8,128)(2,1)S(1)} %get-tuple-element.34), channel_id=1, source_target_pairs={{0,4},{4,0},{8,12},{12,8},{16,20},{20,16},{24,28},{28,24},{1,5},{5... | collective-permute-start | bytes 1179656 | tf_op jit(solution)/shard_map/ppermute | solution.py:22
  18.7 6.1 %collective-permute-start.1 = (bf16[48,4096]{1,0:T(8,128)(2,1)S(1)}, bf16[48,4096]{1,0:T(8,128)(2,1)S(1)}, u32[]{:S(2)}, u32[]{:S(2)}) collective-permute-start(bf16[48,4096]{1,0:T(8,128)(2,1)S(1)} %get-tuple-element.35), channel_id=1, source_target_pairs={{0,4},{4,0},{8,12},{12,8},{16,20},{20,16},{24,28},{28,24},{1,5},{5... | collective-permute-start | bytes 1179656 | tf_op jit(solution)/shard_map/ppermute | solution.py:22
  23.3 31.0 %collective-permute-start.13 = (bf16[128,4096]{1,0:T(8,128)(2,1)}, bf16[128,4096]{1,0:T(8,128)(2,1)S(1)}, u32[]{:S(2)}, u32[]{:S(2)}) collective-permute-start(bf16[128,4096]{1,0:T(8,128)(2,1)} %get-tuple-element.53), channel_id=1, source_target_pairs={{0,8},{4,12},{8,0},{12,4},{16,24},{20,28},{24,16},{28,20},{1,9},{5... | collective-permute-start | bytes 3145736 | tf_op jit(solution)/shard_map/ppermute | solution.py:22
  24.8 10.0 %collective-permute-start.2 = (bf16[48,4096]{1,0:T(8,128)(2,1)S(1)}, bf16[48,4096]{1,0:T(8,128)(2,1)S(1)}, u32[]{:S(2)}, u32[]{:S(2)}) collective-permute-start(bf16[48,4096]{1,0:T(8,128)(2,1)S(1)} %get-tuple-element.36), channel_id=1, source_target_pairs={{0,4},{4,0},{8,12},{12,8},{16,20},{20,16},{24,28},{28,24},{1,5},{5... | collective-permute-start | bytes 1179656 | tf_op jit(solution)/shard_map/ppermute | solution.py:22
  24.8 24.0 %copy-start.4 = (bf16[48,4096]{1,0:T(8,128)(2,1)}, bf16[48,4096]{1,0:T(8,128)(2,1)S(1)}, u32[]{:S(2)}) copy-start(bf16[48,4096]{1,0:T(8,128)(2,1)S(1)} %collective-permute-done.1.refs_2_.refs_1_) | copy-start | bytes 1179652
  24.9 11.2 %collective-permute-start.3 = (bf16[48,4096]{1,0:T(8,128)(2,1)S(1)}, bf16[48,4096]{1,0:T(8,128)(2,1)S(1)}, u32[]{:S(2)}, u32[]{:S(2)}) collective-permute-start(bf16[48,4096]{1,0:T(8,128)(2,1)S(1)} %get-tuple-element.37), channel_id=1, source_target_pairs={{0,4},{4,0},{8,12},{12,8},{16,20},{20,16},{24,28},{28,24},{1,5},{5... | collective-permute-start | bytes 1179656 | tf_op jit(solution)/shard_map/ppermute | solution.py:22
  29.1 14.2 %collective-permute-start.8 = (bf16[48,4096]{1,0:T(8,128)(2,1)}, bf16[48,4096]{1,0:T(8,128)(2,1)}, u32[]{:S(2)}, u32[]{:S(2)}) collective-permute-start(bf16[48,4096]{1,0:T(8,128)(2,1)} %get-tuple-element.42), channel_id=1, source_target_pairs={{0,1},{1,0},{2,3},{3,2},{4,5},{5,4},{6,7},{7,6},{8,9},{9,8},{10,11... | collective-permute-start | bytes 1179656 | tf_op jit(solution)/shard_map/ppermute | solution.py:22
  30.8 12.5 %collective-permute-start.9 = (bf16[48,4096]{1,0:T(8,128)(2,1)}, bf16[48,4096]{1,0:T(8,128)(2,1)}, u32[]{:S(2)}, u32[]{:S(2)}) collective-permute-start(bf16[48,4096]{1,0:T(8,128)(2,1)} %get-tuple-element.43), channel_id=1, source_target_pairs={{0,2},{1,3},{2,0},{3,1},{4,6},{5,7},{6,4},{7,5},{8,10},{9,11},{10,... | collective-permute-start | bytes 1179656 | tf_op jit(solution)/shard_map/ppermute | solution.py:22
  34.8 0.8 copy-start.6
  35.6 18.7 %collective-permute-start.11 = (bf16[48,4096]{1,0:T(8,128)(2,1)}, bf16[48,4096]{1,0:T(8,128)(2,1)}, u32[]{:S(2)}, u32[]{:S(2)}) collective-permute-start(bf16[48,4096]{1,0:T(8,128)(2,1)} %get-tuple-element.51), channel_id=1, source_target_pairs={{0,1},{1,0},{2,3},{3,2},{4,5},{5,4},{6,7},{7,6},{8,9},{9,8},{10,11... | collective-permute-start | bytes 1179656 | tf_op jit(solution)/shard_map/ppermute | solution.py:22
  36.1 0.7 copy-start.9
  36.8 17.5 %collective-permute-start.12 = (bf16[48,4096]{1,0:T(8,128)(2,1)}, bf16[48,4096]{1,0:T(8,128)(2,1)}, u32[]{:S(2)}, u32[]{:S(2)}) collective-permute-start(bf16[48,4096]{1,0:T(8,128)(2,1)} %get-tuple-element.52), channel_id=1, source_target_pairs={{0,2},{1,3},{2,0},{3,1},{4,6},{5,7},{6,4},{7,5},{8,10},{9,11},{10,... | collective-permute-start | bytes 1179656 | tf_op jit(solution)/shard_map/ppermute | solution.py:22
  37.1 17.2 %all-to-all-start = ((bf16[32,8,292]{2,1,0:T(8,128)(2,1)}), bf16[32,8,292]{2,1,0:T(8,128)(2,1)}, u32[]{:S(2)}, u32[]{:S(2)}) async-start(bf16[32,8,292]{2,1,0:T(8,128)(2,1)} %bitcast.8), calls=%async_computation | async-start | bytes 393216 | tf_op jit(solution)/shard_map/all_to_all | solution.py:220
  43.3 1.0 %copy-start.7 = (bf16[48,4096]{1,0:T(8,128)(2,1)S(1)}, bf16[48,4096]{1,0:T(8,128)(2,1)}, u32[]{:S(2)}) copy-start(bf16[48,4096]{1,0:T(8,128)(2,1)} %copy-done.6) | copy-start | bytes 1179652
  44.3 1.0 %copy-start.10 = (bf16[48,4096]{1,0:T(8,128)(2,1)S(1)}, bf16[48,4096]{1,0:T(8,128)(2,1)}, u32[]{:S(2)}) copy-start(bf16[48,4096]{1,0:T(8,128)(2,1)} %copy-done.9) | copy-start | bytes 1179652
  48.9 1.6 %collective-permute-start.10 = (f32[192,352]{1,0:T(8,128)S(1)}, f32[192,352]{1,0:T(8,128)S(1)}, u32[]{:S(2)}, u32[]{:S(2)}) collective-permute-start(f32[192,352]{1,0:T(8,128)S(1)} %get-tuple-element.45), channel_id=1, source_target_pairs={{0,4},{4,0},{8,12},{12,8},{16,20},{20,16},{24,28},{28,24},{1,5},{5... | collective-permute-start | bytes 811016 | tf_op jit(solution)/shard_map/ppermute | solution.py:22
  50.5 0.9 %copy-start.13 = (s32[192,1]{1,0:T(8,128)S(1)}, s32[192,1]{1,0:T(8,128)}, u32[]{:S(2)}) copy-start(s32[192,1]{1,0:T(8,128)} %copy-done.12) | copy-start | bytes 2308
  51.4 0.9 %copy-start.16 = (f32[192,1]{1,0:T(8,128)S(1)}, f32[192,1]{1,0:T(8,128)}, u32[]{:S(2)}) copy-start(f32[192,1]{1,0:T(8,128)} %copy-done.15) | copy-start | bytes 2308
  54.3 1.0 %copy-start.5 = (bf16[48,4096]{1,0:T(8,128)(2,1)S(1)}, bf16[48,4096]{1,0:T(8,128)(2,1)}, u32[]{:S(2)}) copy-start(bf16[48,4096]{1,0:T(8,128)(2,1)} %copy-done.4) | copy-start | bytes 1179652
  55.3 1.0 %copy-start.8 = (bf16[48,4096]{1,0:T(8,128)(2,1)S(1)}, bf16[48,4096]{1,0:T(8,128)(2,1)}, u32[]{:S(2)}) copy-start(bf16[48,4096]{1,0:T(8,128)(2,1)} %copy-done.6) | copy-start | bytes 1179652
  56.3 1.0 %copy-start.11 = (bf16[48,4096]{1,0:T(8,128)(2,1)S(1)}, bf16[48,4096]{1,0:T(8,128)(2,1)}, u32[]{:S(2)}) copy-start(bf16[48,4096]{1,0:T(8,128)(2,1)} %copy-done.9) | copy-start | bytes 1179652
  57.3 3.8 %copy-start.14 = (s32[192,1]{1,0:T(8,128)S(1)}, s32[192,1]{1,0:T(8,128)}, u32[]{:S(2)}) copy-start(s32[192,1]{1,0:T(8,128)} %copy-done.12) | copy-start | bytes 2308
  57.3 3.8 %copy-start.17 = (f32[192,1]{1,0:T(8,128)S(1)}, f32[192,1]{1,0:T(8,128)}, u32[]{:S(2)}) copy-start(f32[192,1]{1,0:T(8,128)} %copy-done.15) | copy-start | bytes 2308
  59.2 1.9 %collective-permute-start.14 = (f32[192,224]{1,0:T(8,128)S(1)}, f32[192,224]{1,0:T(8,128)S(1)}, u32[]{:S(2)}, u32[]{:S(2)}) collective-permute-start(f32[192,224]{1,0:T(8,128)S(1)} %shard_map.65), channel_id=1, source_target_pairs={{0,4},{4,0},{8,12},{12,8},{16,20},{20,16},{24,28},{28,24},{1,5},{5... | collective-permute-start | bytes 516104 | tf_op jit(solution)/shard_map/ppermute | solution.py:22
  63.2 20.4 %all-to-all-start.1 = ((bf16[32,8,864]{2,1,0:T(8,128)(2,1)}), bf16[32,8,864]{2,1,0:T(8,128)(2,1)S(1)}, u32[]{:S(2)}, u32[]{:S(2)}) async-start(bf16[32,8,864]{2,1,0:T(8,128)(2,1)} %bitcast.5), calls=%async_computation.1 | async-start | bytes 917504 | tf_op jit(solution)/shard_map/all_to_all | solution.py:220

commit v4 on v3

v4 whole, which is shorter than its diff:
```python
import functools

import jax
import jax.numpy as jnp
from jax import lax
from jax.experimental import pallas as pl
from jax.experimental.pallas import tpu as pltpu
from jax.sharding import PartitionSpec as P

BOTH = ("ex", "pb")
NT = (((1,), (1,)), ((), ()))
TN = (((0,), (0,)), ((), ()))
LIMIT = pltpu.CompilerParams(vmem_limit_bytes=20 << 20)
FULL = pltpu.CompilerParams(vmem_limit_bytes=60 << 20)
LIGHT = pl.CostEstimate(flops=1, bytes_accessed=1, transcendentals=0)
HBM = pl.BlockSpec(memory_space=pltpu.HBM)
VMEM = pl.BlockSpec(memory_space=pltpu.VMEM)


def moved(value, axis, target):
    count = lax.axis_size(axis)
    return lax.ppermute(value, axis, [(i, target(i)) for i in range(count)])


def one_hot(hits):
    return jnp.where(hits, 1.0, 0.0).astype(jnp.bfloat16)


def pick(select, values):
    return jnp.dot(select, values, preferred_element_type=jnp.float32)


def scores_kernel(groups, count, *refs):
    held, sides = sum(groups), len(groups)
    rows, pieces, outs = refs[:held], refs[held : held + count], refs[held + count :]
    stack = lambda arrays: arrays[0][...] if len(arrays) == 1 else jnp.concatenate([a[...] for a in arrays], axis=0)
    total = lax.dot_general(stack(rows), stack(pieces), NT, preferred_element_type=jnp.float32)
    at = 0
    for out in outs:
        out[...] = total[at : at + out.shape[0]]
        at += out.shape[0]


def scored(groups, pieces):
    width = sum(piece.shape[0] for piece in pieces)
    arrays = [rows for group in groups for rows in group]
    shapes = [jax.ShapeDtypeStruct((sum(rows.shape[0] for rows in group), width), jnp.float32) for group in groups]
    return pl.pallas_call(
        functools.partial(scores_kernel, [len(group) for group in groups], len(pieces)),
        out_shape=shapes,
        compiler_params=LIMIT,
        cost_estimate=LIGHT,
    )(*arrays, *pieces)


def relayed(body, inputs, shapes, rooms, sems, limit):
    return pl.pallas_call(
        body,
        in_specs=[HBM] * len(inputs),
        out_specs=[HBM] * len(shapes),
        out_shape=[jax.ShapeDtypeStruct(shape, inputs[0].dtype) for shape in shapes],
        scratch_shapes=[pltpu.VMEM(room, inputs[0].dtype) for room in rooms] + [pltpu.SemaphoreType.DMA((sems,))],
        compiler_params=limit,
        cost_estimate=LIGHT,
    )(*inputs)


def relay(sems, plan):
    arriving, leaving, at = [], [], 0
    for source, room, _ in plan:
        arriving.append(pltpu.make_async_copy(source, room, sems.at[at]))
        arriving[-1].start()
        at += 1
    for copy, (_, room, targets) in zip(arriving, plan):
        copy.wait()
        for target in targets:
            leaving.append(pltpu.make_async_copy(room, target, sems.at[at]))
            leaving[-1].start()
            at += 1
    for copy in leaving:
        copy.wait()


def cut_inputs(query, train, lent, count):
    half, deep, rows = query.shape[0] // 2, query.shape[1] // 2, train.shape[0]
    ends = half - lent

    def body(query_ref, train_ref, front_ref, back_ref, front_end_ref, back_end_ref, *refs):
        other_refs, (held, kept, sems) = refs[:count], refs[count:]
        core, layer = lax.axis_index("ex") % 2, lax.axis_index("ex") // 2 % 2
        mine = pl.ds(pl.multiple_of(core * deep, 128), deep)
        theirs = pl.ds(pl.multiple_of(deep - core * deep, 128), deep)
        starts = [layer * half, half - layer * half]
        part = lambda start, count: query_ref.at[pl.ds(pl.multiple_of(start, 16), count), mine]
        wholes, tails = (front_ref, back_ref), (front_end_ref, back_end_ref)
        plan = []
        for side in range(2):
            for first, height in ((0, lent), (lent, ends)):
                span = pl.ds(first, height)
                targets = [wholes[side].at[span]] + ([tails[side]] if first else [])
                plan.append((part(starts[side] + first, height), held.at[side, span], targets))
        for index, other_ref in enumerate(other_refs):
            span = pl.ds(index * (rows // count), rows // count)
            plan.append((train_ref.at[span, theirs], kept.at[span], [other_ref]))
        relay(sems, plan)

    shapes = [(half, deep)] * 2 + [(ends, deep)] * 2 + [(rows // count, deep)] * count
    return relayed(body, [query, train], shapes, [(2, half, deep), (rows, deep)], 10 + 2 * count, FULL)


def stacked(*outputs):
    arrays = []
    for output in outputs:
        for array, _, _ in output:
            if not any(array is known for known in arrays):
                arrays.append(array)
    index_of = lambda array: next(index for index, known in enumerate(arrays) if known is array)
    plans = [[(index_of(array), first, count) for array, first, count in output] for output in outputs]

    def body(*refs):
        for plan, out in zip(plans, refs[len(arrays) :]):
            at = 0
            for index, first, count in plan:
                out[at : at + count] = refs[index][first : first + count]
                at += count

    deep = arrays[0].shape[1]
    shapes = [jax.ShapeDtypeStruct((sum(p[2] for p in plan), deep), arrays[0].dtype) for plan in plans]
    return pl.pallas_call(body, out_shape=shapes, compiler_params=LIMIT, cost_estimate=LIGHT)(*arrays)


class Slots:
    def __init__(self, capacity, width, ids):
        self.width = width
        self.full, rest = capacity // 8, capacity % 8
        if rest > 4:
            self.full, rest = self.full + 1, 0
        self.half = width // 2 if rest else 0
        self.groups = self.full + (1 if rest else 0)
        self.at = self.full * width
        self.ids = self.at + self.half
        self.lanes = self.ids + (2 * self.groups if ids else 0)


def ordered(slots, scores, spans):
    rows, total, at = scores.shape[0], None, 0
    for base, count in spans:
        if base is not None:
            column = lax.broadcasted_iota(jnp.int32, (count, slots.width), 0) + base
            place = lax.broadcasted_iota(jnp.int32, (count, slots.width), 1)
            part = pick(scores[:, at : at + count], one_hot(place == column))
            total = part if total is None else total + part
        at += count
    return total


def upright(row):
    count = row.shape[1]
    diagonal = lax.broadcasted_iota(jnp.int32, (count, count), 0) == lax.broadcasted_iota(jnp.int32, (count, count), 1)
    return jnp.sum(jnp.where(diagonal, row, jnp.zeros_like(row)), axis=1, keepdims=True)


def packing(body, shape, residual, placed, *operands):
    rows = residual.shape[0]

    def kernel(scale_ref, row_ref, *refs):
        *refs, scale, row, sems = refs
        copies = [pltpu.make_async_copy(scale_ref, scale, sems.at[0]), pltpu.make_async_copy(row_ref, row, sems.at[1])]
        for copy in copies:
            copy.start()
        for copy in copies:
            copy.wait()
        body(scale[...], row[...], *refs)

    return pl.pallas_call(
        kernel,
        in_specs=[HBM] * 2 + [VMEM] * len(operands),
        out_shape=shape,
        scratch_shapes=[
            pltpu.VMEM((1, rows), residual.dtype),
            pltpu.VMEM((1, rows), placed.dtype),
            pltpu.SemaphoreType.DMA((2,)),
        ],
        compiler_params=LIMIT,
        cost_estimate=LIGHT,
    )(residual[None, :], placed[None, :], *operands)


def weighted(own, got, scale):
    return ((own[...] if got is None else own[...] + got[...]) * upright(scale)).astype(jnp.bfloat16)


def selects(slots, table_rows, height, placed):
    rows = placed.shape[1]
    goal = placed // table_rows
    same = upright(goal) == goal
    before = lax.broadcasted_iota(jnp.int32, (rows, rows), 0) < lax.broadcasted_iota(jnp.int32, (rows, rows), 1)
    rank = jnp.sum(jnp.where(same & before, 1, 0), axis=0, keepdims=True)
    row = lax.broadcasted_iota(jnp.int32, (height, rows), 0)
    found = [one_hot(row == jnp.where(rank // 8 == index, goal * 8 + rank % 8, -1)) for index in range(slots.full)]
    if slots.half:
        late = rank - slots.full * 8
        found += [one_hot(row == jnp.where(late >= 0, goal * 8 + side * 4 + late, -1)) for side in range(2)]
    return found


def digits(slots, table_rows, placed):
    number = upright(placed % table_rows + 1)
    lane = lax.broadcasted_iota(jnp.int32, (number.shape[0], 2 * slots.groups), 1)
    digit = jnp.where(lane % 2 == 0, number // 128, number % 128)
    kept = [jnp.where(lane // 2 == index, digit, 0) for index in range(slots.groups)]
    return [value.astype(jnp.float32).astype(jnp.bfloat16) for value in kept]


def put(slots, found, table, out_ref, ids=None, base_ref=None):
    table = table.astype(jnp.bfloat16)

    def write(start, values):
        values, span = values.astype(jnp.bfloat16), slice(start, start + values.shape[1])
        out_ref[:, span] = values if base_ref is None else values + base_ref[:, span]

    for index in range(slots.full):
        write(index * slots.width, pick(found[index], table))
    if slots.half:
        left, right = (pick(found[slots.full + i], table[:, i * slots.half : (i + 1) * slots.half]) for i in range(2))
        write(slots.at, left + right)
    if ids is not None:
        pairs = [(found[index], ids[min(index, slots.full)]) for index in range(len(found))]
        write(slots.ids, sum(pick(select, digit) for select, digit in pairs))


def called(body, shapes, *operands):
    return pl.pallas_call(body, out_shape=shapes, compiler_params=LIMIT, cost_estimate=LIGHT)(*operands)


def exchanged(rows, devices):
    apart = rows.reshape(devices, 8, rows.shape[1])
    return lax.all_to_all(apart, BOTH, split_axis=0, concat_axis=0).reshape(rows.shape)


def halves(slots, pb, count):
    row = lax.broadcasted_iota(jnp.int32, (count, slots.width), 0)
    unit = lax.broadcasted_iota(jnp.int32, (count, slots.width), 1) // (slots.width // 4)
    peer = row // 8
    y, x, layer = peer // 2 % 2, peer % 2, peer // pb // 2 % 2
    apart = (unit // 2 != (x + y) % 2) & (unit % 2 != layer)
    return (y == 0) != apart


def added(slots, totals, hot, ref, index, lower):
    if index < slots.full:
        values = ref[:, index * slots.width : (index + 1) * slots.width]
    else:
        half = ref[:, slots.at : slots.at + slots.half]
        row = lax.broadcasted_iota(jnp.int32, (half.shape[0], slots.width), 0)
        lane = lax.broadcasted_iota(jnp.int32, (half.shape[0], slots.width), 1)
        values = jnp.where((row % 8 < 4) == (lane < slots.half), jnp.concatenate([half, half], axis=1), 0)
    values = [values] if lower is None else [jnp.where(lower, values, 0), jnp.where(lower, 0, values)]
    parts = [lax.dot_general(hot, v, TN, preferred_element_type=jnp.float32) for v in values]
    return parts if totals is None else [t + p for t, p in zip(totals, parts)]


def first_table_kernel(slots, pb, table_rows, split, got_ref, out_ref, hot_ref=None):
    count = got_ref.shape[0]
    lower = halves(slots, pb, count) if split else None
    entry = lax.broadcasted_iota(jnp.int32, (count, table_rows), 1)
    totals = None
    for index in range(slots.groups):
        at = slots.ids + 2 * index
        number = got_ref[:, at : at + 2].astype(jnp.float32)
        hot = one_hot(entry == (number[:, 0:1] * 128.0 + number[:, 1:2]).astype(jnp.int32) - 1)
        if hot_ref is not None:
            hot_ref[index] = hot
        totals = added(slots, totals, hot, got_ref, index, lower)
    for side, total in enumerate(totals):
        out_ref[:, side * slots.width : (side + 1) * slots.width] = total


def last_table_kernel(slots, pb, first_ref, hot_ref, got_ref, out_ref):
    width, half = slots.width, slots.width // 2
    upper = jnp.logical_not(halves(slots, pb, got_ref.shape[0]))
    totals = None
    for index in range(slots.groups):
        totals = added(slots, totals, hot_ref[index], got_ref, index, upper)
    out_ref[:, :width] = first_ref[:, :width] + totals[0]
    above = first_ref[:, width:] + totals[1]
    out_ref[:, width : width + half] = above[:, half:]
    out_ref[:, width + half :] = above[:, :half]


def on_device(train, query, residual, example_source, source_place):
    rows, depth = train.shape
    block = query.shape[0]
    ex, pb = lax.axis_size("ex"), lax.axis_size("pb")
    me_ex, me_pb = lax.axis_index("ex"), lax.axis_index("pb")
    devices = ex * pb
    table_rows = source_place.shape[0] // devices
    capacity = max(1, -(-2 * rows // devices))
    core, layer = me_ex % 2, (me_ex // 2) % 2
    deep = depth // 2
    on_core = lambda i: i ^ 1
    on_z = lambda i: i ^ 2
    on_x = lambda i: i ^ 1
    on_y = lambda i: i ^ 2
    whole = jax.ShapeDtypeStruct((table_rows, block * pb), jnp.float32)

    placed = jnp.take(source_place, example_source)
    packed_rows = lambda slots: jax.ShapeDtypeStruct((devices * 8, slots.lanes), jnp.bfloat16)

    if pb != 4 or ex % 4 != 0:
        other = moved(lax.dynamic_slice(train, (0, (1 - core) * deep), (rows, deep)), "ex", on_core)
        own = lax.dynamic_slice(train, (0, core * deep), (rows, deep))
        queries = lax.all_gather(lax.dynamic_slice(query, (0, core * deep), (block, deep)), "pb", tiled=True)
        slots = Slots(capacity, block * pb, True)
        own, other = scored([[own], [other]], [queries])

        def pack(scale, row, own_ref, got_ref, out_ref):
            found = selects(slots, table_rows, devices * 8, row)
            put(slots, found, weighted(own_ref, got_ref, scale), out_ref, digits(slots, table_rows, row))

        got = exchanged(packing(pack, packed_rows(slots), residual, placed, own, moved(other, "ex", on_core)), devices)
        return called(functools.partial(first_table_kernel, slots, pb, table_rows, False), whole, got)

    half = block // 2
    lent = half // 2 // 16 * 16
    ends = half - lent
    front, back, front_end, back_end, *others = cut_inputs(query, train, lent, 4)
    x_one = moved(front, "pb", on_x)
    y_one = moved(back, "pb", on_y)
    x_end = moved(back_end, "pb", on_x)
    y_end = moved(front_end, "pb", on_y)

    early, late = Slots(capacity, 2 * block, True), Slots(capacity, 2 * block, False)

    def units():
        me, layer = lax.axis_index("pb"), lax.axis_index("ex") // 2 % 2
        same = (me % 2 + me // 2) % 2
        unit = lambda near, part: (2 * (same if near else 1 - same) + part) * half
        return unit, layer, 1 - layer

    def first_pack(scale, row, home_ref, own_ref, got_ref, out_ref, base_ref):
        unit, mine, theirs = units()
        found = selects(early, table_rows, devices * 8, row)
        near = weighted(own_ref, got_ref, scale)
        table = ordered(early, weighted(home_ref, None, scale), [(unit(True, 0), block)])
        table += ordered(early, near, [(unit(False, mine), half), (unit(False, theirs), half)])
        put(early, found, table, out_ref, digits(early, table_rows, row))
        left = [(None, 2 * half), (unit(False, theirs) + lent, ends), (unit(False, mine) + lent, ends)]
        put(late, found, ordered(late, near, left), base_ref)

    def last_pack(scale, row, own_ref, got_ref, base_ref, out_ref):
        unit, mine, theirs = units()
        found = selects(late, table_rows, devices * 8, row)
        spans = [(unit(True, theirs), half), (unit(True, mine), half)]
        spans += [(unit(False, theirs), lent), (unit(False, mine), lent)]
        put(late, found, ordered(late, weighted(own_ref, got_ref, scale), spans), out_ref, None, base_ref)

    others = [moved(part, "ex", on_core) for part in others]
    own = lax.dynamic_slice(train, (0, core * deep), (rows, deep))
    (scores_own,) = scored([[train]], [query])
    x_one, y_one, others, own, scores_own, placed = lax.optimization_barrier(
        (x_one, y_one, others, own, scores_own, placed)
    )

    (z_sent,) = stacked([(x_one, 0, lent), (y_one, 0, lent)])
    z_lent = moved(z_sent, "ex", on_z)
    x_two = moved(y_one, "pb", on_x)
    y_two = moved(x_one, "pb", on_y)

    own_a, other_a = scored([[own], others], [x_one, y_one, x_end, y_end])
    got_a = moved(other_a, "ex", on_core)
    shapes = [packed_rows(early), packed_rows(late)]
    rows_a, base = packing(first_pack, shapes, residual, placed, scores_own, own_a, got_a)
    sent_a = exchanged(rows_a, devices)
    own, others, base = lax.optimization_barrier((own, others, base))

    pieces = [x_two, y_two, z_lent]
    (other_b,) = scored([others], pieces)
    got_b = moved(other_b, "ex", on_core)
    (own_b,) = scored([[own]], pieces)
    sent_b = exchanged(packing(last_pack, packed_rows(late), residual, placed, own_b, got_b, base), devices)

    hot = jax.ShapeDtypeStruct((early.groups, devices * 8, table_rows), jnp.bfloat16)
    table, hot = called(functools.partial(first_table_kernel, early, pb, table_rows, True), [whole, hot], sent_a)
    return called(functools.partial(last_table_kernel, late, pb), whole, table, hot, sent_b)


def solution(mesh):
    return jax.shard_map(
        on_device,
        mesh=mesh,
        in_specs=(P(BOTH, None), P("pb", None), P(BOTH), P(BOTH), P()),
        out_specs=P(BOTH, None),
        check_vma=False,
    )
```

time: 86 us -> 78.6 us (0.914)
  waiting for transfers between devices: 22.7 us -> 34.2 us
  local copies, waits for them, and re-layouts: 15.5 us -> 4.84 us
  starting transfers between devices: 23.3 us -> 18.1 us
  Pallas kernels: 23.4 us -> 20.9 us
    unnamed x42 -> x18, local copies, waits for them, and re-layouts: 13.8 us -> 2.11 us
    ppermute x15 -> x13, waiting for transfers between devices: 8.92 us -> 19.7 us  [moved(): return lax.ppermute(value, axis, [(i, target(i)) for i in range(count)])]
    pallas_call x5 -> x2, Pallas kernels: 7.53 us -> 2.65 us  [called(): pl.pallas_call(body, out_shape=shapes, compiler_params=LIMIT, cost_estima...]
    all_to_all x2, starting transfers between devices: 11.6 us -> 8.37 us  [exchanged(): lax.all_to_all(apart, BOTH, split_axis=0, concat_axis=0).reshape(rows.shape)]
    pallas_call x1 -> x2, Pallas kernels: 0.2 us -> 2.91 us  [packing(): pl.pallas_call(kernel, in_specs=[HBM] * 2 + [VMEM] * len(operands), out_s...]
    pallas_call x2 -> x1, Pallas kernels: 4.88 us -> 2.3 us  [stacked(): pl.pallas_call(body, out_shape=shapes, compiler_params=LIMIT, cost_estima...]
    ppermute x15 -> x13, starting transfers between devices: 11.6 us -> 9.72 us  [moved(): return lax.ppermute(value, axis, [(i, target(i)) for i in range(count)])]
    pallas_call x4, Pallas kernels: 8.22 us -> 9.75 us  [scored(): pl.pallas_call(functools.partial(scores_kernel, [len(group) for group in...]
  transfers between devices with their start and end apart: 17 -> 15, of which waited for: 6 -> 8; matrix products, arithmetic and copies ran while one was open for 2% -> 4% of each run, Pallas kernels for 18% -> 20%
where the time goes in v4:
time: 78.6 us; the launch traced here: 78.3 us
  waiting for transfers between devices  34.2 us (44%)
  Pallas kernels  20.9 us (27%)
  starting transfers between devices  18.1 us (23%)
  local copies, waits for them, and re-layouts  4.84 us (6%)
    ppermute x13, waiting for transfers between devices, moved(): return lax.ppermute(value, axis, [(i, target(i)) for i in range(count)])  19.7 us
    all_to_all x2, waiting for transfers between devices, exchanged(): lax.all_to_all(apart, BOTH, split_axis=0, concat_axis=0).reshape(rows.shape)  14.5 us
    pallas_call x4, Pallas kernels, scored(): pl.pallas_call(functools.partial(scores_kernel, [len(group) for group in...  9.75 us
    ppermute x13, starting transfers between devices, moved(): return lax.ppermute(value, axis, [(i, target(i)) for i in range(count)])  9.72 us
    all_to_all x2, starting transfers between devices, exchanged(): lax.all_to_all(apart, BOTH, split_axis=0, concat_axis=0).reshape(rows.shape)  8.37 us
    pallas_call x1, Pallas kernels, relayed(): pl.pallas_call(body, in_specs=[HBM] * len(inputs), out_specs=[HBM] * len(...  3.3 us
    pallas_call x2, Pallas kernels, packing(): pl.pallas_call(kernel, in_specs=[HBM] * 2 + [VMEM] * len(operands), out_s...  2.91 us
    pallas_call x2, Pallas kernels, called(): pl.pallas_call(body, out_shape=shapes, compiler_params=LIMIT, cost_estima...  2.65 us
  transfers between devices with their start and end apart: 15, of which 8 were waited for; matrix products, arithmetic and copies ran while one was open for 4% of the time, Pallas kernels for 20%

profile of v4, /device:TPU:0, one launch (start us, length us, event | category | flops | bytes accessed | tf_op | source)
XLA Modules:
  0.0 78.3 jit_solution(16848526689033397323)
XLA Ops:
  0.0 3.3 %shard_map.55 = (bf16[96,4096]{1,0:T(8,128)(2,1)}, bf16[96,4096]{1,0:T(8,128)(2,1)}, bf16[48,4096]{1,0:T(8,128)(2,1)}, bf16[48,4096]{1,0:T(8,128)(2,1)}, bf16[48...) custom-call(bf16[192,8192]{1,0:T(8,128)(2,1)} %refs_1_.1, ...), custom_call_target="tpu_custom_call" | custom-call | flops 1 | bytes 1 | tf_op jit(solution)/shard_map/pallas_call | solution.py:57
  3.3 0.0 copy-start.8
  3.3 3.0 %collective-permute-start = (bf16[96,4096]{1,0:T(8,128)(2,1)}, bf16[96,4096]{1,0:T(8,128)(2,1)}, u32[]{:S(2)}, u32[]{:S(2)}) collective-permute-start(bf16[96,4096]{1,0:T(8,128)(2,1)} %get-tuple-element.34), channel_id=1, source_target_pairs={{0,1},{1,0},{2,3},{3,2},{4,5},{5,4},{6,7},{7,6},{8,9},{9,8},{10,11... | collective-permute-start | bytes 2359304 | tf_op jit(solution)/shard_map/ppermute | solution.py:22
  6.3 1.5 %collective-permute-start.1 = (bf16[96,4096]{1,0:T(8,128)(2,1)}, bf16[96,4096]{1,0:T(8,128)(2,1)}, u32[]{:S(2)}, u32[]{:S(2)}) collective-permute-start(bf16[96,4096]{1,0:T(8,128)(2,1)} %get-tuple-element.35), channel_id=1, source_target_pairs={{0,2},{1,3},{2,0},{3,1},{4,6},{5,7},{6,4},{7,5},{8,10},{9,11},{10,... | collective-permute-start | bytes 2359304 | tf_op jit(solution)/shard_map/ppermute | solution.py:22
  7.9 0.0 collective-permute-start.2
  7.9 0.5 collective-permute-start.3
  8.4 0.0 collective-permute-start.4
  8.4 0.0 copy-done.1
  8.4 1.3 %constant_dynamic-slice_fusion.refs_0_ = bf16[192,4096]{1,0:T(8,128)(2,1)} fusion(bf16[192,8192]{1,0:T(8,128)(2,1)S(1)} %copy-done.1, s32[]{:T(128)S(6)} %select_n.20), kind=kLoop, calls=%fused_computation.4 | loop fusion | bytes 3145732 | tf_op jit(solution)/shard_map/dynamic_slice | solution.py:359
  9.7 0.3 collective-permute-done.2.refs_1_.refs_0_
  9.9 0.3 collective-permute-start.5
  10.2 0.6 copy-done.3
  10.8 1.0 %shard_map.56.refs_0_ = f32[192,192]{1,0:T(8,128)S(1)} custom-call(bf16[192,8192]{1,0:T(8,128)(2,1)S(1)} %copy-done.1, bf16[192,8192]{1,0:T(8,128)(2,1)S(1)} %copy-done.3), custom_call_target="tpu_custom_call" | custom-call | flops 1 | bytes 1 | tf_op jit(solution)/shard_map/pallas_call | solution.py:48
  11.9 1.4 %gather_fusion = s32[192]{0:T(256)S(1)} fusion(s32[8192]{0:T(1024)S(1)} %copy-done, s32[1024]{0:T(1024)S(1)} %pad_clamp_fusion), kind=kCustom, calls=%fused_computation | custom fusion | bytes 2304 | tf_op jit(solution)/shard_map/jit(_take)/gather | solution.py:307
  13.3 0.0 collective-permute-done.3.refs_2_.refs_1_
  13.3 0.6 collective-permute-start.6
  13.9 0.0 collective-permute-done.4.refs_3_.refs_2_
  13.9 0.1 collective-permute-start.7
  14.0 0.0 collective-permute-done.5.refs_4_.refs_3_
  14.0 11.0 %collective-permute-done.refs_5_.refs_0_ = bf16[96,4096]{1,0:T(8,128)(2,1)} collective-permute-done((bf16[96,4096]{1,0:T(8,128)(2,1)}, bf16[96,4096]{1,0:T(8,128)(2,1)}, u32[]{:S(2)}, u32[]{:S(2)}) %collective-permute-start) | collective-permute-done | bytes 786464 | tf_op jit(solution)/shard_map/ppermute | solution.py:22
  25.0 2.1 %collective-permute-done.1.refs_6_.refs_1_ = bf16[96,4096]{1,0:T(8,128)(2,1)} collective-permute-done((bf16[96,4096]{1,0:T(8,128)(2,1)}, bf16[96,4096]{1,0:T(8,128)(2,1)}, u32[]{:S(2)}, u32[]{:S(2)}) %collective-permute-start.1) | collective-permute-done | bytes 786464 | tf_op jit(solution)/shard_map/ppermute | solution.py:22
  27.1 2.3 %shard_map.60 = bf16[96,4096]{1,0:T(8,128)(2,1)} custom-call(bf16[96,4096]{1,0:T(8,128)(2,1)} %collective-permute-done.refs_5_.refs_0_, bf16[96,4096]{1,0:T(8,128)(2,1)} %collective-permute-done.1.refs_6_.refs_1_), custom_call_target="tpu_custom_call" | custom-call | flops 1 | bytes 1 | tf_op jit(solution)/shard_map/pallas_call | solution.py:129
  29.4 1.6 %collective-permute-start.11 = (bf16[96,4096]{1,0:T(8,128)(2,1)}, bf16[96,4096]{1,0:T(8,128)(2,1)S(1)}, u32[]{:S(2)}, u32[]{:S(2)}) collective-permute-start(bf16[96,4096]{1,0:T(8,128)(2,1)} %shard_map.60), channel_id=1, source_target_pairs={{0,8},{4,12},{8,0},{12,4},{16,24},{20,28},{24,16},{28,20},{1,9},{5... | collective-permute-start | bytes 2359304 | tf_op jit(solution)/shard_map/ppermute | solution.py:22
  31.0 1.5 %collective-permute-start.10 = (bf16[96,4096]{1,0:T(8,128)(2,1)}, bf16[96,4096]{1,0:T(8,128)(2,1)S(1)}, u32[]{:S(2)}, u32[]{:S(2)}) collective-permute-start(bf16[96,4096]{1,0:T(8,128)(2,1)} %collective-permute-done.refs_5_.refs_0_), channel_id=1, source_target_pairs={{0,2},{1,3},{2,0},{3,1},{4,6},{5,7},{6,4},{7,5},{8,10},{9,11},{10,... | collective-permute-start | bytes 2359304 | tf_op jit(solution)/shard_map/ppermute | solution.py:22
  32.5 0.5 collective-permute-start.9
  33.0 0.0 collective-permute-done.6.refs_7_
  33.1 2.4 %collective-permute-done.7.refs_8_ = bf16[48,4096]{1,0:T(8,128)(2,1)S(1)} collective-permute-done((bf16[48,4096]{1,0:T(8,128)(2,1)}, bf16[48,4096]{1,0:T(8,128)(2,1)S(1)}, u32[]{:S(2)}, u32[]{:S(2)}) %collective-permute-start.7) | collective-permute-done | bytes 393248 | tf_op jit(solution)/shard_map/ppermute | solution.py:22
  35.4 3.6 %shard_map.57 = (f32[192,288]{1,0:T(8,128)S(1)}, f32[192,288]{1,0:T(8,128)S(1)}) custom-call(bf16[192,4096]{1,0:T(8,128)(2,1)S(1)} %copy-done.2, bf16[48,4096]{1,0:T(8,128)(2,1)} %collective-permute-done.2.refs_1_.refs_0_, bf16[48,4096]{1,0:T(8,128)(2,1)} %collective-permute-done.3.refs_2_.refs_1_, bf16[48,4096]{1,0:T(8,128)(2,1)} %collective-permute-done.4.refs_3_.refs_2_, ...), custom_call_target="tpu_custom_call" | custom-call | flops 1 | bytes 1 | tf_op jit(solution)/shard_map/pallas_call | solution.py:48
  39.1 0.1 collective-permute-start.8
  39.2 1.6 %collective-permute-done.8.refs_2_ = f32[192,288]{1,0:T(8,128)S(1)} collective-permute-done((f32[192,288]{1,0:T(8,128)S(1)}, f32[192,288]{1,0:T(8,128)S(1)}, u32[]{:S(2)}, u32[]{:S(2)}) %collective-permute-start.8) | collective-permute-done | bytes 221216 | tf_op jit(solution)/shard_map/ppermute | solution.py:22
  40.7 1.3 %shard_map.58 = (bf16[256,580]{1,0:T(8,128)(2,1)S(1)}, bf16[256,576]{1,0:T(8,128)(2,1)S(1)}) custom-call(f32[1,192]{1,0:T(1,128)S(1)} %bitcast.11, s32[1,192]{1,0:T(1,128)S(1)} %bitcast.9, f32[192,192]{1,0:T(8,128)S(1)} %shard_map.56.refs_0_, f32[192,288]{1,0:T(8,128)S(1)} %get-tuple-element.51.refs_1_, f32[192,288]{1,0:T(8,128)S(1)} %collective-permute-done.8.refs_2_), custom_call_target="tpu_custom_call" | custom-call | flops 1 | bytes 1 | tf_op jit(solution)/shard_map/pallas_call | solution.py:175
  42.1 0.7 copy-done.4
  42.8 0.7 copy-done.5
  43.5 4.9 %all-to-all-start = ((bf16[32,8,580]{2,1,0:T(8,128)(2,1)}), bf16[32,8,580]{2,1,0:T(8,128)(2,1)S(1)}, u32[]{:S(2)}, u32[]{:S(2)}) async-start(bf16[32,8,580]{2,1,0:T(8,128)(2,1)} %bitcast.8), calls=%async_computation | async-start | bytes 655360 | tf_op jit(solution)/shard_map/all_to_all | solution.py:238
  48.5 0.0 collective-permute-done.11.refs_3_.refs_6_
  48.5 2.4 %collective-permute-done.10.refs_2_.refs_5_ = bf16[96,4096]{1,0:T(8,128)(2,1)S(1)} collective-permute-done((bf16[96,4096]{1,0:T(8,128)(2,1)}, bf16[96,4096]{1,0:T(8,128)(2,1)S(1)}, u32[]{:S(2)}, u32[]{:S(2)}) %collective-permute-start.10) | collective-permute-done | bytes 786464 | tf_op jit(solution)/shard_map/ppermute | solution.py:22
  50.8 0.0 collective-permute-done.9.refs_1_.refs_4_
  50.8 2.8 %shard_map.62 = f32[192,288]{1,0:T(8,128)S(1)} custom-call(bf16[48,4096]{1,0:T(8,128)(2,1)} %collective-permute-done.2.refs_1_.refs_0_, bf16[48,4096]{1,0:T(8,128)(2,1)} %collective-permute-done.3.refs_2_.refs_1_, bf16[48,4096]{1,0:T(8,128)(2,1)} %collective-permute-done.4.refs_3_.refs_2_, bf16[48,4096]{1,0:T(8,128)(2,1)} %collective-permute-done.5.refs_4_.refs_3_, ...), custom_call_target="tpu_custom_call" | custom-call | flops 1 | bytes 1 | tf_op jit(solution)/shard_map/pallas_call | solution.py:48
  53.6 0.1 collective-permute-start.12
  53.7 2.3 %shard_map.61.refs_0_ = f32[192,288]{1,0:T(8,128)S(1)} custom-call(bf16[192,4096]{1,0:T(8,128)(2,1)S(1)} %copy-done.2, bf16[96,4096]{1,0:T(8,128)(2,1)} %collective-permute-done.9.refs_1_.refs_4_, bf16[96,4096]{1,0:T(8,128)(2,1)S(1)} %collective-permute-done.10.refs_2_.refs_5_, bf16[96,4096]{1,0:T(8,128)(2,1)S(1)} %collective-permute-done.11.refs_3_.refs_6_), custom_call_target="tpu_custom_call" | custom-call | flops 1 | bytes 1 | tf_op jit(solution)/shard_map/pallas_call | solution.py:48
  56.0 0.0 collective-permute-done.12.refs_1_
  56.1 0.0 copy-done.6
  56.1 1.6 %shard_map.63 = bf16[256,576]{1,0:T(8,128)(2,1)} custom-call(f32[1,192]{1,0:T(1,128)S(1)} %bitcast.12, s32[1,192]{1,0:T(1,128)S(1)} %bitcast.10, f32[192,288]{1,0:T(8,128)S(1)} %shard_map.61.refs_0_, f32[192,288]{1,0:T(8,128)S(1)} %collective-permute-done.12.refs_1_, bf16[256,576]{1,0:T(8,128)(2,1)S(1)} %copy-done.6), custom_call_target="tpu_custom_call" | custom-call | flops 1 | bytes 1 | tf_op jit(solution)/shard_map/pallas_call | solution.py:175
  57.6 3.1 %all-to-all-done = bf16[32,8,580]{2,1,0:T(8,128)(2,1)S(1)} async-done(((bf16[32,8,580]{2,1,0:T(8,128)(2,1)}), bf16[32,8,580]{2,1,0:T(8,128)(2,1)S(1)}, u32[]{:S(2)}, u32[]{:S(2)}) %all-to-all-start) | async-done | bytes 296992 | tf_op jit(solution)/shard_map/all_to_all | solution.py:238
  60.7 3.4 %all-to-all-start.1 = ((bf16[32,8,576]{2,1,0:T(8,128)(2,1)}), bf16[32,8,576]{2,1,0:T(8,128)(2,1)S(1)}, u32[]{:S(2)}, u32[]{:S(2)}) async-start(bf16[32,8,576]{2,1,0:T(8,128)(2,1)} %bitcast.4), calls=%async_computation.1 | async-start | bytes 655360 | tf_op jit(solution)/shard_map/all_to_all | solution.py:238
  64.2 0.9 %shard_map.59 = (f32[256,768]{1,0:T(8,128)S(1)}, bf16[2,256,256]{2,1,0:T(8,128)(2,1)S(1)}) custom-call(bf16[256,580]{1,0:T(8,128)(2,1)S(1)} %bitcast.6), custom_call_target="tpu_custom_call" | custom-call | flops 1 | bytes 1 | tf_op jit(solution)/shard_map/pallas_call | solution.py:233
  65.1 11.4 %all-to-all-done.1 = bf16[32,8,576]{2,1,0:T(8,128)(2,1)S(1)} async-done(((bf16[32,8,576]{2,1,0:T(8,128)(2,1)}), bf16[32,8,576]{2,1,0:T(8,128)(2,1)S(1)}, u32[]{:S(2)}, u32[]{:S(2)}) %all-to-all-start.1) | async-done | bytes 294944 | tf_op jit(solution)/shard_map/all_to_all | solution.py:238
  76.5 1.8 %shard_map.64 = f32[256,768]{1,0:T(8,128)} custom-call(f32[256,768]{1,0:T(8,128)S(1)} %get-tuple-element.54.first_ref, bf16[2,256,256]{2,1,0:T(8,128)(2,1)S(1)} %get-tuple-element.55.hot_ref, bf16[256,576]{1,0:T(8,128)(2,1)S(1)} %bitcast.7), custom_call_target="tpu_custom_call" | custom-call | flops 1 | bytes 1 | tf_op jit(solution)/shard_map/pallas_call | solution.py:233
  (15 shorter events, 0.0 us)
Async XLA Ops:
  0.0 11.8 %copy-start = (s32[8192]{0:T(1024)S(1)}, s32[8192]{0:T(1024)}, u32[]{:S(2)}) copy-start(s32[8192]{0:T(1024)} %param.9) | copy-start | bytes 98308
  0.0 8.4 %copy-start.1 = (bf16[192,8192]{1,0:T(8,128)(2,1)S(1)}, bf16[192,8192]{1,0:T(8,128)(2,1)}, u32[]{:S(2)}) copy-start(bf16[192,8192]{1,0:T(8,128)(2,1)} %refs_0_.1) | copy-start | bytes 9437188
  3.3 6.9 %copy-start.8 = (s32[192]{0:T(256)S(1)}, s32[192]{0:T(256)}, u32[]{:S(2)}) copy-start(s32[192]{0:T(256)} %param.8) | copy-start | bytes 2308
  3.3 21.7 %collective-permute-start = (bf16[96,4096]{1,0:T(8,128)(2,1)}, bf16[96,4096]{1,0:T(8,128)(2,1)}, u32[]{:S(2)}, u32[]{:S(2)}) collective-permute-start(bf16[96,4096]{1,0:T(8,128)(2,1)} %get-tuple-element.34), channel_id=1, source_target_pairs={{0,1},{1,0},{2,3},{3,2},{4,5},{5,4},{6,7},{7,6},{8,9},{9,8},{10,11... | collective-permute-start | bytes 2359304 | tf_op jit(solution)/shard_map/ppermute | solution.py:22
  6.3 20.8 %collective-permute-start.1 = (bf16[96,4096]{1,0:T(8,128)(2,1)}, bf16[96,4096]{1,0:T(8,128)(2,1)}, u32[]{:S(2)}, u32[]{:S(2)}) collective-permute-start(bf16[96,4096]{1,0:T(8,128)(2,1)} %get-tuple-element.35), channel_id=1, source_target_pairs={{0,2},{1,3},{2,0},{3,1},{4,6},{5,7},{6,4},{7,5},{8,10},{9,11},{10,... | collective-permute-start | bytes 2359304 | tf_op jit(solution)/shard_map/ppermute | solution.py:22
  7.9 2.1 %collective-permute-start.2 = (bf16[48,4096]{1,0:T(8,128)(2,1)}, bf16[48,4096]{1,0:T(8,128)(2,1)}, u32[]{:S(2)}, u32[]{:S(2)}) collective-permute-start(bf16[48,4096]{1,0:T(8,128)(2,1)} %get-tuple-element.36), channel_id=1, source_target_pairs={{0,4},{4,0},{8,12},{12,8},{16,20},{20,16},{24,28},{28,24},{1,5},{5... | collective-permute-start | bytes 1179656 | tf_op jit(solution)/shard_map/ppermute | solution.py:22
  7.9 5.5 %collective-permute-start.3 = (bf16[48,4096]{1,0:T(8,128)(2,1)}, bf16[48,4096]{1,0:T(8,128)(2,1)}, u32[]{:S(2)}, u32[]{:S(2)}) collective-permute-start(bf16[48,4096]{1,0:T(8,128)(2,1)} %get-tuple-element.37), channel_id=1, source_target_pairs={{0,4},{4,0},{8,12},{12,8},{16,20},{20,16},{24,28},{28,24},{1,5},{5... | collective-permute-start | bytes 1179656 | tf_op jit(solution)/shard_map/ppermute | solution.py:22
  8.4 5.6 %collective-permute-start.4 = (bf16[48,4096]{1,0:T(8,128)(2,1)}, bf16[48,4096]{1,0:T(8,128)(2,1)}, u32[]{:S(2)}, u32[]{:S(2)}) collective-permute-start(bf16[48,4096]{1,0:T(8,128)(2,1)} %get-tuple-element.38), channel_id=1, source_target_pairs={{0,4},{4,0},{8,12},{12,8},{16,20},{20,16},{24,28},{28,24},{1,5},{5... | collective-permute-start | bytes 1179656 | tf_op jit(solution)/shard_map/ppermute | solution.py:22
  8.4 2.5 %copy-start.3 = (bf16[192,8192]{1,0:T(8,128)(2,1)S(1)}, bf16[192,8192]{1,0:T(8,128)(2,1)}, u32[]{:S(2)}) copy-start(bf16[192,8192]{1,0:T(8,128)(2,1)} %refs_1_.1) | copy-start | bytes 9437188
  9.9 4.1 %collective-permute-start.5 = (bf16[48,4096]{1,0:T(8,128)(2,1)}, bf16[48,4096]{1,0:T(8,128)(2,1)}, u32[]{:S(2)}, u32[]{:S(2)}) collective-permute-start(bf16[48,4096]{1,0:T(8,128)(2,1)} %get-tuple-element.39), channel_id=1, source_target_pairs={{0,4},{4,0},{8,12},{12,8},{16,20},{20,16},{24,28},{28,24},{1,5},{5... | collective-permute-start | bytes 1179656 | tf_op jit(solution)/shard_map/ppermute | solution.py:22
  11.8 23.6 %copy-start.2 = (bf16[192,4096]{1,0:T(8,128)(2,1)S(1)}, bf16[192,4096]{1,0:T(8,128)(2,1)}, u32[]{:S(2)}) copy-start(bf16[192,4096]{1,0:T(8,128)(2,1)} %constant_dynamic-slice_fusion.refs_0_) | copy-start | bytes 4718596
  13.3 19.7 %collective-permute-start.6 = (bf16[48,4096]{1,0:T(8,128)(2,1)}, bf16[48,4096]{1,0:T(8,128)(2,1)S(1)}, u32[]{:S(2)}, u32[]{:S(2)}) collective-permute-start(bf16[48,4096]{1,0:T(8,128)(2,1)} %get-tuple-element.49), channel_id=1, source_target_pairs={{0,1},{1,0},{2,3},{3,2},{4,5},{5,4},{6,7},{7,6},{8,9},{9,8},{10,11... | collective-permute-start | bytes 1179656 | tf_op jit(solution)/shard_map/ppermute | solution.py:22
  13.9 21.5 %collective-permute-start.7 = (bf16[48,4096]{1,0:T(8,128)(2,1)}, bf16[48,4096]{1,0:T(8,128)(2,1)S(1)}, u32[]{:S(2)}, u32[]{:S(2)}) collective-permute-start(bf16[48,4096]{1,0:T(8,128)(2,1)} %get-tuple-element.50), channel_id=1, source_target_pairs={{0,2},{1,3},{2,0},{3,1},{4,6},{5,7},{6,4},{7,5},{8,10},{9,11},{10,... | collective-permute-start | bytes 1179656 | tf_op jit(solution)/shard_map/ppermute | solution.py:22
  29.4 11.3 %copy-start.7 = (f32[192]{0:T(256)S(1)}, f32[192]{0:T(256)}, u32[]{:S(2)}) copy-start(f32[192]{0:T(256)} %param.7) | copy-start | bytes 2308
  29.4 19.0 %collective-permute-start.11 = (bf16[96,4096]{1,0:T(8,128)(2,1)}, bf16[96,4096]{1,0:T(8,128)(2,1)S(1)}, u32[]{:S(2)}, u32[]{:S(2)}) collective-permute-start(bf16[96,4096]{1,0:T(8,128)(2,1)} %shard_map.60), channel_id=1, source_target_pairs={{0,8},{4,12},{8,0},{12,4},{16,24},{20,28},{24,16},{28,20},{1,9},{5... | collective-permute-start | bytes 2359304 | tf_op jit(solution)/shard_map/ppermute | solution.py:22
  31.0 19.8 %collective-permute-start.10 = (bf16[96,4096]{1,0:T(8,128)(2,1)}, bf16[96,4096]{1,0:T(8,128)(2,1)S(1)}, u32[]{:S(2)}, u32[]{:S(2)}) collective-permute-start(bf16[96,4096]{1,0:T(8,128)(2,1)} %collective-permute-done.refs_5_.refs_0_), channel_id=1, source_target_pairs={{0,2},{1,3},{2,0},{3,1},{4,6},{5,7},{6,4},{7,5},{8,10},{9,11},{10,... | collective-permute-start | bytes 2359304 | tf_op jit(solution)/shard_map/ppermute | solution.py:22
  32.5 18.3 %collective-permute-start.9 = (bf16[96,4096]{1,0:T(8,128)(2,1)}, bf16[96,4096]{1,0:T(8,128)(2,1)}, u32[]{:S(2)}, u32[]{:S(2)}) collective-permute-start(bf16[96,4096]{1,0:T(8,128)(2,1)} %collective-permute-done.1.refs_6_.refs_1_), channel_id=1, source_target_pairs={{0,1},{1,0},{2,3},{3,2},{4,5},{5,4},{6,7},{7,6},{8,9},{9,8},{10,11... | collective-permute-start | bytes 2359304 | tf_op jit(solution)/shard_map/ppermute | solution.py:22
  39.1 1.6 %collective-permute-start.8 = (f32[192,288]{1,0:T(8,128)S(1)}, f32[192,288]{1,0:T(8,128)S(1)}, u32[]{:S(2)}, u32[]{:S(2)}) collective-permute-start(f32[192,288]{1,0:T(8,128)S(1)} %get-tuple-element.52), channel_id=1, source_target_pairs={{0,4},{4,0},{8,12},{12,8},{16,20},{20,16},{24,28},{28,24},{1,5},{5... | collective-permute-start | bytes 663560 | tf_op jit(solution)/shard_map/ppermute | solution.py:22
  42.1 0.7 copy-start.4
  42.8 0.7 copy-start.5
  43.5 17.2 %all-to-all-start = ((bf16[32,8,580]{2,1,0:T(8,128)(2,1)}), bf16[32,8,580]{2,1,0:T(8,128)(2,1)S(1)}, u32[]{:S(2)}, u32[]{:S(2)}) async-start(bf16[32,8,580]{2,1,0:T(8,128)(2,1)} %bitcast.8), calls=%async_computation | async-start | bytes 655360 | tf_op jit(solution)/shard_map/all_to_all | solution.py:238
  53.6 2.4 %copy-start.6 = (bf16[256,576]{1,0:T(8,128)(2,1)S(1)}, bf16[256,576]{1,0:T(8,128)(2,1)}, u32[]{:S(2)}) copy-start(bf16[256,576]{1,0:T(8,128)(2,1)} %copy-done.5) | copy-start | bytes 884740
  53.6 2.4 %collective-permute-start.12 = (f32[192,288]{1,0:T(8,128)S(1)}, f32[192,288]{1,0:T(8,128)S(1)}, u32[]{:S(2)}, u32[]{:S(2)}) collective-permute-start(f32[192,288]{1,0:T(8,128)S(1)} %shard_map.62), channel_id=1, source_target_pairs={{0,4},{4,0},{8,12},{12,8},{16,20},{20,16},{24,28},{28,24},{1,5},{5... | collective-permute-start | bytes 663560 | tf_op jit(solution)/shard_map/ppermute | solution.py:22
  60.7 15.7 %all-to-all-start.1 = ((bf16[32,8,576]{2,1,0:T(8,128)(2,1)}), bf16[32,8,576]{2,1,0:T(8,128)(2,1)S(1)}, u32[]{:S(2)}, u32[]{:S(2)}) async-start(bf16[32,8,576]{2,1,0:T(8,128)(2,1)} %bitcast.4), calls=%async_computation.1 | async-start | bytes 655360 | tf_op jit(solution)/shard_map/all_to_all | solution.py:238

commit v5 on v4

--- a/solution.py
+++ b/solution.py
@@ -348,12 +348,13 @@
         left = [(None, 2 * half), (unit(False, theirs) + lent, ends), (unit(False, mine) + lent, ends)]
         put(late, found, ordered(late, near, left), base_ref)
 
-    def last_pack(scale, row, own_ref, got_ref, base_ref, out_ref):
+    def last_pack(scale, row, own_z, got_z, own_ref, got_ref, base_ref, out_ref):
         unit, mine, theirs = units()
         found = selects(late, table_rows, devices * 8, row)
+        lent_spans = [(unit(False, theirs), lent), (unit(False, mine), lent)]
         spans = [(unit(True, theirs), half), (unit(True, mine), half)]
-        spans += [(unit(False, theirs), lent), (unit(False, mine), lent)]
-        put(late, found, ordered(late, weighted(own_ref, got_ref, scale), spans), out_ref, None, base_ref)
+        table = ordered(late, weighted(own_z, got_z, scale), lent_spans)
+        put(late, found, table + ordered(late, weighted(own_ref, got_ref, scale), spans), out_ref, None, base_ref)
 
     others = [moved(part, "ex", on_core) for part in others]
     own = lax.dynamic_slice(train, (0, core * deep), (rows, deep))
@@ -374,11 +375,14 @@
     sent_a = exchanged(rows_a, devices)
     own, others, base = lax.optimization_barrier((own, others, base))
 
-    pieces = [x_two, y_two, z_lent]
+    own_z, other_z = scored([[own], others], [z_lent])
+    x_two, y_two, own_z, other_z = lax.optimization_barrier((x_two, y_two, own_z, other_z))
+    got_z = moved(other_z, "ex", on_core)
+    pieces = [x_two, y_two]
     (other_b,) = scored([others], pieces)
     got_b = moved(other_b, "ex", on_core)
     (own_b,) = scored([[own]], pieces)
-    sent_b = exchanged(packing(last_pack, packed_rows(late), residual, placed, own_b, got_b, base), devices)
+    sent_b = exchanged(packing(last_pack, packed_rows(late), residual, placed, own_z, got_z, own_b, got_b, base), devices)
 
     hot = jax.ShapeDtypeStruct((early.groups, devices * 8, table_rows), jnp.bfloat16)
     table, hot = called(functools.partial(first_table_kernel, early, pb, table_rows, True), [whole, hot], sent_a)

time: 78.6 us -> 78 us (level)
  waiting for transfers between devices: 34.2 us -> 28.9 us
  local copies, waits for them, and re-layouts: 4.84 us -> 8.21 us
    ppermute x13 -> x14, waiting for transfers between devices: 19.7 us -> 14 us  [moved(): return lax.ppermute(value, axis, [(i, target(i)) for i in range(count)])]
    unnamed x18 -> x16, local copies, waits for them, and re-layouts: 2.11 us -> 5.27 us
    ppermute x13 -> x14, starting transfers between devices: 9.72 us -> 10.8 us  [moved(): return lax.ppermute(value, axis, [(i, target(i)) for i in range(count)])]
    pallas_call x4 -> x5, Pallas kernels: 9.75 us -> 10.4 us  [scored(): pl.pallas_call(functools.partial(scores_kernel, [len(group) for group in...]
  transfers between devices with their start and end apart: 15 -> 16, of which waited for: 8 -> 8; matrix products, arithmetic and copies ran while one was open for 4% -> 4% of each run, Pallas kernels for 20% -> 21%
where the time goes in v5:
time: 78 us; the launch traced here: 77.4 us
  waiting for transfers between devices  28.9 us (37%)
  Pallas kernels  21.4 us (27%)
  starting transfers between devices  18.7 us (24%)
  local copies, waits for them, and re-layouts  8.21 us (11%)
    all_to_all x2, waiting for transfers between devices, exchanged(): lax.all_to_all(apart, BOTH, split_axis=0, concat_axis=0).reshape(rows.shape)  14.9 us
    ppermute x14, waiting for transfers between devices, moved(): return lax.ppermute(value, axis, [(i, target(i)) for i in range(count)])  14 us
    ppermute x14, starting transfers between devices, moved(): return lax.ppermute(value, axis, [(i, target(i)) for i in range(count)])  10.8 us
    pallas_call x5, Pallas kernels, scored(): pl.pallas_call(functools.partial(scores_kernel, [len(group) for group in...  10.4 us
    all_to_all x2, starting transfers between devices, exchanged(): lax.all_to_all(apart, BOTH, split_axis=0, concat_axis=0).reshape(rows.shape)  7.89 us
    unnamed x16, local copies, waits for them, and re-layouts  5.27 us
    pallas_call x1, Pallas kernels, relayed(): pl.pallas_call(body, in_specs=[HBM] * len(inputs), out_specs=[HBM] * len(...  3.09 us
    pallas_call x2, Pallas kernels, packing(): pl.pallas_call(kernel, in_specs=[HBM] * 2 + [VMEM] * len(operands), out_s...  2.91 us
  transfers between devices with their start and end apart: 16, of which 8 were waited for; matrix products, arithmetic and copies ran while one was open for 4% of the time, Pallas kernels for 21%

profile of v5, /device:TPU:0, one launch (start us, length us, event | category | flops | bytes accessed | tf_op | source)
XLA Modules:
  0.0 77.4 jit_solution(9444698217186288875)
XLA Ops:
  0.0 3.1 %shard_map.55 = (bf16[96,4096]{1,0:T(8,128)(2,1)}, bf16[96,4096]{1,0:T(8,128)(2,1)}, bf16[48,4096]{1,0:T(8,128)(2,1)}, bf16[48,4096]{1,0:T(8,128)(2,1)}, bf16[48...) custom-call(bf16[192,8192]{1,0:T(8,128)(2,1)} %refs_1_.1, ...), custom_call_target="tpu_custom_call" | custom-call | flops 1 | bytes 1 | tf_op jit(solution)/shard_map/pallas_call | solution.py:57
  3.1 0.0 copy-start.7
  3.1 3.0 %collective-permute-start = (bf16[96,4096]{1,0:T(8,128)(2,1)}, bf16[96,4096]{1,0:T(8,128)(2,1)}, u32[]{:S(2)}, u32[]{:S(2)}) collective-permute-start(bf16[96,4096]{1,0:T(8,128)(2,1)} %get-tuple-element.40), channel_id=1, source_target_pairs={{0,1},{1,0},{2,3},{3,2},{4,5},{5,4},{6,7},{7,6},{8,9},{9,8},{10,11... | collective-permute-start | bytes 2359304 | tf_op jit(solution)/shard_map/ppermute | solution.py:22
  6.1 1.5 %collective-permute-start.1 = (bf16[96,4096]{1,0:T(8,128)(2,1)}, bf16[96,4096]{1,0:T(8,128)(2,1)}, u32[]{:S(2)}, u32[]{:S(2)}) collective-permute-start(bf16[96,4096]{1,0:T(8,128)(2,1)} %get-tuple-element.41), channel_id=1, source_target_pairs={{0,2},{1,3},{2,0},{3,1},{4,6},{5,7},{6,4},{7,5},{8,10},{9,11},{10,... | collective-permute-start | bytes 2359304 | tf_op jit(solution)/shard_map/ppermute | solution.py:22
  7.6 0.0 collective-permute-start.2
  7.6 0.5 collective-permute-start.3
  8.1 0.0 collective-permute-start.4
  8.1 1.5 %constant_dynamic-slice_fusion.refs_0_ = bf16[192,4096]{1,0:T(8,128)(2,1)S(1)} fusion(bf16[192,8192]{1,0:T(8,128)(2,1)} %refs_0_.1, s32[]{:T(128)S(6)} %select_n.20), kind=kLoop, calls=%fused_computation.4 | loop fusion | bytes 3145732 | tf_op jit(solution)/shard_map/dynamic_slice | solution.py:360
  9.7 0.6 collective-permute-start.5
  10.3 0.6 collective-permute-start.6
  10.9 0.0 collective-permute-done.4.refs_3_.refs_2_
  10.9 0.3 collective-permute-start.7
  11.2 1.9 %copy-done.1 = bf16[192,8192]{1,0:T(8,128)(2,1)S(1)} copy-done((bf16[192,8192]{1,0:T(8,128)(2,1)S(1)}, bf16[192,8192]{1,0:T(8,128)(2,1)}, u32[]{:S(2)}) %copy-start.1) | copy-done | bytes 3145752
  13.1 1.9 %copy-done.2 = bf16[192,8192]{1,0:T(8,128)(2,1)S(1)} copy-done((bf16[192,8192]{1,0:T(8,128)(2,1)S(1)}, bf16[192,8192]{1,0:T(8,128)(2,1)}, u32[]{:S(2)}) %copy-start.2) | copy-done | bytes 3145752
  15.0 1.0 %shard_map.56.refs_0_ = f32[192,192]{1,0:T(8,128)S(1)} custom-call(bf16[192,8192]{1,0:T(8,128)(2,1)S(1)} %copy-done.1, bf16[192,8192]{1,0:T(8,128)(2,1)S(1)} %copy-done.2), custom_call_target="tpu_custom_call" | custom-call | flops 1 | bytes 1 | tf_op jit(solution)/shard_map/pallas_call | solution.py:48
  16.0 1.4 %gather_fusion = s32[192]{0:T(256)S(1)} fusion(s32[8192]{0:T(1024)S(1)} %copy-done, s32[1024]{0:T(1024)S(1)} %pad_clamp_fusion), kind=kCustom, calls=%fused_computation | custom fusion | bytes 2304 | tf_op jit(solution)/shard_map/jit(_take)/gather | solution.py:307
  17.5 0.0 collective-permute-done.5.refs_4_.refs_3_
  17.5 7.3 %collective-permute-done.refs_5_.refs_0_ = bf16[96,4096]{1,0:T(8,128)(2,1)} collective-permute-done((bf16[96,4096]{1,0:T(8,128)(2,1)}, bf16[96,4096]{1,0:T(8,128)(2,1)}, u32[]{:S(2)}, u32[]{:S(2)}) %collective-permute-start) | collective-permute-done | bytes 786464 | tf_op jit(solution)/shard_map/ppermute | solution.py:22
  24.8 2.1 %collective-permute-done.1.refs_6_.refs_1_ = bf16[96,4096]{1,0:T(8,128)(2,1)} collective-permute-done((bf16[96,4096]{1,0:T(8,128)(2,1)}, bf16[96,4096]{1,0:T(8,128)(2,1)}, u32[]{:S(2)}, u32[]{:S(2)}) %collective-permute-start.1) | collective-permute-done | bytes 786464 | tf_op jit(solution)/shard_map/ppermute | solution.py:22
  26.9 2.3 %shard_map.60 = bf16[96,4096]{1,0:T(8,128)(2,1)} custom-call(bf16[96,4096]{1,0:T(8,128)(2,1)} %collective-permute-done.refs_5_.refs_0_, bf16[96,4096]{1,0:T(8,128)(2,1)} %collective-permute-done.1.refs_6_.refs_1_), custom_call_target="tpu_custom_call" | custom-call | flops 1 | bytes 1 | tf_op jit(solution)/shard_map/pallas_call | solution.py:129
  29.2 1.6 %collective-permute-start.11 = (bf16[96,4096]{1,0:T(8,128)(2,1)}, bf16[96,4096]{1,0:T(8,128)(2,1)}, u32[]{:S(2)}, u32[]{:S(2)}) collective-permute-start(bf16[96,4096]{1,0:T(8,128)(2,1)} %shard_map.60), channel_id=1, source_target_pairs={{0,8},{4,12},{8,0},{12,4},{16,24},{20,28},{24,16},{28,20},{1,9},{5... | collective-permute-start | bytes 2359304 | tf_op jit(solution)/shard_map/ppermute | solution.py:22
  30.8 1.5 %collective-permute-start.10 = (bf16[96,4096]{1,0:T(8,128)(2,1)}, bf16[96,4096]{1,0:T(8,128)(2,1)}, u32[]{:S(2)}, u32[]{:S(2)}) collective-permute-start(bf16[96,4096]{1,0:T(8,128)(2,1)} %collective-permute-done.refs_5_.refs_0_), channel_id=1, source_target_pairs={{0,2},{1,3},{2,0},{3,1},{4,6},{5,7},{6,4},{7,5},{8,10},{9,11},{10,... | collective-permute-start | bytes 2359304 | tf_op jit(solution)/shard_map/ppermute | solution.py:22
  32.3 0.5 collective-permute-start.9
  32.8 0.1 collective-permute-done.6.refs_7_
  32.9 2.4 %collective-permute-done.7.refs_8_ = bf16[48,4096]{1,0:T(8,128)(2,1)} collective-permute-done((bf16[48,4096]{1,0:T(8,128)(2,1)}, bf16[48,4096]{1,0:T(8,128)(2,1)}, u32[]{:S(2)}, u32[]{:S(2)}) %collective-permute-start.7) | collective-permute-done | bytes 393248 | tf_op jit(solution)/shard_map/ppermute | solution.py:22
  35.3 3.4 %shard_map.57 = (f32[192,288]{1,0:T(8,128)S(1)}, f32[192,288]{1,0:T(8,128)S(1)}) custom-call(bf16[192,4096]{1,0:T(8,128)(2,1)S(1)} %constant_dynamic-slice_fusion.refs_0_, bf16[48,4096]{1,0:T(8,128)(2,1)S(1)} %collective-permute-done.2.refs_1_.refs_0_, bf16[48,4096]{1,0:T(8,128)(2,1)S(1)} %collective-permute-done.3.refs_2_.refs_1_, ...), custom_call_target="tpu_custom_call" | custom-call | flops 1 | bytes 1 | tf_op jit(solution)/shard_map/pallas_call | solution.py:48
  38.7 0.1 collective-permute-start.8
  38.8 1.6 %collective-permute-done.8.refs_2_ = f32[192,288]{1,0:T(8,128)S(1)} collective-permute-done((f32[192,288]{1,0:T(8,128)S(1)}, f32[192,288]{1,0:T(8,128)S(1)}, u32[]{:S(2)}, u32[]{:S(2)}) %collective-permute-start.8) | collective-permute-done | bytes 221216 | tf_op jit(solution)/shard_map/ppermute | solution.py:22
  40.4 1.3 %shard_map.58 = (bf16[256,580]{1,0:T(8,128)(2,1)S(1)}, bf16[256,576]{1,0:T(8,128)(2,1)S(1)}) custom-call(f32[1,192]{1,0:T(1,128)S(1)} %bitcast.11, s32[1,192]{1,0:T(1,128)S(1)} %bitcast.9, f32[192,192]{1,0:T(8,128)S(1)} %shard_map.56.refs_0_, f32[192,288]{1,0:T(8,128)S(1)} %get-tuple-element.57.refs_1_, f32[192,288]{1,0:T(8,128)S(1)} %collective-permute-done.8.refs_2_), custom_call_target="tpu_custom_call" | custom-call | flops 1 | bytes 1 | tf_op jit(solution)/shard_map/pallas_call | solution.py:175
  41.7 0.7 copy-done.3
  42.4 0.7 copy-done.4
  43.2 4.9 %all-to-all-start = ((bf16[32,8,580]{2,1,0:T(8,128)(2,1)}), bf16[32,8,580]{2,1,0:T(8,128)(2,1)S(1)}, u32[]{:S(2)}, u32[]{:S(2)}) async-start(bf16[32,8,580]{2,1,0:T(8,128)(2,1)} %bitcast.8), calls=%async_computation | async-start | bytes 655360 | tf_op jit(solution)/shard_map/all_to_all | solution.py:238
  48.1 0.0 collective-permute-done.11.refs_5_
  48.1 2.1 %shard_map.61 = (f32[192,96]{1,0:T(8,128)S(1)}, f32[192,96]{1,0:T(8,128)S(1)}) custom-call(bf16[192,4096]{1,0:T(8,128)(2,1)S(1)} %constant_dynamic-slice_fusion.refs_0_, bf16[48,4096]{1,0:T(8,128)(2,1)S(1)} %collective-permute-done.2.refs_1_.refs_0_, bf16[48,4096]{1,0:T(8,128)(2,1)S(1)} %collective-permute-done.3.refs_2_.refs_1_, ...), custom_call_target="tpu_custom_call" | custom-call | flops 1 | bytes 1 | tf_op jit(solution)/shard_map/pallas_call | solution.py:48
  50.2 0.5 collective-permute-done.10.refs_2_.refs_5_
  50.7 0.0 collective-permute-done.9.refs_1_.refs_4_
  50.7 2.0 %shard_map.63 = f32[192,192]{1,0:T(8,128)S(1)} custom-call(bf16[48,4096]{1,0:T(8,128)(2,1)S(1)} %collective-permute-done.2.refs_1_.refs_0_, bf16[48,4096]{1,0:T(8,128)(2,1)S(1)} %collective-permute-done.3.refs_2_.refs_1_, bf16[48,4096]{1,0:T(8,128)(2,1)S(1)} %collective-permute-done.4.refs_3_.refs_2_, ...), custom_call_target="tpu_custom_call" | custom-call | flops 1 | bytes 1 | tf_op jit(solution)/shard_map/pallas_call | solution.py:48
  52.7 0.1 collective-permute-start.13
  52.8 0.5 collective-permute-start.12
  53.3 2.0 %shard_map.62.refs_2_ = f32[192,192]{1,0:T(8,128)S(1)} custom-call(bf16[192,4096]{1,0:T(8,128)(2,1)S(1)} %constant_dynamic-slice_fusion.refs_0_, bf16[96,4096]{1,0:T(8,128)(2,1)} %collective-permute-done.9.refs_1_.refs_4_, bf16[96,4096]{1,0:T(8,128)(2,1)} %collective-permute-done.10.refs_2_.refs_5_), custom_call_target="tpu_custom_call" | custom-call | flops 1 | bytes 1 | tf_op jit(solution)/shard_map/pallas_call | solution.py:48
  55.3 0.0 collective-permute-done.12.refs_1_
  55.3 0.0 collective-permute-done.13.refs_3_
  55.3 1.6 %shard_map.64 = bf16[256,576]{1,0:T(8,128)(2,1)} custom-call(f32[1,192]{1,0:T(1,128)S(1)} %bitcast.12, s32[1,192]{1,0:T(1,128)S(1)} %bitcast.10, f32[192,96]{1,0:T(8,128)S(1)} %get-tuple-element.70.refs_0_, f32[192,96]{1,0:T(8,128)S(1)} %collective-permute-done.12.refs_1_, f32[192,192]{1,0:T(8,128)S(1)} %shard_map.62.refs_2_, ...), custom_call_target="tpu_custom_call" | custom-call | flops 1 | bytes 1 | tf_op jit(solution)/shard_map/pallas_call | solution.py:175
  56.9 3.5 %all-to-all-done = bf16[32,8,580]{2,1,0:T(8,128)(2,1)S(1)} async-done(((bf16[32,8,580]{2,1,0:T(8,128)(2,1)}), bf16[32,8,580]{2,1,0:T(8,128)(2,1)S(1)}, u32[]{:S(2)}, u32[]{:S(2)}) %all-to-all-start) | async-done | bytes 296992 | tf_op jit(solution)/shard_map/all_to_all | solution.py:238
  60.4 3.0 %all-to-all-start.1 = ((bf16[32,8,576]{2,1,0:T(8,128)(2,1)}), bf16[32,8,576]{2,1,0:T(8,128)(2,1)S(1)}, u32[]{:S(2)}, u32[]{:S(2)}) async-start(bf16[32,8,576]{2,1,0:T(8,128)(2,1)} %bitcast.4), calls=%async_computation.1 | async-start | bytes 655360 | tf_op jit(solution)/shard_map/all_to_all | solution.py:238
  63.4 0.9 %shard_map.59 = (f32[256,768]{1,0:T(8,128)S(1)}, bf16[2,256,256]{2,1,0:T(8,128)(2,1)S(1)}) custom-call(bf16[256,580]{1,0:T(8,128)(2,1)S(1)} %bitcast.6), custom_call_target="tpu_custom_call" | custom-call | flops 1 | bytes 1 | tf_op jit(solution)/shard_map/pallas_call | solution.py:233
  64.3 11.4 %all-to-all-done.1 = bf16[32,8,576]{2,1,0:T(8,128)(2,1)S(1)} async-done(((bf16[32,8,576]{2,1,0:T(8,128)(2,1)}), bf16[32,8,576]{2,1,0:T(8,128)(2,1)S(1)}, u32[]{:S(2)}, u32[]{:S(2)}) %all-to-all-start.1) | async-done | bytes 294944 | tf_op jit(solution)/shard_map/all_to_all | solution.py:238
  75.7 1.8 %shard_map.65 = f32[256,768]{1,0:T(8,128)} custom-call(f32[256,768]{1,0:T(8,128)S(1)} %get-tuple-element.60.first_ref, bf16[2,256,256]{2,1,0:T(8,128)(2,1)S(1)} %get-tuple-element.61.hot_ref, bf16[256,576]{1,0:T(8,128)(2,1)S(1)} %bitcast.7), custom_call_target="tpu_custom_call" | custom-call | flops 1 | bytes 1 | tf_op jit(solution)/shard_map/pallas_call | solution.py:233
  (16 shorter events, 0.0 us)
Async XLA Ops:
  0.0 16.0 %copy-start = (s32[8192]{0:T(1024)S(1)}, s32[8192]{0:T(1024)}, u32[]{:S(2)}) copy-start(s32[8192]{0:T(1024)} %param.9) | copy-start | bytes 98308
  3.1 7.1 %copy-start.7 = (s32[192]{0:T(256)S(1)}, s32[192]{0:T(256)}, u32[]{:S(2)}) copy-start(s32[192]{0:T(256)} %param.8) | copy-start | bytes 2308
  3.1 21.7 %collective-permute-start = (bf16[96,4096]{1,0:T(8,128)(2,1)}, bf16[96,4096]{1,0:T(8,128)(2,1)}, u32[]{:S(2)}, u32[]{:S(2)}) collective-permute-start(bf16[96,4096]{1,0:T(8,128)(2,1)} %get-tuple-element.40), channel_id=1, source_target_pairs={{0,1},{1,0},{2,3},{3,2},{4,5},{5,4},{6,7},{7,6},{8,9},{9,8},{10,11... | collective-permute-start | bytes 2359304 | tf_op jit(solution)/shard_map/ppermute | solution.py:22
  6.1 20.8 %collective-permute-start.1 = (bf16[96,4096]{1,0:T(8,128)(2,1)}, bf16[96,4096]{1,0:T(8,128)(2,1)}, u32[]{:S(2)}, u32[]{:S(2)}) collective-permute-start(bf16[96,4096]{1,0:T(8,128)(2,1)} %get-tuple-element.41), channel_id=1, source_target_pairs={{0,2},{1,3},{2,0},{3,1},{4,6},{5,7},{6,4},{7,5},{8,10},{9,11},{10,... | collective-permute-start | bytes 2359304 | tf_op jit(solution)/shard_map/ppermute | solution.py:22
  7.6 2.0 %collective-permute-start.2 = (bf16[48,4096]{1,0:T(8,128)(2,1)}, bf16[48,4096]{1,0:T(8,128)(2,1)S(1)}, u32[]{:S(2)}, u32[]{:S(2)}) collective-permute-start(bf16[48,4096]{1,0:T(8,128)(2,1)} %get-tuple-element.42), channel_id=1, source_target_pairs={{0,4},{4,0},{8,12},{12,8},{16,20},{20,16},{24,28},{28,24},{1,5},{5... | collective-permute-start | bytes 1179656 | tf_op jit(solution)/shard_map/ppermute | solution.py:22
  7.6 2.6 %collective-permute-start.3 = (bf16[48,4096]{1,0:T(8,128)(2,1)}, bf16[48,4096]{1,0:T(8,128)(2,1)S(1)}, u32[]{:S(2)}, u32[]{:S(2)}) collective-permute-start(bf16[48,4096]{1,0:T(8,128)(2,1)} %get-tuple-element.43), channel_id=1, source_target_pairs={{0,4},{4,0},{8,12},{12,8},{16,20},{20,16},{24,28},{28,24},{1,5},{5... | collective-permute-start | bytes 1179656 | tf_op jit(solution)/shard_map/ppermute | solution.py:22
  8.1 2.7 %collective-permute-start.4 = (bf16[48,4096]{1,0:T(8,128)(2,1)}, bf16[48,4096]{1,0:T(8,128)(2,1)S(1)}, u32[]{:S(2)}, u32[]{:S(2)}) collective-permute-start(bf16[48,4096]{1,0:T(8,128)(2,1)} %get-tuple-element.44), channel_id=1, source_target_pairs={{0,4},{4,0},{8,12},{12,8},{16,20},{20,16},{24,28},{28,24},{1,5},{5... | collective-permute-start | bytes 1179656 | tf_op jit(solution)/shard_map/ppermute | solution.py:22
  9.7 7.8 %collective-permute-start.5 = (bf16[48,4096]{1,0:T(8,128)(2,1)}, bf16[48,4096]{1,0:T(8,128)(2,1)S(1)}, u32[]{:S(2)}, u32[]{:S(2)}) collective-permute-start(bf16[48,4096]{1,0:T(8,128)(2,1)} %get-tuple-element.45), channel_id=1, source_target_pairs={{0,4},{4,0},{8,12},{12,8},{16,20},{20,16},{24,28},{28,24},{1,5},{5... | collective-permute-start | bytes 1179656 | tf_op jit(solution)/shard_map/ppermute | solution.py:22
  10.3 22.6 %collective-permute-start.6 = (bf16[48,4096]{1,0:T(8,128)(2,1)}, bf16[48,4096]{1,0:T(8,128)(2,1)}, u32[]{:S(2)}, u32[]{:S(2)}) collective-permute-start(bf16[48,4096]{1,0:T(8,128)(2,1)} %get-tuple-element.55), channel_id=1, source_target_pairs={{0,1},{1,0},{2,3},{3,2},{4,5},{5,4},{6,7},{7,6},{8,9},{9,8},{10,11... | collective-permute-start | bytes 1179656 | tf_op jit(solution)/shard_map/ppermute | solution.py:22
  10.9 24.5 %collective-permute-start.7 = (bf16[48,4096]{1,0:T(8,128)(2,1)}, bf16[48,4096]{1,0:T(8,128)(2,1)}, u32[]{:S(2)}, u32[]{:S(2)}) collective-permute-start(bf16[48,4096]{1,0:T(8,128)(2,1)} %get-tuple-element.56), channel_id=1, source_target_pairs={{0,2},{1,3},{2,0},{3,1},{4,6},{5,7},{6,4},{7,5},{8,10},{9,11},{10,... | collective-permute-start | bytes 1179656 | tf_op jit(solution)/shard_map/ppermute | solution.py:22
  11.2 1.9 %copy-start.1 = (bf16[192,8192]{1,0:T(8,128)(2,1)S(1)}, bf16[192,8192]{1,0:T(8,128)(2,1)}, u32[]{:S(2)}) copy-start(bf16[192,8192]{1,0:T(8,128)(2,1)} %refs_0_.1) | copy-start | bytes 9437188
  13.1 1.9 %copy-start.2 = (bf16[192,8192]{1,0:T(8,128)(2,1)S(1)}, bf16[192,8192]{1,0:T(8,128)(2,1)}, u32[]{:S(2)}) copy-start(bf16[192,8192]{1,0:T(8,128)(2,1)} %refs_1_.1) | copy-start | bytes 9437188
  29.2 11.2 %copy-start.6 = (f32[192]{0:T(256)S(1)}, f32[192]{0:T(256)}, u32[]{:S(2)}) copy-start(f32[192]{0:T(256)} %param.7) | copy-start | bytes 2308
  29.2 18.9 %collective-permute-start.11 = (bf16[96,4096]{1,0:T(8,128)(2,1)}, bf16[96,4096]{1,0:T(8,128)(2,1)}, u32[]{:S(2)}, u32[]{:S(2)}) collective-permute-start(bf16[96,4096]{1,0:T(8,128)(2,1)} %shard_map.60), channel_id=1, source_target_pairs={{0,8},{4,12},{8,0},{12,4},{16,24},{20,28},{24,16},{28,20},{1,9},{5... | collective-permute-start | bytes 2359304 | tf_op jit(solution)/shard_map/ppermute | solution.py:22
  30.8 19.9 %collective-permute-start.10 = (bf16[96,4096]{1,0:T(8,128)(2,1)}, bf16[96,4096]{1,0:T(8,128)(2,1)}, u32[]{:S(2)}, u32[]{:S(2)}) collective-permute-start(bf16[96,4096]{1,0:T(8,128)(2,1)} %collective-permute-done.refs_5_.refs_0_), channel_id=1, source_target_pairs={{0,2},{1,3},{2,0},{3,1},{4,6},{5,7},{6,4},{7,5},{8,10},{9,11},{10,... | collective-permute-start | bytes 2359304 | tf_op jit(solution)/shard_map/ppermute | solution.py:22
  32.3 18.4 %collective-permute-start.9 = (bf16[96,4096]{1,0:T(8,128)(2,1)}, bf16[96,4096]{1,0:T(8,128)(2,1)}, u32[]{:S(2)}, u32[]{:S(2)}) collective-permute-start(bf16[96,4096]{1,0:T(8,128)(2,1)} %collective-permute-done.1.refs_6_.refs_1_), channel_id=1, source_target_pairs={{0,1},{1,0},{2,3},{3,2},{4,5},{5,4},{6,7},{7,6},{8,9},{9,8},{10,11... | collective-permute-start | bytes 2359304 | tf_op jit(solution)/shard_map/ppermute | solution.py:22
  38.7 1.6 %collective-permute-start.8 = (f32[192,288]{1,0:T(8,128)S(1)}, f32[192,288]{1,0:T(8,128)S(1)}, u32[]{:S(2)}, u32[]{:S(2)}) collective-permute-start(f32[192,288]{1,0:T(8,128)S(1)} %get-tuple-element.58), channel_id=1, source_target_pairs={{0,4},{4,0},{8,12},{12,8},{16,20},{20,16},{24,28},{28,24},{1,5},{5... | collective-permute-start | bytes 663560 | tf_op jit(solution)/shard_map/ppermute | solution.py:22
  41.7 0.7 copy-start.3
  42.4 0.7 copy-start.4
  43.2 17.2 %all-to-all-start = ((bf16[32,8,580]{2,1,0:T(8,128)(2,1)}), bf16[32,8,580]{2,1,0:T(8,128)(2,1)S(1)}, u32[]{:S(2)}, u32[]{:S(2)}) async-start(bf16[32,8,580]{2,1,0:T(8,128)(2,1)} %bitcast.8), calls=%async_computation | async-start | bytes 655360 | tf_op jit(solution)/shard_map/all_to_all | solution.py:238
  50.7 4.6 %copy-start.5 = (bf16[256,576]{1,0:T(8,128)(2,1)S(1)}, bf16[256,576]{1,0:T(8,128)(2,1)}, u32[]{:S(2)}) copy-start(bf16[256,576]{1,0:T(8,128)(2,1)} %copy-done.4) | copy-start | bytes 884740
  52.7 2.5 %collective-permute-start.13 = (f32[192,192]{1,0:T(8,128)S(1)}, f32[192,192]{1,0:T(8,128)S(1)}, u32[]{:S(2)}, u32[]{:S(2)}) collective-permute-start(f32[192,192]{1,0:T(8,128)S(1)} %shard_map.63), channel_id=1, source_target_pairs={{0,4},{4,0},{8,12},{12,8},{16,20},{20,16},{24,28},{28,24},{1,5},{5... | collective-permute-start | bytes 442376 | tf_op jit(solution)/shard_map/ppermute | solution.py:22
  52.8 2.5 %collective-permute-start.12 = (f32[192,96]{1,0:T(8,128)S(1)}, f32[192,96]{1,0:T(8,128)S(1)}, u32[]{:S(2)}, u32[]{:S(2)}) collective-permute-start(f32[192,96]{1,0:T(8,128)S(1)} %get-tuple-element.71), channel_id=1, source_target_pairs={{0,4},{4,0},{8,12},{12,8},{16,20},{20,16},{24,28},{28,24},{1,5},{5... | collective-permute-start | bytes 221192 | tf_op jit(solution)/shard_map/ppermute | solution.py:22
  60.4 15.3 %all-to-all-start.1 = ((bf16[32,8,576]{2,1,0:T(8,128)(2,1)}), bf16[32,8,576]{2,1,0:T(8,128)(2,1)S(1)}, u32[]{:S(2)}, u32[]{:S(2)}) async-start(bf16[32,8,576]{2,1,0:T(8,128)(2,1)} %bitcast.4), calls=%async_computation.1 | async-start | bytes 655360 | tf_op jit(solution)/shard_map/all_to_all | solution.py:238

commit v6 on v4

v6 whole, which is shorter than its diff:
```python
import functools

import jax
import jax.numpy as jnp
from jax import lax
from jax.experimental import pallas as pl
from jax.experimental.pallas import tpu as pltpu
from jax.sharding import PartitionSpec as P

BOTH = ("ex", "pb")
NT = (((1,), (1,)), ((), ()))
LIMIT = pltpu.CompilerParams(vmem_limit_bytes=20 << 20)
LIGHT = pl.CostEstimate(flops=1, bytes_accessed=1, transcendentals=0)
HBM = pl.BlockSpec(memory_space=pltpu.HBM)
VMEM = pl.BlockSpec(memory_space=pltpu.VMEM)


def moved(value, target):
    ex, pb = lax.axis_size("ex"), lax.axis_size("pb")
    place = lambda e, p: e * pb + p
    return lax.ppermute(value, BOTH, [(place(e, p), place(*target(e, p))) for e in range(ex) for p in range(pb)])


def one_hot(hits):
    return jnp.where(hits, 1.0, 0.0).astype(jnp.bfloat16)


def pick(select, values):
    return jnp.dot(select, values, preferred_element_type=jnp.float32)


def scores_kernel(groups, count, *refs):
    held = sum(groups)
    rows, pieces, outs = refs[:held], refs[held : held + count], refs[held + count :]
    stack = lambda arrays: arrays[0][...] if len(arrays) == 1 else jnp.concatenate([a[...] for a in arrays], axis=0)
    total = lax.dot_general(stack(rows), stack(pieces), NT, preferred_element_type=jnp.float32)
    at = 0
    for out in outs:
        part = total[at : at + out.shape[0]]
        at += out.shape[0]

        @pl.when(pl.program_id(0) == 0)
        def _():
            out[...] = part

        @pl.when(pl.program_id(0) > 0)
        def _():
            out[...] += part


def scored(groups, pieces):
    width, deep = sum(piece.shape[0] for piece in pieces), pieces[0].shape[1]
    arrays = [rows for group in groups for rows in group]
    shapes = [jax.ShapeDtypeStruct((sum(rows.shape[0] for rows in group), width), jnp.float32) for group in groups]
    steps = 2
    chunk = lambda array: pl.BlockSpec((array.shape[0], deep // steps), lambda k: (0, k))
    return pl.pallas_call(
        functools.partial(scores_kernel, [len(group) for group in groups], len(pieces)),
        grid=(steps,),
        in_specs=[chunk(array) for array in [*arrays, *pieces]],
        out_specs=[pl.BlockSpec(shape.shape, lambda k: (0, 0)) for shape in shapes],
        out_shape=shapes,
        compiler_params=LIMIT,
        cost_estimate=LIGHT,
    )(*arrays, *pieces)


def copied(query, count):
    depth = query.shape[1]
    parts = 4
    height = count // parts

    def body(query_ref, out_ref, held, sems):
        mine = (lax.axis_index("ex") // 2 + lax.axis_index("ex")) % 2
        start = mine * (query_ref.shape[0] // 2)
        spans = [pl.ds(part * height, height) for part in range(parts)]
        source = lambda part: query_ref.at[pl.ds(pl.multiple_of(start + part * height, 16), height)]
        arriving = [pltpu.make_async_copy(source(i), held.at[spans[i]], sems.at[i]) for i in range(parts)]
        leaving = [pltpu.make_async_copy(held.at[spans[i]], out_ref.at[spans[i]], sems.at[parts + i]) for i in range(parts)]
        for copy in arriving:
            copy.start()
        for first, second in zip(arriving, leaving):
            first.wait()
            second.start()
        for copy in leaving:
            copy.wait()

    return pl.pallas_call(
        body,
        in_specs=[HBM],
        out_specs=HBM,
        out_shape=jax.ShapeDtypeStruct((count, depth), query.dtype),
        scratch_shapes=[pltpu.VMEM((count, depth), query.dtype), pltpu.SemaphoreType.DMA((2 * parts,))],
        compiler_params=pltpu.CompilerParams(vmem_limit_bytes=60 << 20),
        cost_estimate=LIGHT,
    )(query)


class Slots:
    def __init__(self, capacity, width, ids):
        self.width = width
        self.full, rest = capacity // 8, capacity % 8
        if rest > 4:
            self.full, rest = self.full + 1, 0
        self.half = width // 2 if rest else 0
        self.groups = self.full + (1 if rest else 0)
        self.at = self.full * width
        self.ids = self.at + self.half
        self.lanes = self.ids + (2 * self.groups if ids else 0)


def ordered(slots, scores, spans):
    column = jnp.concatenate(
        [
            jnp.full((count, 1), -1, jnp.int32)
            if base is None
            else lax.broadcasted_iota(jnp.int32, (count, 1), 0) + base
            for base, count in spans
        ],
        axis=0,
    )
    place = lax.broadcasted_iota(jnp.int32, (column.shape[0], slots.width), 1)
    return pick(scores, one_hot(place == column))


def upright(row):
    count = row.shape[1]
    diagonal = lax.broadcasted_iota(jnp.int32, (count, count), 0) == lax.broadcasted_iota(jnp.int32, (count, count), 1)
    return jnp.sum(jnp.where(diagonal, row, jnp.zeros_like(row)), axis=1, keepdims=True)


def flat(column):
    count = column.shape[0]
    diagonal = lax.broadcasted_iota(jnp.int32, (count, count), 0) == lax.broadcasted_iota(jnp.int32, (count, count), 1)
    return jnp.sum(jnp.where(diagonal, column, jnp.zeros_like(column)), axis=0, keepdims=True)


def packing(body, shape, residual, placed, *operands):
    rows = residual.shape[0]

    def kernel(scale_ref, row_ref, *refs):
        *refs, scale, row, sems = refs
        copies = [pltpu.make_async_copy(scale_ref, scale, sems.at[0]), pltpu.make_async_copy(row_ref, row, sems.at[1])]
        for copy in copies:
            copy.start()
        for copy in copies:
            copy.wait()
        body(scale[...], row[...], *refs)

    return pl.pallas_call(
        kernel,
        in_specs=[HBM] * 2 + [VMEM] * len(operands),
        out_shape=shape,
        scratch_shapes=[
            pltpu.VMEM((1, rows), residual.dtype),
            pltpu.VMEM((1, rows), placed.dtype),
            pltpu.SemaphoreType.DMA((2,)),
        ],
        compiler_params=LIMIT,
        cost_estimate=LIGHT,
    )(residual[None, :], placed[None, :], *operands)


def weighted(own, got, scale):
    return ((own[...] if got is None else own[...] + got[...]) * upright(scale)).astype(jnp.bfloat16)


def selects(slots, table_rows, height, placed):
    rows = placed.shape[1]
    goal = placed // table_rows
    same = upright(goal) == goal
    before = lax.broadcasted_iota(jnp.int32, (rows, 1), 0) < lax.broadcasted_iota(jnp.int32, (1, rows), 1)
    rank = jnp.sum(jnp.where(same & before, 1, 0), axis=0, keepdims=True)
    targets = [jnp.where(rank // 8 == index, goal * 8 + rank % 8, -1) for index in range(slots.full)]
    if slots.half:
        late = rank - slots.full * 8
        sides = [jnp.where(late >= 0, goal * 8 + side * 4 + late, -1) for side in range(2)]
        targets.append(jnp.concatenate(sides, axis=1))
    row = lambda target: lax.broadcasted_iota(jnp.int32, (height, target.shape[1]), 0)
    return [one_hot(row(target) == target) for target in targets]


def digits(slots, table_rows, placed):
    number = upright(placed % table_rows + 1)
    lane = lax.broadcasted_iota(jnp.int32, (number.shape[0], 2 * slots.groups), 1)
    digit = jnp.where(lane % 2 == 0, number // 128, number % 128)
    kept = [jnp.where(lane // 2 == index, digit, 0) for index in range(slots.groups)]
    return [value.astype(jnp.float32).astype(jnp.bfloat16) for value in kept]


def put(slots, found, table, out_ref, ids=None, base_ref=None):
    table = table.astype(jnp.bfloat16)

    def write(start, values):
        values, span = values.astype(jnp.bfloat16), slice(start, start + values.shape[1])
        out_ref[:, span] = values if base_ref is None else values + base_ref[:, span]

    for index in range(slots.full):
        write(index * slots.width, pick(found[index], table))
    stacked_halves = lambda left, right: jnp.concatenate([left, right], axis=0)
    if slots.half:
        write(slots.at, pick(found[slots.full], stacked_halves(table[:, : slots.half], table[:, slots.half :])))
    if ids is not None:
        digit = [ids[index] if index < slots.full else stacked_halves(ids[index], ids[index]) for index in range(len(found))]
        write(slots.ids, sum(pick(select, values) for select, values in zip(found, digit)))


def called(body, shapes, *operands):
    return pl.pallas_call(body, out_shape=shapes, compiler_params=LIMIT, cost_estimate=LIGHT)(*operands)


def exchanged(rows, devices):
    apart = rows.reshape(devices, 8, rows.shape[1])
    return lax.all_to_all(apart, BOTH, split_axis=0, concat_axis=0).reshape(rows.shape)


def halves(slots, pb, count):
    peer = lax.broadcasted_iota(jnp.int32, (count, 1), 0) // 8
    unit = lax.broadcasted_iota(jnp.int32, (1, slots.width), 1) // (slots.width // 4)
    y, x, layer = peer // 2 % 2, peer % 2, peer // pb // 2 % 2
    apart = (unit // 2 != (x + y) % 2) & (unit % 2 != layer)
    return (y == 0) != apart


def added(slots, totals, hot, ref, index, lower):
    if index < slots.full:
        values = ref[:, index * slots.width : (index + 1) * slots.width]
    else:
        half = ref[:, slots.at : slots.at + slots.half]
        row = lax.broadcasted_iota(jnp.int32, (half.shape[0], 1), 0)
        lane = lax.broadcasted_iota(jnp.int32, (1, slots.width), 1)
        values = jnp.where((row % 8 < 4) == (lane < slots.half), jnp.concatenate([half, half], axis=1), 0)
    values = [values] if lower is None else [jnp.where(lower, values, 0), jnp.where(lower, 0, values)]
    parts = [pick(hot, v) for v in values]
    return parts if totals is None else [t + p for t, p in zip(totals, parts)]


def first_table_kernel(slots, pb, table_rows, split, got_ref, out_ref, hot_ref=None):
    count = got_ref.shape[0]
    lower = halves(slots, pb, count) if split else None
    entry = lax.broadcasted_iota(jnp.int32, (table_rows, count), 0)
    totals = None
    for index in range(slots.groups):
        at = slots.ids + 2 * index
        number = got_ref[:, at : at + 2].astype(jnp.float32)
        hot = one_hot(entry == flat(number[:, 0:1] * 128.0 + number[:, 1:2]).astype(jnp.int32) - 1)
        if hot_ref is not None:
            hot_ref[index] = hot
        totals = added(slots, totals, hot, got_ref, index, lower)
    for side, total in enumerate(totals):
        out_ref[:, side * slots.width : (side + 1) * slots.width] = total


def last_table_kernel(slots, pb, first_ref, hot_ref, got_ref, out_ref):
    width, half = slots.width, slots.width // 2
    upper = jnp.logical_not(halves(slots, pb, got_ref.shape[0]))
    totals = None
    for index in range(slots.groups):
        totals = added(slots, totals, hot_ref[index], got_ref, index, upper)
    out_ref[:, :width] = first_ref[:, :width] + totals[0]
    above = first_ref[:, width:] + totals[1]
    out_ref[:, width : width + half] = above[:, half:]
    out_ref[:, width + half :] = above[:, :half]


def on_device(train, query, residual, example_source, source_place):
    rows, depth = train.shape
    block = query.shape[0]
    ex, pb = lax.axis_size("ex"), lax.axis_size("pb")
    me_ex, me_pb = lax.axis_index("ex"), lax.axis_index("pb")
    devices = ex * pb
    table_rows = source_place.shape[0] // devices
    capacity = max(1, -(-2 * rows // devices))
    core, layer = me_ex % 2, (me_ex // 2) % 2
    on_core = lambda e, p: (e ^ 1, p)
    on_z = lambda e, p: (e ^ 2, p)
    near = lambda e, p: (e, p ^ (1 + e % 2))
    across = lambda e, p: (e, p ^ (2 - e % 2))
    whole = jax.ShapeDtypeStruct((table_rows, block * pb), jnp.float32)

    placed = jnp.take(source_place, example_source)
    packed_rows = lambda slots: jax.ShapeDtypeStruct((devices * 8, slots.lanes), jnp.bfloat16)

    if pb != 4 or ex % 4 != 0:
        deep = depth // 2
        other = moved(lax.dynamic_slice(train, (0, (1 - core) * deep), (rows, deep)), on_core)
        own = lax.dynamic_slice(train, (0, core * deep), (rows, deep))
        queries = lax.all_gather(lax.dynamic_slice(query, (0, core * deep), (block, deep)), "pb", tiled=True)
        slots = Slots(capacity, block * pb, True)
        own, other = scored([[own], [other]], [queries])

        def pack(scale, row, own_ref, got_ref, out_ref):
            found = selects(slots, table_rows, devices * 8, row)
            put(slots, found, weighted(own_ref, got_ref, scale), out_ref, digits(slots, table_rows, row))

        got = exchanged(packing(pack, packed_rows(slots), residual, placed, own, moved(other, on_core)), devices)
        return called(functools.partial(first_table_kernel, slots, pb, table_rows, False), whole, got)

    half = block // 2
    head = half * 2 // 3
    lent = head
    ends = half - lent
    mine = (layer + core) % 2
    cut = lambda start, count: lax.dynamic_slice(query, (start, 0), (count, depth))
    one = moved(copied(query, head), near)
    tail = moved(cut(mine * half + head, half - head), near)
    rest = moved(cut((1 - mine) * half + lent, ends), near)
    other = moved(train, on_core)

    early, late = Slots(capacity, 2 * block, True), Slots(capacity, 2 * block, False)

    def units():
        me = lax.axis_index("pb")
        same = (me % 2 + me // 2) % 2
        unit = lambda near, part: (2 * (same if near else 1 - same) + part) * half
        return unit, (lax.axis_index("ex") // 2 + lax.axis_index("ex")) % 2

    def first_pack(scale, row, home_ref, own_ref, got_ref, out_ref):
        unit, part = units()
        found = selects(early, table_rows, devices * 8, row)
        own, got = weighted(own_ref, None, scale), weighted(got_ref, None, scale)
        table = ordered(early, weighted(home_ref, None, scale), [(unit(True, 0), block)])
        table += ordered(early, own, [(unit(False, part), half)])
        table += ordered(early, got, [(unit(False, 1 - part), half)])
        put(early, found, table, out_ref, digits(early, table_rows, row))

    def last_pack(scale, row, own_ref, got_ref, out_ref):
        unit, part = units()
        found = selects(late, table_rows, devices * 8, row)

        def spans(side):
            across, beside = unit(True, side), unit(False, 1 - side)
            return [(beside, lent), (across, head), (across + head, half - head), (beside + lent, ends)]

        table = ordered(late, weighted(own_ref, None, scale), spans(part))
        table += ordered(late, weighted(got_ref, None, scale), spans(1 - part))
        put(late, found, table, out_ref)

    (scores_own,) = scored([[train]], [query])
    one, other, scores_own, placed = lax.optimization_barrier((one, other, scores_own, placed))
    z_lent = moved(one, on_z)
    two = moved(one, across)
    two_tail = moved(tail, across)

    own_a, other_a = scored([[train], [other]], [one, tail])
    got_a = moved(other_a, on_core)
    rows_a = packing(first_pack, packed_rows(early), residual, placed, scores_own, own_a, got_a)
    train, other, rows_a = lax.optimization_barrier((train, other, rows_a))
    sent_a = exchanged(rows_a, devices)

    pieces = [z_lent, two, two_tail, rest]
    own_b, other_b = scored([[train], [other]], pieces)
    got_b = moved(other_b, on_core)
    rows_b = packing(last_pack, packed_rows(late), residual, placed, own_b, got_b)
    sent_b = exchanged(rows_b, devices)

    hot = jax.ShapeDtypeStruct((early.groups, table_rows, devices * 8), jnp.bfloat16)
    table, hot = called(functools.partial(first_table_kernel, early, pb, table_rows, True), [whole, hot], sent_a)
    return called(functools.partial(last_table_kernel, late, pb), whole, table, hot, sent_b)


def solution(mesh):
    return jax.shard_map(
        on_device,
        mesh=mesh,
        in_specs=(P(BOTH, None), P("pb", None), P(BOTH), P(BOTH), P()),
        out_specs=P(BOTH, None),
        check_vma=False,
    )
```

time: 78.6 us -> 76.9 us (0.978)
  starting transfers between devices: 18.1 us -> 24 us
  waiting for transfers between devices: 34.2 us -> 29.3 us
  Pallas kernels: 20.9 us -> 16.7 us
  local copies, waits for them, and re-layouts: 4.84 us -> 6.35 us
    all_to_all x2, starting transfers between devices: 8.37 us -> 13 us  [exchanged(): lax.all_to_all(apart, BOTH, split_axis=0, concat_axis=0).reshape(rows.shape)]
    pallas_call x2 -> x1, Pallas kernels: 5.6 us -> 2.24 us  [copied(): pl.pallas_call(body, in_specs=[HBM], out_specs=HBM, out_shape=jax.ShapeDt...]
    all_to_all x2, waiting for transfers between devices: 14.5 us -> 11.4 us  [exchanged(): lax.all_to_all(apart, BOTH, split_axis=0, concat_axis=0).reshape(rows.shape)]
    ppermute x13 -> x9, waiting for transfers between devices: 19.7 us -> 18 us  [moved(): lax.ppermute(value, BOTH, [(place(e, p), place(*target(e, p))) for e in r...]
    ppermute x13 -> x9, starting transfers between devices: 9.72 us -> 11.1 us  [moved(): lax.ppermute(value, BOTH, [(place(e, p), place(*target(e, p))) for e in r...]
    dynamic_slice x1, local copies, waits for them, and re-layouts: 1.29 us -> 2.23 us  [on_device(): lax.dynamic_slice(query, (start, 0), (count, depth))]
    unnamed x18 -> x12, local copies, waits for them, and re-layouts: 2.11 us -> 2.68 us
    pallas_call x4 -> x3, Pallas kernels: 9.75 us -> 9.38 us  [scored(): pl.pallas_call(functools.partial(scores_kernel, [len(group) for group in...]
  transfers between devices with their start and end apart: 15 -> 11, of which waited for: 8 -> 6; matrix products, arithmetic and copies ran while one was open for 4% -> 5% of each run, Pallas kernels for 20% -> 19%
where the time goes in v6:
time: 76.9 us; the launch traced here: 76.6 us
  waiting for transfers between devices  29.3 us (38%)
  starting transfers between devices  24 us (31%)
  Pallas kernels  16.7 us (22%)
  local copies, waits for them, and re-layouts  6.35 us (8%)
    ppermute x9, waiting for transfers between devices, moved(): lax.ppermute(value, BOTH, [(place(e, p), place(*target(e, p))) for e in r...  18 us
    all_to_all x2, starting transfers between devices, exchanged(): lax.all_to_all(apart, BOTH, split_axis=0, concat_axis=0).reshape(rows.shape)  13 us
    all_to_all x2, waiting for transfers between devices, exchanged(): lax.all_to_all(apart, BOTH, split_axis=0, concat_axis=0).reshape(rows.shape)  11.4 us
    ppermute x9, starting transfers between devices, moved(): lax.ppermute(value, BOTH, [(place(e, p), place(*target(e, p))) for e in r...  11.1 us
    pallas_call x3, Pallas kernels, scored(): pl.pallas_call(functools.partial(scores_kernel, [len(group) for group in...  9.38 us
    unnamed x12, local copies, waits for them, and re-layouts  2.68 us
    pallas_call x2, Pallas kernels, called(): pl.pallas_call(body, out_shape=shapes, compiler_params=LIMIT, cost_estima...  2.68 us
    pallas_call x2, Pallas kernels, packing(): pl.pallas_call(kernel, in_specs=[HBM] * 2 + [VMEM] * len(operands), out_s...  2.4 us
  transfers between devices with their start and end apart: 11, of which 6 were waited for; matrix products, arithmetic and copies ran while one was open for 5% of the time, Pallas kernels for 19%

profile of v6, /device:TPU:0, one launch (start us, length us, event | category | flops | bytes accessed | tf_op | source)
XLA Modules:
  0.0 76.6 jit_solution(2405223484833488860)
XLA Ops:
  0.0 0.0 copy-start
  0.0 0.0 copy-start.1
  0.0 0.5 collective-permute-start.1
  0.5 2.2 %shard_map.55 = bf16[64,8192]{1,0:T(8,128)(2,1)} custom-call(bf16[192,8192]{1,0:T(8,128)(2,1)} %refs_1_.1), custom_call_target="tpu_custom_call" | custom-call | flops 1 | bytes 1 | tf_op jit(solution)/shard_map/pallas_call | solution.py:88
  2.7 2.5 %collective-permute-start = (bf16[64,8192]{1,0:T(8,128)(2,1)}, bf16[64,8192]{1,0:T(8,128)(2,1)}, u32[]{:S(2)}, u32[]{:S(2)}) collective-permute-start(bf16[64,8192]{1,0:T(8,128)(2,1)} %shard_map.55), channel_id=1, source_target_pairs={{0,1},{1,0},{2,3},{3,2},{4,6},{5,7},{6,4},{7,5},{8,9},{9,8},{10,11... | collective-permute-start | bytes 3145736 | tf_op jit(solution)/shard_map/ppermute | solution.py:21
  5.2 2.2 %constant_dynamic-slice_fusion = (bf16[32,8192]{1,0:T(8,128)(2,1)}, bf16[32,8192]{1,0:T(8,128)(2,1)}) fusion(bf16[192,8192]{1,0:T(8,128)(2,1)} %refs_1_.1, s32[]{:T(128)S(6)} %select_n.41, s32[]{:T(128)S(6)} %select_n.40), kind=kLoop, calls=%fused_computation.4 | loop fusion | bytes 2097160 | tf_op jit(solution)/shard_map/dynamic_slice | solution.py:304
  7.4 0.1 collective-permute-start.2
  7.5 0.0 copy-done.1
  7.5 0.0 copy-start.2
  7.5 1.9 %copy-done.2 = bf16[192,8192]{1,0:T(8,128)(2,1)S(1)} copy-done((bf16[192,8192]{1,0:T(8,128)(2,1)S(1)}, bf16[192,8192]{1,0:T(8,128)(2,1)}, u32[]{:S(2)}) %copy-start.2) | copy-done | bytes 3145752
  9.4 0.0 copy-start.5
  9.4 1.7 %shard_map.56.refs_0_ = f32[192,192]{1,0:T(8,128)S(1)} custom-call(bf16[192,8192]{1,0:T(8,128)(2,1)S(1)} %copy-done.1, bf16[192,8192]{1,0:T(8,128)(2,1)S(1)} %copy-done.2), custom_call_target="tpu_custom_call" | custom-call | flops 1 | bytes 1 | tf_op jit(solution)/shard_map/pallas_call | solution.py:57
  11.1 0.0 copy-done.5
  11.1 0.0 copy-done
  11.1 1.4 %gather_fusion = s32[192]{0:T(256)S(1)} fusion(s32[8192]{0:T(1024)S(1)} %copy-done, s32[1024]{0:T(1024)S(1)} %pad_clamp_fusion), kind=kCustom, calls=%fused_computation | custom fusion | bytes 2304 | tf_op jit(solution)/shard_map/jit(_take)/gather | solution.py:281
  12.6 5.7 %collective-permute-done.refs_2_ = bf16[64,8192]{1,0:T(8,128)(2,1)} collective-permute-done((bf16[64,8192]{1,0:T(8,128)(2,1)}, bf16[64,8192]{1,0:T(8,128)(2,1)}, u32[]{:S(2)}, u32[]{:S(2)}) %collective-permute-start) | collective-permute-done | bytes 1048608 | tf_op jit(solution)/shard_map/ppermute | solution.py:21
  18.3 0.0 collective-permute-done.1.refs_1_
  18.3 2.1 %collective-permute-start.4 = (bf16[64,8192]{1,0:T(8,128)(2,1)}, bf16[64,8192]{1,0:T(8,128)(2,1)}, u32[]{:S(2)}, u32[]{:S(2)}) collective-permute-start(bf16[64,8192]{1,0:T(8,128)(2,1)} %collective-permute-done.refs_2_), channel_id=1, source_target_pairs={{0,8},{1,9},{2,10},{3,11},{4,12},{5,13},{6,14},{7,15},{8,0},{9,1},... | collective-permute-start | bytes 3145736 | tf_op jit(solution)/shard_map/ppermute | solution.py:21
  20.4 1.5 %collective-permute-start.5 = (bf16[64,8192]{1,0:T(8,128)(2,1)}, bf16[64,8192]{1,0:T(8,128)(2,1)}, u32[]{:S(2)}, u32[]{:S(2)}) collective-permute-start(bf16[64,8192]{1,0:T(8,128)(2,1)} %collective-permute-done.refs_2_), channel_id=1, source_target_pairs={{0,2},{1,3},{2,0},{3,1},{4,5},{5,4},{6,7},{7,6},{8,10},{9,11},{10,... | collective-permute-start | bytes 3145736 | tf_op jit(solution)/shard_map/ppermute | solution.py:21
  21.9 0.0 copy-start.4
  21.9 1.5 %collective-permute-start.7 = (bf16[32,8192]{1,0:T(8,128)(2,1)}, bf16[32,8192]{1,0:T(8,128)(2,1)}, u32[]{:S(2)}, u32[]{:S(2)}) collective-permute-start(bf16[32,8192]{1,0:T(8,128)(2,1)} %get-tuple-element.31), channel_id=1, source_target_pairs={{0,1},{1,0},{2,3},{3,2},{4,6},{5,7},{6,4},{7,5},{8,9},{9,8},{10,11... | collective-permute-start | bytes 1572872 | tf_op jit(solution)/shard_map/ppermute | solution.py:21
  23.4 1.6 %collective-permute-done.2.refs_3_ = bf16[32,8192]{1,0:T(8,128)(2,1)} collective-permute-done((bf16[32,8192]{1,0:T(8,128)(2,1)}, bf16[32,8192]{1,0:T(8,128)(2,1)}, u32[]{:S(2)}, u32[]{:S(2)}) %collective-permute-start.2) | collective-permute-done | bytes 524320 | tf_op jit(solution)/shard_map/ppermute | solution.py:21
  25.1 2.5 %collective-permute-start.6 = (bf16[32,8192]{1,0:T(8,128)(2,1)}, bf16[32,8192]{1,0:T(8,128)(2,1)}, u32[]{:S(2)}, u32[]{:S(2)}) collective-permute-start(bf16[32,8192]{1,0:T(8,128)(2,1)} %collective-permute-done.2.refs_3_), channel_id=1, source_target_pairs={{0,2},{1,3},{2,0},{3,1},{4,5},{5,4},{6,7},{7,6},{8,10},{9,11},{10,... | collective-permute-start | bytes 1572872 | tf_op jit(solution)/shard_map/ppermute | solution.py:21
  27.6 3.7 %shard_map.57 = (f32[192,96]{1,0:T(8,128)S(1)}, f32[192,96]{1,0:T(8,128)S(1)}) custom-call(bf16[192,8192]{1,0:T(8,128)(2,1)S(1)} %copy-done.1, bf16[192,8192]{1,0:T(8,128)(2,1)} %collective-permute-done.1.refs_1_, bf16[64,8192]{1,0:T(8,128)(2,1)} %collective-permute-done.refs_2_, bf16[32,8192]{1,0:T(8,128)(2,1)} %collective-permute-done.2.refs_3_), custom_call_target="tpu_custom_call" | custom-call | flops 1 | bytes 1 | tf_op jit(solution)/shard_map/pallas_call | solution.py:57
  31.3 0.1 collective-permute-start.3
  31.3 1.3 %collective-permute-done.3.refs_2_ = f32[192,96]{1,0:T(8,128)S(1)} collective-permute-done((f32[192,96]{1,0:T(8,128)S(1)}, f32[192,96]{1,0:T(8,128)S(1)}, u32[]{:S(2)}, u32[]{:S(2)}) %collective-permute-start.3) | collective-permute-done | bytes 73760 | tf_op jit(solution)/shard_map/ppermute | solution.py:21
  32.6 0.0 copy-done.4
  32.6 1.0 %shard_map.58 = bf16[256,580]{1,0:T(8,128)(2,1)S(1)} custom-call(f32[1,192]{1,0:T(1,128)S(1)} %bitcast.11, s32[1,192]{1,0:T(1,128)S(1)} %bitcast.9, f32[192,192]{1,0:T(8,128)S(1)} %shard_map.56.refs_0_, f32[192,96]{1,0:T(8,128)S(1)} %get-tuple-element.22.refs_1_, f32[192,96]{1,0:T(8,128)S(1)} %collective-permute-done.3.refs_2_), custom_call_target="tpu_custom_call" | custom-call | flops 1 | bytes 1 | tf_op jit(solution)/shard_map/pallas_call | solution.py:150
  33.6 0.0 copy-start.3
  33.6 0.8 %copy-done.3 = bf16[256,580]{1,0:T(8,128)(2,1)} copy-done((bf16[256,580]{1,0:T(8,128)(2,1)}, bf16[256,580]{1,0:T(8,128)(2,1)S(1)}, u32[]{:S(2)}) %copy-start.3) | copy-done | bytes 296984
  34.4 6.0 %all-to-all-start = ((bf16[32,8,580]{2,1,0:T(8,128)(2,1)}), bf16[32,8,580]{2,1,0:T(8,128)(2,1)S(1)}, u32[]{:S(2)}, u32[]{:S(2)}) async-start(bf16[32,8,580]{2,1,0:T(8,128)(2,1)} %bitcast.7), calls=%async_computation | async-start | bytes 655360 | tf_op jit(solution)/shard_map/all_to_all | solution.py:214
  40.4 0.0 collective-permute-done.7.refs_5_
  40.4 8.1 %collective-permute-done.6.refs_4_ = bf16[32,8192]{1,0:T(8,128)(2,1)} collective-permute-done((bf16[32,8192]{1,0:T(8,128)(2,1)}, bf16[32,8192]{1,0:T(8,128)(2,1)}, u32[]{:S(2)}, u32[]{:S(2)}) %collective-permute-start.6) | collective-permute-done | bytes 524320 | tf_op jit(solution)/shard_map/ppermute | solution.py:21
  48.6 0.0 collective-permute-done.4.refs_2_
  48.6 0.0 collective-permute-done.5.refs_3_
  48.6 4.0 %shard_map.60 = (f32[192,192]{1,0:T(8,128)S(1)}, f32[192,192]{1,0:T(8,128)S(1)}) custom-call(bf16[192,8192]{1,0:T(8,128)(2,1)S(1)} %copy-done.1, bf16[192,8192]{1,0:T(8,128)(2,1)} %collective-permute-done.1.refs_1_, bf16[64,8192]{1,0:T(8,128)(2,1)} %collective-permute-done.4.refs_2_, bf16[64,8192]{1,0:T(8,128)(2,1)} %collective-permute-done.5.refs_3_, ...), custom_call_target="tpu_custom_call" | custom-call | flops 1 | bytes 1 | tf_op jit(solution)/shard_map/pallas_call | solution.py:57
  52.6 0.3 collective-permute-start.8
  52.9 1.2 %collective-permute-done.8.refs_1_ = f32[192,192]{1,0:T(8,128)S(1)} collective-permute-done((f32[192,192]{1,0:T(8,128)S(1)}, f32[192,192]{1,0:T(8,128)S(1)}, u32[]{:S(2)}, u32[]{:S(2)}) %collective-permute-start.8) | collective-permute-done | bytes 147488 | tf_op jit(solution)/shard_map/ppermute | solution.py:21
  54.1 1.4 %shard_map.61 = bf16[256,576]{1,0:T(8,128)(2,1)} custom-call(f32[1,192]{1,0:T(1,128)S(1)} %bitcast.12, s32[1,192]{1,0:T(1,128)S(1)} %bitcast.10, f32[192,192]{1,0:T(8,128)S(1)} %get-tuple-element.29.refs_0_, f32[192,192]{1,0:T(8,128)S(1)} %collective-permute-done.8.refs_1_), custom_call_target="tpu_custom_call" | custom-call | flops 1 | bytes 1 | tf_op jit(solution)/shard_map/pallas_call | solution.py:150
  55.6 0.0 all-to-all-done
  55.6 6.9 %all-to-all-start.1 = ((bf16[32,8,576]{2,1,0:T(8,128)(2,1)}), bf16[32,8,576]{2,1,0:T(8,128)(2,1)S(1)}, u32[]{:S(2)}, u32[]{:S(2)}) async-start(bf16[32,8,576]{2,1,0:T(8,128)(2,1)} %bitcast.4), calls=%async_computation.1 | async-start | bytes 655360 | tf_op jit(solution)/shard_map/all_to_all | solution.py:214
  62.5 0.9 %shard_map.59 = (f32[256,768]{1,0:T(8,128)S(1)}, bf16[2,256,256]{2,1,0:T(8,128)(2,1)S(1)}) custom-call(bf16[256,580]{1,0:T(8,128)(2,1)S(1)} %bitcast.6), custom_call_target="tpu_custom_call" | custom-call | flops 1 | bytes 1 | tf_op jit(solution)/shard_map/pallas_call | solution.py:209
  63.4 11.4 %all-to-all-done.1 = bf16[32,8,576]{2,1,0:T(8,128)(2,1)S(1)} async-done(((bf16[32,8,576]{2,1,0:T(8,128)(2,1)}), bf16[32,8,576]{2,1,0:T(8,128)(2,1)S(1)}, u32[]{:S(2)}, u32[]{:S(2)}) %all-to-all-start.1) | async-done | bytes 294944 | tf_op jit(solution)/shard_map/all_to_all | solution.py:214
  74.8 1.8 %shard_map.62 = f32[256,768]{1,0:T(8,128)} custom-call(f32[256,768]{1,0:T(8,128)S(1)} %get-tuple-element.25.first_ref, bf16[2,256,256]{2,1,0:T(8,128)(2,1)S(1)} %get-tuple-element.26.hot_ref, bf16[256,576]{1,0:T(8,128)(2,1)S(1)} %bitcast.8), custom_call_target="tpu_custom_call" | custom-call | flops 1 | bytes 1 | tf_op jit(solution)/shard_map/pallas_call | solution.py:209
  (3 shorter events, 0.0 us)
Async XLA Ops:
  0.0 11.1 %copy-start = (s32[8192]{0:T(1024)S(1)}, s32[8192]{0:T(1024)}, u32[]{:S(2)}) copy-start(s32[8192]{0:T(1024)} %param.9) | copy-start | bytes 98308
  0.0 7.5 %copy-start.1 = (bf16[192,8192]{1,0:T(8,128)(2,1)S(1)}, bf16[192,8192]{1,0:T(8,128)(2,1)}, u32[]{:S(2)}) copy-start(bf16[192,8192]{1,0:T(8,128)(2,1)} %refs_0_.4) | copy-start | bytes 9437188
  0.0 18.3 %collective-permute-start.1 = (bf16[192,8192]{1,0:T(8,128)(2,1)}, bf16[192,8192]{1,0:T(8,128)(2,1)}, u32[]{:S(2)}, u32[]{:S(2)}) collective-permute-start(bf16[192,8192]{1,0:T(8,128)(2,1)} %refs_0_.4), channel_id=1, source_target_pairs={{0,4},{1,5},{2,6},{3,7},{4,0},{5,1},{6,2},{7,3},{8,12},{9,13},{10,... | collective-permute-start | bytes 9437192 | tf_op jit(solution)/shard_map/ppermute | solution.py:21
  2.7 15.6 %collective-permute-start = (bf16[64,8192]{1,0:T(8,128)(2,1)}, bf16[64,8192]{1,0:T(8,128)(2,1)}, u32[]{:S(2)}, u32[]{:S(2)}) collective-permute-start(bf16[64,8192]{1,0:T(8,128)(2,1)} %shard_map.55), channel_id=1, source_target_pairs={{0,1},{1,0},{2,3},{3,2},{4,6},{5,7},{6,4},{7,5},{8,9},{9,8},{10,11... | collective-permute-start | bytes 3145736 | tf_op jit(solution)/shard_map/ppermute | solution.py:21
  7.4 17.6 %collective-permute-start.2 = (bf16[32,8192]{1,0:T(8,128)(2,1)}, bf16[32,8192]{1,0:T(8,128)(2,1)}, u32[]{:S(2)}, u32[]{:S(2)}) collective-permute-start(bf16[32,8192]{1,0:T(8,128)(2,1)} %get-tuple-element.32), channel_id=1, source_target_pairs={{0,1},{1,0},{2,3},{3,2},{4,6},{5,7},{6,4},{7,5},{8,9},{9,8},{10,11... | collective-permute-start | bytes 1572872 | tf_op jit(solution)/shard_map/ppermute | solution.py:21
  7.5 1.9 %copy-start.2 = (bf16[192,8192]{1,0:T(8,128)(2,1)S(1)}, bf16[192,8192]{1,0:T(8,128)(2,1)}, u32[]{:S(2)}) copy-start(bf16[192,8192]{1,0:T(8,128)(2,1)} %refs_1_.1) | copy-start | bytes 9437188
  9.4 1.7 %copy-start.5 = (s32[192]{0:T(256)S(1)}, s32[192]{0:T(256)}, u32[]{:S(2)}) copy-start(s32[192]{0:T(256)} %param.8) | copy-start | bytes 2308
  18.3 30.2 %collective-permute-start.4 = (bf16[64,8192]{1,0:T(8,128)(2,1)}, bf16[64,8192]{1,0:T(8,128)(2,1)}, u32[]{:S(2)}, u32[]{:S(2)}) collective-permute-start(bf16[64,8192]{1,0:T(8,128)(2,1)} %collective-permute-done.refs_2_), channel_id=1, source_target_pairs={{0,8},{1,9},{2,10},{3,11},{4,12},{5,13},{6,14},{7,15},{8,0},{9,1},... | collective-permute-start | bytes 3145736 | tf_op jit(solution)/shard_map/ppermute | solution.py:21
  20.4 28.1 %collective-permute-start.5 = (bf16[64,8192]{1,0:T(8,128)(2,1)}, bf16[64,8192]{1,0:T(8,128)(2,1)}, u32[]{:S(2)}, u32[]{:S(2)}) collective-permute-start(bf16[64,8192]{1,0:T(8,128)(2,1)} %collective-permute-done.refs_2_), channel_id=1, source_target_pairs={{0,2},{1,3},{2,0},{3,1},{4,5},{5,4},{6,7},{7,6},{8,10},{9,11},{10,... | collective-permute-start | bytes 3145736 | tf_op jit(solution)/shard_map/ppermute | solution.py:21
  21.9 10.7 %copy-start.4 = (f32[192]{0:T(256)S(1)}, f32[192]{0:T(256)}, u32[]{:S(2)}) copy-start(f32[192]{0:T(256)} %param.7) | copy-start | bytes 2308
  21.9 18.5 %collective-permute-start.7 = (bf16[32,8192]{1,0:T(8,128)(2,1)}, bf16[32,8192]{1,0:T(8,128)(2,1)}, u32[]{:S(2)}, u32[]{:S(2)}) collective-permute-start(bf16[32,8192]{1,0:T(8,128)(2,1)} %get-tuple-element.31), channel_id=1, source_target_pairs={{0,1},{1,0},{2,3},{3,2},{4,6},{5,7},{6,4},{7,5},{8,9},{9,8},{10,11... | collective-permute-start | bytes 1572872 | tf_op jit(solution)/shard_map/ppermute | solution.py:21
  25.1 23.5 %collective-permute-start.6 = (bf16[32,8192]{1,0:T(8,128)(2,1)}, bf16[32,8192]{1,0:T(8,128)(2,1)}, u32[]{:S(2)}, u32[]{:S(2)}) collective-permute-start(bf16[32,8192]{1,0:T(8,128)(2,1)} %collective-permute-done.2.refs_3_), channel_id=1, source_target_pairs={{0,2},{1,3},{2,0},{3,1},{4,5},{5,4},{6,7},{7,6},{8,10},{9,11},{10,... | collective-permute-start | bytes 1572872 | tf_op jit(solution)/shard_map/ppermute | solution.py:21
  31.3 1.4 %collective-permute-start.3 = (f32[192,96]{1,0:T(8,128)S(1)}, f32[192,96]{1,0:T(8,128)S(1)}, u32[]{:S(2)}, u32[]{:S(2)}) collective-permute-start(f32[192,96]{1,0:T(8,128)S(1)} %get-tuple-element.23), channel_id=1, source_target_pairs={{0,4},{1,5},{2,6},{3,7},{4,0},{5,1},{6,2},{7,3},{8,12},{9,13},{10,... | collective-permute-start | bytes 221192 | tf_op jit(solution)/shard_map/ppermute | solution.py:21
  33.6 0.8 %copy-start.3 = (bf16[256,580]{1,0:T(8,128)(2,1)}, bf16[256,580]{1,0:T(8,128)(2,1)S(1)}, u32[]{:S(2)}) copy-start(bf16[256,580]{1,0:T(8,128)(2,1)S(1)} %shard_map.58) | copy-start | bytes 890884
  34.4 21.2 %all-to-all-start = ((bf16[32,8,580]{2,1,0:T(8,128)(2,1)}), bf16[32,8,580]{2,1,0:T(8,128)(2,1)S(1)}, u32[]{:S(2)}, u32[]{:S(2)}) async-start(bf16[32,8,580]{2,1,0:T(8,128)(2,1)} %bitcast.7), calls=%async_computation | async-start | bytes 655360 | tf_op jit(solution)/shard_map/all_to_all | solution.py:214
  52.6 1.5 %collective-permute-start.8 = (f32[192,192]{1,0:T(8,128)S(1)}, f32[192,192]{1,0:T(8,128)S(1)}, u32[]{:S(2)}, u32[]{:S(2)}) collective-permute-start(f32[192,192]{1,0:T(8,128)S(1)} %get-tuple-element.30), channel_id=1, source_target_pairs={{0,4},{1,5},{2,6},{3,7},{4,0},{5,1},{6,2},{7,3},{8,12},{9,13},{10,... | collective-permute-start | bytes 442376 | tf_op jit(solution)/shard_map/ppermute | solution.py:21
  55.6 19.2 %all-to-all-start.1 = ((bf16[32,8,576]{2,1,0:T(8,128)(2,1)}), bf16[32,8,576]{2,1,0:T(8,128)(2,1)S(1)}, u32[]{:S(2)}, u32[]{:S(2)}) async-start(bf16[32,8,576]{2,1,0:T(8,128)(2,1)} %bitcast.4), calls=%async_computation.1 | async-start | bytes 655360 | tf_op jit(solution)/shard_map/all_to_all | solution.py:214

commit v7 on v6

--- a/solution.py
+++ b/solution.py
@@ -9,7 +9,7 @@
 
 BOTH = ("ex", "pb")
 NT = (((1,), (1,)), ((), ()))
-LIMIT = pltpu.CompilerParams(vmem_limit_bytes=20 << 20)
+LIMIT = pltpu.CompilerParams(vmem_limit_bytes=14 << 20)
 LIGHT = pl.CostEstimate(flops=1, bytes_accessed=1, transcendentals=0)
 HBM = pl.BlockSpec(memory_space=pltpu.HBM)
 VMEM = pl.BlockSpec(memory_space=pltpu.VMEM)
@@ -67,7 +67,7 @@
 
 def copied(query, count):
     depth = query.shape[1]
-    parts = 4
+    parts = 2
     height = count // parts
 
     def body(query_ref, out_ref, held, sems):

time: 76.9 us -> 77 us (level)
  transfers between devices with their start and end apart: 11 -> 11, of which waited for: 6 -> 6; matrix products, arithmetic and copies ran while one was open for 5% -> 5% of each run, Pallas kernels for 19% -> 20%
where the time goes in v7:
time: 77 us; the launch traced here: 76.6 us
  waiting for transfers between devices  29.3 us (38%)
  starting transfers between devices  24 us (31%)
  Pallas kernels  16.8 us (22%)
  local copies, waits for them, and re-layouts  6.35 us (8%)
    ppermute x9, waiting for transfers between devices, moved(): lax.ppermute(value, BOTH, [(place(e, p), place(*target(e, p))) for e in r...  18 us
    all_to_all x2, starting transfers between devices, exchanged(): lax.all_to_all(apart, BOTH, split_axis=0, concat_axis=0).reshape(rows.shape)  13 us
    all_to_all x2, waiting for transfers between devices, exchanged(): lax.all_to_all(apart, BOTH, split_axis=0, concat_axis=0).reshape(rows.shape)  11.4 us
    ppermute x9, starting transfers between devices, moved(): lax.ppermute(value, BOTH, [(place(e, p), place(*target(e, p))) for e in r...  11.1 us
    pallas_call x3, Pallas kernels, scored(): pl.pallas_call(functools.partial(scores_kernel, [len(group) for group in...  9.38 us
    unnamed x12, local copies, waits for them, and re-layouts  2.68 us
    pallas_call x2, Pallas kernels, called(): pl.pallas_call(body, out_shape=shapes, compiler_params=LIMIT, cost_estima...  2.68 us
    pallas_call x2, Pallas kernels, packing(): pl.pallas_call(kernel, in_specs=[HBM] * 2 + [VMEM] * len(operands), out_s...  2.39 us
  transfers between devices with their start and end apart: 11, of which 6 were waited for; matrix products, arithmetic and copies ran while one was open for 5% of the time, Pallas kernels for 20%

profile of v7, /device:TPU:0, one launch (start us, length us, event | category | flops | bytes accessed | tf_op | source)
XLA Modules:
  0.0 76.6 jit_solution(4009112823674040777)
XLA Ops:
  0.0 0.0 copy-start
  0.0 0.0 copy-start.1
  0.0 0.5 collective-permute-start.1
  0.5 2.3 %shard_map.55 = bf16[64,8192]{1,0:T(8,128)(2,1)} custom-call(bf16[192,8192]{1,0:T(8,128)(2,1)} %refs_1_.1), custom_call_target="tpu_custom_call" | custom-call | flops 1 | bytes 1 | tf_op jit(solution)/shard_map/pallas_call | solution.py:88
  2.8 2.5 %collective-permute-start = (bf16[64,8192]{1,0:T(8,128)(2,1)}, bf16[64,8192]{1,0:T(8,128)(2,1)}, u32[]{:S(2)}, u32[]{:S(2)}) collective-permute-start(bf16[64,8192]{1,0:T(8,128)(2,1)} %shard_map.55), channel_id=1, source_target_pairs={{0,1},{1,0},{2,3},{3,2},{4,6},{5,7},{6,4},{7,5},{8,9},{9,8},{10,11... | collective-permute-start | bytes 3145736 | tf_op jit(solution)/shard_map/ppermute | solution.py:21
  5.3 2.2 %constant_dynamic-slice_fusion = (bf16[32,8192]{1,0:T(8,128)(2,1)}, bf16[32,8192]{1,0:T(8,128)(2,1)}) fusion(bf16[192,8192]{1,0:T(8,128)(2,1)} %refs_1_.1, s32[]{:T(128)S(6)} %select_n.41, s32[]{:T(128)S(6)} %select_n.40), kind=kLoop, calls=%fused_computation.4 | loop fusion | bytes 2097160 | tf_op jit(solution)/shard_map/dynamic_slice | solution.py:304
  7.5 0.1 collective-permute-start.2
  7.6 0.0 copy-done.1
  7.6 0.0 copy-start.2
  7.6 1.9 %copy-done.2 = bf16[192,8192]{1,0:T(8,128)(2,1)S(1)} copy-done((bf16[192,8192]{1,0:T(8,128)(2,1)S(1)}, bf16[192,8192]{1,0:T(8,128)(2,1)}, u32[]{:S(2)}) %copy-start.2) | copy-done | bytes 3145752
  9.5 0.0 copy-start.5
  9.5 1.7 %shard_map.56.refs_0_ = f32[192,192]{1,0:T(8,128)S(1)} custom-call(bf16[192,8192]{1,0:T(8,128)(2,1)S(1)} %copy-done.1, bf16[192,8192]{1,0:T(8,128)(2,1)S(1)} %copy-done.2), custom_call_target="tpu_custom_call" | custom-call | flops 1 | bytes 1 | tf_op jit(solution)/shard_map/pallas_call | solution.py:57
  11.1 0.0 copy-done.5
  11.2 0.0 copy-done
  11.2 1.4 %gather_fusion = s32[192]{0:T(256)S(1)} fusion(s32[8192]{0:T(1024)S(1)} %copy-done, s32[1024]{0:T(1024)S(1)} %pad_clamp_fusion), kind=kCustom, calls=%fused_computation | custom fusion | bytes 2304 | tf_op jit(solution)/shard_map/jit(_take)/gather | solution.py:281
  12.6 5.7 %collective-permute-done.refs_2_ = bf16[64,8192]{1,0:T(8,128)(2,1)} collective-permute-done((bf16[64,8192]{1,0:T(8,128)(2,1)}, bf16[64,8192]{1,0:T(8,128)(2,1)}, u32[]{:S(2)}, u32[]{:S(2)}) %collective-permute-start) | collective-permute-done | bytes 1048608 | tf_op jit(solution)/shard_map/ppermute | solution.py:21
  18.4 0.0 collective-permute-done.1.refs_1_
  18.4 2.1 %collective-permute-start.4 = (bf16[64,8192]{1,0:T(8,128)(2,1)}, bf16[64,8192]{1,0:T(8,128)(2,1)}, u32[]{:S(2)}, u32[]{:S(2)}) collective-permute-start(bf16[64,8192]{1,0:T(8,128)(2,1)} %collective-permute-done.refs_2_), channel_id=1, source_target_pairs={{0,8},{1,9},{2,10},{3,11},{4,12},{5,13},{6,14},{7,15},{8,0},{9,1},... | collective-permute-start | bytes 3145736 | tf_op jit(solution)/shard_map/ppermute | solution.py:21
  20.5 1.5 %collective-permute-start.5 = (bf16[64,8192]{1,0:T(8,128)(2,1)}, bf16[64,8192]{1,0:T(8,128)(2,1)}, u32[]{:S(2)}, u32[]{:S(2)}) collective-permute-start(bf16[64,8192]{1,0:T(8,128)(2,1)} %collective-permute-done.refs_2_), channel_id=1, source_target_pairs={{0,2},{1,3},{2,0},{3,1},{4,5},{5,4},{6,7},{7,6},{8,10},{9,11},{10,... | collective-permute-start | bytes 3145736 | tf_op jit(solution)/shard_map/ppermute | solution.py:21
  22.0 0.0 copy-start.4
  22.0 1.5 %collective-permute-start.7 = (bf16[32,8192]{1,0:T(8,128)(2,1)}, bf16[32,8192]{1,0:T(8,128)(2,1)}, u32[]{:S(2)}, u32[]{:S(2)}) collective-permute-start(bf16[32,8192]{1,0:T(8,128)(2,1)} %get-tuple-element.31), channel_id=1, source_target_pairs={{0,1},{1,0},{2,3},{3,2},{4,6},{5,7},{6,4},{7,5},{8,9},{9,8},{10,11... | collective-permute-start | bytes 1572872 | tf_op jit(solution)/shard_map/ppermute | solution.py:21
  23.5 1.6 %collective-permute-done.2.refs_3_ = bf16[32,8192]{1,0:T(8,128)(2,1)} collective-permute-done((bf16[32,8192]{1,0:T(8,128)(2,1)}, bf16[32,8192]{1,0:T(8,128)(2,1)}, u32[]{:S(2)}, u32[]{:S(2)}) %collective-permute-start.2) | collective-permute-done | bytes 524320 | tf_op jit(solution)/shard_map/ppermute | solution.py:21
  25.1 2.5 %collective-permute-start.6 = (bf16[32,8192]{1,0:T(8,128)(2,1)}, bf16[32,8192]{1,0:T(8,128)(2,1)}, u32[]{:S(2)}, u32[]{:S(2)}) collective-permute-start(bf16[32,8192]{1,0:T(8,128)(2,1)} %collective-permute-done.2.refs_3_), channel_id=1, source_target_pairs={{0,2},{1,3},{2,0},{3,1},{4,5},{5,4},{6,7},{7,6},{8,10},{9,11},{10,... | collective-permute-start | bytes 1572872 | tf_op jit(solution)/shard_map/ppermute | solution.py:21
  27.6 3.7 %shard_map.57 = (f32[192,96]{1,0:T(8,128)S(1)}, f32[192,96]{1,0:T(8,128)S(1)}) custom-call(bf16[192,8192]{1,0:T(8,128)(2,1)S(1)} %copy-done.1, bf16[192,8192]{1,0:T(8,128)(2,1)} %collective-permute-done.1.refs_1_, bf16[64,8192]{1,0:T(8,128)(2,1)} %collective-permute-done.refs_2_, bf16[32,8192]{1,0:T(8,128)(2,1)} %collective-permute-done.2.refs_3_), custom_call_target="tpu_custom_call" | custom-call | flops 1 | bytes 1 | tf_op jit(solution)/shard_map/pallas_call | solution.py:57
  31.3 0.1 collective-permute-start.3
  31.4 1.3 %collective-permute-done.3.refs_2_ = f32[192,96]{1,0:T(8,128)S(1)} collective-permute-done((f32[192,96]{1,0:T(8,128)S(1)}, f32[192,96]{1,0:T(8,128)S(1)}, u32[]{:S(2)}, u32[]{:S(2)}) %collective-permute-start.3) | collective-permute-done | bytes 73760 | tf_op jit(solution)/shard_map/ppermute | solution.py:21
  32.7 0.0 copy-done.4
  32.7 1.0 %shard_map.58 = bf16[256,580]{1,0:T(8,128)(2,1)S(1)} custom-call(f32[1,192]{1,0:T(1,128)S(1)} %bitcast.11, s32[1,192]{1,0:T(1,128)S(1)} %bitcast.9, f32[192,192]{1,0:T(8,128)S(1)} %shard_map.56.refs_0_, f32[192,96]{1,0:T(8,128)S(1)} %get-tuple-element.22.refs_1_, f32[192,96]{1,0:T(8,128)S(1)} %collective-permute-done.3.refs_2_), custom_call_target="tpu_custom_call" | custom-call | flops 1 | bytes 1 | tf_op jit(solution)/shard_map/pallas_call | solution.py:150
  33.6 0.0 copy-start.3
  33.6 0.8 %copy-done.3 = bf16[256,580]{1,0:T(8,128)(2,1)} copy-done((bf16[256,580]{1,0:T(8,128)(2,1)}, bf16[256,580]{1,0:T(8,128)(2,1)S(1)}, u32[]{:S(2)}) %copy-start.3) | copy-done | bytes 296984
  34.4 6.0 %all-to-all-start = ((bf16[32,8,580]{2,1,0:T(8,128)(2,1)}), bf16[32,8,580]{2,1,0:T(8,128)(2,1)S(1)}, u32[]{:S(2)}, u32[]{:S(2)}) async-start(bf16[32,8,580]{2,1,0:T(8,128)(2,1)} %bitcast.7), calls=%async_computation | async-start | bytes 655360 | tf_op jit(solution)/shard_map/all_to_all | solution.py:214
  40.5 0.0 collective-permute-done.7.refs_5_
  40.5 8.1 %collective-permute-done.6.refs_4_ = bf16[32,8192]{1,0:T(8,128)(2,1)} collective-permute-done((bf16[32,8192]{1,0:T(8,128)(2,1)}, bf16[32,8192]{1,0:T(8,128)(2,1)}, u32[]{:S(2)}, u32[]{:S(2)}) %collective-permute-start.6) | collective-permute-done | bytes 524320 | tf_op jit(solution)/shard_map/ppermute | solution.py:21
  48.6 0.0 collective-permute-done.4.refs_2_
  48.6 0.0 collective-permute-done.5.refs_3_
  48.6 4.0 %shard_map.60 = (f32[192,192]{1,0:T(8,128)S(1)}, f32[192,192]{1,0:T(8,128)S(1)}) custom-call(bf16[192,8192]{1,0:T(8,128)(2,1)S(1)} %copy-done.1, bf16[192,8192]{1,0:T(8,128)(2,1)} %collective-permute-done.1.refs_1_, bf16[64,8192]{1,0:T(8,128)(2,1)} %collective-permute-done.4.refs_2_, bf16[64,8192]{1,0:T(8,128)(2,1)} %collective-permute-done.5.refs_3_, ...), custom_call_target="tpu_custom_call" | custom-call | flops 1 | bytes 1 | tf_op jit(solution)/shard_map/pallas_call | solution.py:57
  52.7 0.3 collective-permute-start.8
  53.0 1.2 %collective-permute-done.8.refs_1_ = f32[192,192]{1,0:T(8,128)S(1)} collective-permute-done((f32[192,192]{1,0:T(8,128)S(1)}, f32[192,192]{1,0:T(8,128)S(1)}, u32[]{:S(2)}, u32[]{:S(2)}) %collective-permute-start.8) | collective-permute-done | bytes 147488 | tf_op jit(solution)/shard_map/ppermute | solution.py:21
  54.2 1.4 %shard_map.61 = bf16[256,576]{1,0:T(8,128)(2,1)} custom-call(f32[1,192]{1,0:T(1,128)S(1)} %bitcast.12, s32[1,192]{1,0:T(1,128)S(1)} %bitcast.10, f32[192,192]{1,0:T(8,128)S(1)} %get-tuple-element.29.refs_0_, f32[192,192]{1,0:T(8,128)S(1)} %collective-permute-done.8.refs_1_), custom_call_target="tpu_custom_call" | custom-call | flops 1 | bytes 1 | tf_op jit(solution)/shard_map/pallas_call | solution.py:150
  55.6 0.0 all-to-all-done
  55.6 6.9 %all-to-all-start.1 = ((bf16[32,8,576]{2,1,0:T(8,128)(2,1)}), bf16[32,8,576]{2,1,0:T(8,128)(2,1)S(1)}, u32[]{:S(2)}, u32[]{:S(2)}) async-start(bf16[32,8,576]{2,1,0:T(8,128)(2,1)} %bitcast.4), calls=%async_computation.1 | async-start | bytes 655360 | tf_op jit(solution)/shard_map/all_to_all | solution.py:214
  62.6 0.9 %shard_map.59 = (f32[256,768]{1,0:T(8,128)S(1)}, bf16[2,256,256]{2,1,0:T(8,128)(2,1)S(1)}) custom-call(bf16[256,580]{1,0:T(8,128)(2,1)S(1)} %bitcast.6), custom_call_target="tpu_custom_call" | custom-call | flops 1 | bytes 1 | tf_op jit(solution)/shard_map/pallas_call | solution.py:209
  63.5 11.4 %all-to-all-done.1 = bf16[32,8,576]{2,1,0:T(8,128)(2,1)S(1)} async-done(((bf16[32,8,576]{2,1,0:T(8,128)(2,1)}), bf16[32,8,576]{2,1,0:T(8,128)(2,1)S(1)}, u32[]{:S(2)}, u32[]{:S(2)}) %all-to-all-start.1) | async-done | bytes 294944 | tf_op jit(solution)/shard_map/all_to_all | solution.py:214
  74.9 1.8 %shard_map.62 = f32[256,768]{1,0:T(8,128)} custom-call(f32[256,768]{1,0:T(8,128)S(1)} %get-tuple-element.25.first_ref, bf16[2,256,256]{2,1,0:T(8,128)(2,1)S(1)} %get-tuple-element.26.hot_ref, bf16[256,576]{1,0:T(8,128)(2,1)S(1)} %bitcast.8), custom_call_target="tpu_custom_call" | custom-call | flops 1 | bytes 1 | tf_op jit(solution)/shard_map/pallas_call | solution.py:209
  (3 shorter events, 0.0 us)
Async XLA Ops:
  0.0 11.2 %copy-start = (s32[8192]{0:T(1024)S(1)}, s32[8192]{0:T(1024)}, u32[]{:S(2)}) copy-start(s32[8192]{0:T(1024)} %param.9) | copy-start | bytes 98308
  0.0 7.6 %copy-start.1 = (bf16[192,8192]{1,0:T(8,128)(2,1)S(1)}, bf16[192,8192]{1,0:T(8,128)(2,1)}, u32[]{:S(2)}) copy-start(bf16[192,8192]{1,0:T(8,128)(2,1)} %refs_0_.4) | copy-start | bytes 9437188
  0.0 18.4 %collective-permute-start.1 = (bf16[192,8192]{1,0:T(8,128)(2,1)}, bf16[192,8192]{1,0:T(8,128)(2,1)}, u32[]{:S(2)}, u32[]{:S(2)}) collective-permute-start(bf16[192,8192]{1,0:T(8,128)(2,1)} %refs_0_.4), channel_id=1, source_target_pairs={{0,4},{1,5},{2,6},{3,7},{4,0},{5,1},{6,2},{7,3},{8,12},{9,13},{10,... | collective-permute-start | bytes 9437192 | tf_op jit(solution)/shard_map/ppermute | solution.py:21
  2.8 15.6 %collective-permute-start = (bf16[64,8192]{1,0:T(8,128)(2,1)}, bf16[64,8192]{1,0:T(8,128)(2,1)}, u32[]{:S(2)}, u32[]{:S(2)}) collective-permute-start(bf16[64,8192]{1,0:T(8,128)(2,1)} %shard_map.55), channel_id=1, source_target_pairs={{0,1},{1,0},{2,3},{3,2},{4,6},{5,7},{6,4},{7,5},{8,9},{9,8},{10,11... | collective-permute-start | bytes 3145736 | tf_op jit(solution)/shard_map/ppermute | solution.py:21
  7.5 17.6 %collective-permute-start.2 = (bf16[32,8192]{1,0:T(8,128)(2,1)}, bf16[32,8192]{1,0:T(8,128)(2,1)}, u32[]{:S(2)}, u32[]{:S(2)}) collective-permute-start(bf16[32,8192]{1,0:T(8,128)(2,1)} %get-tuple-element.32), channel_id=1, source_target_pairs={{0,1},{1,0},{2,3},{3,2},{4,6},{5,7},{6,4},{7,5},{8,9},{9,8},{10,11... | collective-permute-start | bytes 1572872 | tf_op jit(solution)/shard_map/ppermute | solution.py:21
  7.6 1.9 %copy-start.2 = (bf16[192,8192]{1,0:T(8,128)(2,1)S(1)}, bf16[192,8192]{1,0:T(8,128)(2,1)}, u32[]{:S(2)}) copy-start(bf16[192,8192]{1,0:T(8,128)(2,1)} %refs_1_.1) | copy-start | bytes 9437188
  9.5 1.7 %copy-start.5 = (s32[192]{0:T(256)S(1)}, s32[192]{0:T(256)}, u32[]{:S(2)}) copy-start(s32[192]{0:T(256)} %param.8) | copy-start | bytes 2308
  18.4 30.3 %collective-permute-start.4 = (bf16[64,8192]{1,0:T(8,128)(2,1)}, bf16[64,8192]{1,0:T(8,128)(2,1)}, u32[]{:S(2)}, u32[]{:S(2)}) collective-permute-start(bf16[64,8192]{1,0:T(8,128)(2,1)} %collective-permute-done.refs_2_), channel_id=1, source_target_pairs={{0,8},{1,9},{2,10},{3,11},{4,12},{5,13},{6,14},{7,15},{8,0},{9,1},... | collective-permute-start | bytes 3145736 | tf_op jit(solution)/shard_map/ppermute | solution.py:21
  20.5 28.2 %collective-permute-start.5 = (bf16[64,8192]{1,0:T(8,128)(2,1)}, bf16[64,8192]{1,0:T(8,128)(2,1)}, u32[]{:S(2)}, u32[]{:S(2)}) collective-permute-start(bf16[64,8192]{1,0:T(8,128)(2,1)} %collective-permute-done.refs_2_), channel_id=1, source_target_pairs={{0,2},{1,3},{2,0},{3,1},{4,5},{5,4},{6,7},{7,6},{8,10},{9,11},{10,... | collective-permute-start | bytes 3145736 | tf_op jit(solution)/shard_map/ppermute | solution.py:21
  22.0 10.7 %copy-start.4 = (f32[192]{0:T(256)S(1)}, f32[192]{0:T(256)}, u32[]{:S(2)}) copy-start(f32[192]{0:T(256)} %param.7) | copy-start | bytes 2308
  22.0 18.5 %collective-permute-start.7 = (bf16[32,8192]{1,0:T(8,128)(2,1)}, bf16[32,8192]{1,0:T(8,128)(2,1)}, u32[]{:S(2)}, u32[]{:S(2)}) collective-permute-start(bf16[32,8192]{1,0:T(8,128)(2,1)} %get-tuple-element.31), channel_id=1, source_target_pairs={{0,1},{1,0},{2,3},{3,2},{4,6},{5,7},{6,4},{7,5},{8,9},{9,8},{10,11... | collective-permute-start | bytes 1572872 | tf_op jit(solution)/shard_map/ppermute | solution.py:21
  25.1 23.5 %collective-permute-start.6 = (bf16[32,8192]{1,0:T(8,128)(2,1)}, bf16[32,8192]{1,0:T(8,128)(2,1)}, u32[]{:S(2)}, u32[]{:S(2)}) collective-permute-start(bf16[32,8192]{1,0:T(8,128)(2,1)} %collective-permute-done.2.refs_3_), channel_id=1, source_target_pairs={{0,2},{1,3},{2,0},{3,1},{4,5},{5,4},{6,7},{7,6},{8,10},{9,11},{10,... | collective-permute-start | bytes 1572872 | tf_op jit(solution)/shard_map/ppermute | solution.py:21
  31.3 1.4 %collective-permute-start.3 = (f32[192,96]{1,0:T(8,128)S(1)}, f32[192,96]{1,0:T(8,128)S(1)}, u32[]{:S(2)}, u32[]{:S(2)}) collective-permute-start(f32[192,96]{1,0:T(8,128)S(1)} %get-tuple-element.23), channel_id=1, source_target_pairs={{0,4},{1,5},{2,6},{3,7},{4,0},{5,1},{6,2},{7,3},{8,12},{9,13},{10,... | collective-permute-start | bytes 221192 | tf_op jit(solution)/shard_map/ppermute | solution.py:21
  33.6 0.8 %copy-start.3 = (bf16[256,580]{1,0:T(8,128)(2,1)}, bf16[256,580]{1,0:T(8,128)(2,1)S(1)}, u32[]{:S(2)}) copy-start(bf16[256,580]{1,0:T(8,128)(2,1)S(1)} %shard_map.58) | copy-start | bytes 890884
  34.4 21.2 %all-to-all-start = ((bf16[32,8,580]{2,1,0:T(8,128)(2,1)}), bf16[32,8,580]{2,1,0:T(8,128)(2,1)S(1)}, u32[]{:S(2)}, u32[]{:S(2)}) async-start(bf16[32,8,580]{2,1,0:T(8,128)(2,1)} %bitcast.7), calls=%async_computation | async-start | bytes 655360 | tf_op jit(solution)/shard_map/all_to_all | solution.py:214
  52.7 1.5 %collective-permute-start.8 = (f32[192,192]{1,0:T(8,128)S(1)}, f32[192,192]{1,0:T(8,128)S(1)}, u32[]{:S(2)}, u32[]{:S(2)}) collective-permute-start(f32[192,192]{1,0:T(8,128)S(1)} %get-tuple-element.30), channel_id=1, source_target_pairs={{0,4},{1,5},{2,6},{3,7},{4,0},{5,1},{6,2},{7,3},{8,12},{9,13},{10,... | collective-permute-start | bytes 442376 | tf_op jit(solution)/shard_map/ppermute | solution.py:21
  55.6 19.2 %all-to-all-start.1 = ((bf16[32,8,576]{2,1,0:T(8,128)(2,1)}), bf16[32,8,576]{2,1,0:T(8,128)(2,1)S(1)}, u32[]{:S(2)}, u32[]{:S(2)}) async-start(bf16[32,8,576]{2,1,0:T(8,128)(2,1)} %bitcast.4), calls=%async_computation.1 | async-start | bytes 655360 | tf_op jit(solution)/shard_map/all_to_all | solution.py:214
